TPU v7x, 256 devices: a whole 4x4x8 slice. The times are simulated.
256 devices in a mesh: dp: 8 (over y, core), bucket: 32 (over x, z).
Axes of the slice: x: 4, y: 4, z: 8, core: 2. Of those that a mesh axis runs over, the one named last changes fastest.
Arguments:
- frames: bfloat16 [393216, 512], P(('dp', 'bucket')), may hold values from -60 to 60, as said below
- lengths: int32 [8, 1024], P('dp'), may hold values from 1 to 48, as said below
- owners: int32 [8, 1024], P('dp'), may hold values from 0 to 31, as said below
- upstream: bfloat16 [196608, 512], P(('dp', 'bucket')), may hold values from -6 to 6
- ln_gain: float32 [512], replicated, may hold values from 0.1 to 1.9
- w_in: bfloat16 [512, 1024], replicated, may hold values from -0.25 to 0.25
- w_dw: float32 [512, 31], replicated, may hold values from -1 to 1
- bn_gain: float32 [512], replicated, may hold values from 0.1 to 1.9
- bn_bias: float32 [512], replicated, may hold values from -3 to 3
- w_out: bfloat16 [512, 512], replicated, may hold values from -0.25 to 0.25
Outputs:
- out_frames: bfloat16 [196608, 512], P(('dp', 'bucket'))
- grad_frames: bfloat16 [393216, 512], P(('dp', 'bucket'))
- grad_w_in: float32 [512, 1024], P('bucket')
- grad_w_out: float32 [512, 512], P('bucket')
- grad_w_dw: float32 [512, 31], P('bucket')
- grad_ln_gain: float32 [512], P('bucket')
- grad_bn_gain: float32 [512], replicated
- grad_bn_bias: float32 [512], replicated
Inputs may be any that keep to these rules, and one draw needn't show every extreme that they name: `frames`: frame rows past an utterance's length are not read. In each group every owner receives exactly 1 utterances from each loader shard, their lengths sum to exactly 768 with one of exactly 48, and the lengths an owner receives do not fall with the loader index. `owners`: in each group and loader shard every owner index appears exactly 1 times.
All inputs are finite; a program needn't handle non-finite values.
Results may differ from a plain program's by a relative error of at most 0.013.
Values may be sent and summed in bfloat16 or wider, within the bound.
No kernel may reach another device: no remote copies, remote signals or barrier semaphores. Data moves between devices by JAX's collectives and lax.ppermute only.
A program may use at most 128 MiB of HBM per device.

v0:
```python
import functools

import jax
import jax.numpy as jnp
from jax import lax
from jax.sharding import Mesh
from jax.sharding import PartitionSpec as P

BUCKET = ("bucket_0", "bucket_1")
DP = ("dp_0", "dp_1")
DP_BUCKET = ("dp_0", "dp_1", "bucket_0", "bucket_1")


EPSILON = 1e-05


def by_axis(value, axes):
    return functools.reduce(lax.psum, axes, value)


def scatter_axes(value, axes, dim):
    for axis in axes:
        value = lax.psum_scatter(value, axis, scatter_dimension=dim, tiled=True)
    return value


def sent_to_all(value, axis):
    copies = jnp.broadcast_to(value, (lax.axis_size(axis), *value.shape))
    return lax.all_to_all(copies, axis, split_axis=0, concat_axis=0, tiled=True)


def of_everyone(value, axis):
    everything = sent_to_all(value, axis)
    return jnp.sum(everything.astype(jnp.float32), axis=0)


def normalize_rows(frame_rows, ln_gain):
    values = frame_rows.astype(jnp.float32)
    centred = values - jnp.mean(values, axis=1, keepdims=True)
    inverse = lax.rsqrt(jnp.mean(centred * centred, axis=1, keepdims=True) + EPSILON)
    normed = centred * inverse
    return ((normed * ln_gain).astype(jnp.bfloat16), normed, inverse)


def normalize_back(grad_h, normed, inverse, ln_gain):
    scaled = grad_h * ln_gain
    inner_sum = jnp.mean(scaled * normed, axis=1, keepdims=True)
    return inverse * (scaled - jnp.mean(scaled, axis=1, keepdims=True) - normed * inner_sum)


def conv_forward(gated_rows, segment, w_dw):
    width_half = w_dw.shape[1] // 2
    length_all = gated_rows.shape[1]
    padded = jnp.pad(gated_rows, ((0, 0), (width_half, width_half), (0, 0)))
    seg_pad = jnp.pad(segment, ((0, 0), (width_half, width_half)), constant_values=-1)
    result = jnp.zeros(gated_rows.shape, jnp.float32)
    for offset in range(w_dw.shape[1]):
        same_seg = (seg_pad[:, offset : offset + length_all] == segment)[:, :, None]
        shifted = padded[:, offset : offset + length_all].astype(jnp.float32)
        result = result + jnp.where(same_seg, shifted, 0.0) * w_dw[:, offset]
    return result


def conv_backward(grad_conv, gated_rows, segment, w_dw):
    width_half = w_dw.shape[1] // 2
    length_all = gated_rows.shape[1]
    padded = jnp.pad(gated_rows, ((0, 0), (width_half, width_half), (0, 0)))
    grad_pad = jnp.pad(grad_conv, ((0, 0), (width_half, width_half), (0, 0)))
    seg_pad = jnp.pad(segment, ((0, 0), (width_half, width_half)), constant_values=-1)
    grad_gated = jnp.zeros(grad_conv.shape, jnp.float32)
    grad_cols = []
    for offset in range(w_dw.shape[1]):
        same_fwd = (seg_pad[:, offset : offset + length_all] == segment)[:, :, None]
        shifted = jnp.where(
            same_fwd, padded[:, offset : offset + length_all].astype(jnp.float32), 0.0
        )
        grad_cols.append(jnp.sum(shifted * grad_conv, axis=(0, 1)))
        back_start = 2 * width_half - offset
        same_back = (seg_pad[:, back_start : back_start + length_all] == segment)[:, :, None]
        grad_gated = (
            grad_gated
            + jnp.where(same_back, grad_pad[:, back_start : back_start + length_all], 0.0)
            * w_dw[:, offset]
        )
    return (grad_gated, jnp.stack(grad_cols, axis=1))


def local(frames, lengths, owners, upstream, ln_gain, w_in, w_dw, bn_gain, bn_bias, w_out):
    loaders = lax.axis_size(BUCKET)
    own_index = lax.axis_index(BUCKET)
    feature_count = frames.shape[1]
    slot_count = lengths.shape[1] // loaders
    span_max = frames.shape[0] // slot_count
    pair_count = slot_count // loaders
    own_rows = upstream.shape[0]
    total_frames = float(own_rows * loaders * lax.axis_size(DP))
    lens_all = lengths[0].reshape(loaders, slot_count)
    dest_all = owners[0].reshape(loaders, slot_count)
    owner_ids = jnp.arange(loaders, dtype=jnp.int32)
    onehot = (dest_all[:, :, None] == owner_ids[None, None, :]).astype(jnp.int32)
    earlier = jnp.cumsum(onehot, axis=1) - onehot
    ranking = jnp.sum(earlier * onehot, axis=2)
    send_pos = dest_all * pair_count + ranking
    my_pos = lax.dynamic_index_in_dim(send_pos, own_index, 0, keepdims=False)
    send_order = (
        jnp.zeros((slot_count,), jnp.int32).at[my_pos].set(jnp.arange(slot_count, dtype=jnp.int32))
    )
    slot_frames = frames.reshape(slot_count, span_max, feature_count)
    outgoing = jnp.take(slot_frames, send_order, axis=0).reshape(
        loaders, pair_count, span_max, feature_count
    )
    incoming = lax.all_to_all(outgoing, BUCKET, split_axis=0, concat_axis=0, tiled=True)
    incoming_rows = incoming.reshape(slot_count * span_max, feature_count)
    pair_ids = jnp.arange(pair_count, dtype=jnp.int32)
    to_me = (dest_all == own_index)[:, :, None] & (ranking[:, :, None] == pair_ids[None, None, :])
    recv_lens = jnp.sum(jnp.where(to_me, lens_all[:, :, None], 0), axis=1).reshape(-1)
    starts = jnp.cumsum(recv_lens) - recv_lens
    position = jnp.arange(span_max, dtype=jnp.int32)
    slot_valid = position[None, :] < recv_lens[:, None]
    row_ids = jnp.arange(own_rows, dtype=jnp.int32)
    row_slot = jnp.sum((starts[None, :] <= row_ids[:, None]).astype(jnp.int32), axis=1) - 1
    row_offset = row_ids - jnp.take(starts, row_slot)
    packed_source = row_slot * span_max + row_offset
    slot_target = jnp.minimum(
        jnp.where(slot_valid, starts[:, None] + position[None, :], own_rows - 1), own_rows - 1
    ).reshape(-1)
    slot_valid_flat = slot_valid.reshape(-1)
    work_frames = jnp.take(incoming_rows, packed_source, axis=0)
    segment = row_slot[None, :]
    valid_rows = row_ids >= 0
    group_count = segment.shape[0]
    group_length = segment.shape[1]
    normed_h, normed, inverse = normalize_rows(work_frames, ln_gain)
    projected = jnp.dot(normed_h, w_in, preferred_element_type=jnp.float32)
    linear = projected[:, :feature_count]
    gate_sig = jax.nn.sigmoid(projected[:, feature_count:])
    gated_rows = jnp.where(valid_rows[:, None], linear * gate_sig, 0.0).astype(jnp.bfloat16)
    gated_blocks = gated_rows.reshape(group_count, group_length, feature_count)
    conv_rows = conv_forward(gated_blocks, segment, w_dw).reshape(-1, feature_count)
    masked = jnp.where(valid_rows[:, None], conv_rows, 0.0)
    first_sum, second_sum = (
        by_axis(jnp.sum(masked, axis=0), DP_BUCKET),
        by_axis(jnp.sum(masked * masked, axis=0), DP_BUCKET),
    )
    centre = first_sum / total_frames
    variance = second_sum / total_frames - centre * centre
    bn_inverse = lax.rsqrt(variance + EPSILON)
    bn_normed = (conv_rows - centre) * bn_inverse
    bn_value = bn_normed * bn_gain + bn_bias
    bn_sig = jax.nn.sigmoid(bn_value)
    swished = (bn_value * bn_sig).astype(jnp.bfloat16)
    out_rows = jnp.dot(swished, w_out, preferred_element_type=jnp.float32).astype(jnp.bfloat16)
    grad_wout = jnp.einsum("rd,re->de", swished, upstream, preferred_element_type=jnp.float32)
    grad_swish = jnp.einsum("re,de->rd", upstream, w_out, preferred_element_type=jnp.float32)
    grad_bn_rows = grad_swish * (bn_sig * (1.0 + bn_value * (1.0 - bn_sig)))
    bias_total, gain_total = (
        by_axis(jnp.sum(grad_bn_rows, axis=0), DP_BUCKET),
        by_axis(jnp.sum(grad_bn_rows * bn_normed, axis=0), DP_BUCKET),
    )
    grad_conv = jnp.where(
        valid_rows[:, None],
        bn_gain
        * bn_inverse
        * (grad_bn_rows - bias_total / total_frames - bn_normed * (gain_total / total_frames)),
        0.0,
    )
    grad_gated, grad_wdw = conv_backward(
        grad_conv.reshape(group_count, group_length, feature_count), gated_blocks, segment, w_dw
    )
    grad_gated = jnp.where(valid_rows[:, None], grad_gated.reshape(-1, feature_count), 0.0)
    grad_proj = jnp.concatenate(
        [grad_gated * gate_sig, grad_gated * linear * gate_sig * (1.0 - gate_sig)], axis=1
    ).astype(jnp.bfloat16)
    grad_win = jnp.einsum("rd,rf->df", normed_h, grad_proj, preferred_element_type=jnp.float32)
    grad_h = jnp.einsum("rf,df->rd", grad_proj, w_in, preferred_element_type=jnp.float32)
    grad_ln = jnp.sum(grad_h * normed, axis=0)
    grad_work = jnp.where(
        valid_rows[:, None], normalize_back(grad_h, normed, inverse, ln_gain), 0.0
    ).astype(jnp.bfloat16)
    grad_slots = jnp.where(slot_valid_flat[:, None], jnp.take(grad_work, slot_target, axis=0), 0)
    returned = lax.all_to_all(
        grad_slots.reshape(loaders, pair_count, span_max, feature_count),
        BUCKET,
        split_axis=0,
        concat_axis=0,
        tiled=True,
    )
    grad_frames = jnp.take(
        returned.reshape(slot_count, span_max, feature_count), my_pos, axis=0
    ).reshape(-1, feature_count)
    row_sums = (
        scatter_axes(grad_win, BUCKET, 0),
        scatter_axes(grad_wout, BUCKET, 0),
        scatter_axes(grad_wdw, BUCKET, 0),
        scatter_axes(grad_ln, BUCKET, 0),
    )
    shares = (
        of_everyone(row_sums[0].astype(jnp.bfloat16), DP).astype(jnp.float32),
        of_everyone(row_sums[1].astype(jnp.bfloat16), DP).astype(jnp.float32),
        of_everyone(row_sums[2].astype(jnp.bfloat16), DP).astype(jnp.float32),
        of_everyone(row_sums[3].astype(jnp.bfloat16), DP).astype(jnp.float32),
    )
    return (
        out_rows,
        grad_frames,
        shares[0],
        shares[1],
        shares[2],
        shares[3],
        gain_total,
        bias_total,
    )


def solution(mesh):
    torus = Mesh(mesh.devices.reshape(4, 2, 4, 8), ("dp_0", "dp_1", "bucket_0", "bucket_1"))
    in_specs = (
        P(DP_BUCKET, None),
        P(DP, None),
        P(DP, None),
        P(DP_BUCKET, None),
        P(),
        P(),
        P(),
        P(),
        P(),
        P(),
    )
    out_specs = (
        P(DP_BUCKET, None),
        P(DP_BUCKET, None),
        P(BUCKET, None),
        P(BUCKET, None),
        P(BUCKET, None),
        P(BUCKET),
        P(),
        P(),
    )
    return jax.shard_map(local, mesh=torus, in_specs=in_specs, out_specs=out_specs, check_vma=False)
```

profile of v0, /device:TPU:32, one launch (start us, length us, event | category | flops | bytes accessed | tf_op | source)
XLA Modules:
  0.0 410.9 jit_solution(8831659155091519255)
XLA Ops:
  13.2 11.3 %all-to-all-start = ((bf16[32,1,48,512]{3,2,1,0:T(8,128)(2,1)}), bf16[32,1,48,512]{3,2,1,0:T(8,128)(2,1)S(1)}, u32[]{:S(2)}, u32[]{:S(2)}) async-start(bf16[32,1,48,512]{3,2,1,0:T(8,128)(2,1)} %select_bitcast_fusion), calls=%async_computation | async-start | bytes 3145728 | tf_op jit(solution)/shard_map/all_to_all | solution.py:112
  26.7 4.4 %fusion.67 = (s32[768]{0:T(1024)S(1)}, s32[768,1]{0,1:T(1,128)S(1)}) fusion(s32[]{:T(128)} %bitcast.27, s32[]{:T(128)} %bitcast.28, s32[]{:T(128)} %bitcast.29, s32[]{:T(128)} %bitcast.30, s32[]{:T(128)} %bitcast.31, s32[]{:T(128)} %bitcast.33, s32[]{:T(128)} %bitcast.32, s32[768]{0:T(1024)S(1)} %get-tuple-element.158, s32[768]{0:T(1024)S(1)} %get-tuple-element.159), kind=kLoop, calls=%fused_computation.245 | loop fusion | flops 10752 | bytes 12316 | tf_op jit(solution)/shard_map/jit(_take)/gather | solution.py:122
  32.1 15.7 %compare_and_fusion.1 = (pred[768]{0:T(1024)(128)(4,1)S(1)}, s32[768]{0:T(1024)S(1)}) fusion(s32[768]{0:T(1024)S(1)} %convert_reduce_fusion.3, pred[768]{0:T(1024)(128)(4,1)S(1)} %get-tuple-element.98, pred[768]{0:T(1024)(128)(4,1)S(1)} %get-tuple-element.96, pred[768]{0:T(1024)(128)(4,1)S(1)} %get-tuple-element.97, ...), kind=kLoop, calls=%fused_computation.244 | loop fusion | flops 32256 | bytes 29284 | tf_op jit(solution)/shard_map/jit(_take)/and | solution.py:128
  48.6 15.1 %all-to-all-done = bf16[32,1,48,512]{3,2,1,0:T(8,128)(2,1)S(1)} async-done(((bf16[32,1,48,512]{3,2,1,0:T(8,128)(2,1)}), bf16[32,1,48,512]{3,2,1,0:T(8,128)(2,1)S(1)}, u32[]{:S(2)}, u32[]{:S(2)}) %all-to-all-start) | async-done | bytes 1572896 | tf_op jit(solution)/shard_map/all_to_all | solution.py:112
  72.7 10.3 %fusion.80 = (f32[512]{0:T(512)S(1)}, f32[1,768,512]{2,1,0:T(8,128)S(1)}) fusion(f32[512]{0:T(512)S(1)} %bitcast.277, pred[768]{0:T(1024)(128)(4,1)S(1)} %get-tuple-element.73, f32[512]{0:T(512)S(1)} %bitcast.279, pred[768]{0:T(1024)(128)(4,1)S(1)} %get-tuple-element.45, f32[512]{0:T(512)S(1)} %bitcast.283, pred[768]{0:T(1024)(128)(4,1)S(1)} %get-tuple-element.46, ...), kind=kLoop, calls=%fused_computation.272 | loop fusion | flops 50331136 | bytes 5593600 | tf_op jit(solution)/shard_map/reduce_sum | solution.py:142
  83.3 10.7 %all-reduce.10 = (f32[512]{0:T(512)S(1)}, f32[512]{0:T(512)S(1)}) all-reduce(f32[512]{0:T(512)S(1)} %fusion.54, f32[512]{0:T(512)S(1)} %get-tuple-element.118), channel_id=1, replica_groups=mesh['dp_0'=4,'dp_1'=2,'bucket_0'=4,'bucket_1'=8] {'dp_0'}, use_global_device_ids=true, to_apply=%region_14.16 | all-reduce | flops 1024 | bytes 8192 | tf_op jit(solution)/shard_map/psum | solution.py:18
  96.4 8.9 %all-reduce.8 = (f32[512]{0:T(512)S(1)}, f32[512]{0:T(512)S(1)}) all-reduce(f32[512]{0:T(512)S(1)} %get-tuple-element.113, f32[512]{0:T(512)S(1)} %get-tuple-element.114), channel_id=1, replica_groups=mesh['dp_0'=4,'dp_1'=2,'bucket_0'=4,'bucket_1'=8] {'bucket_0'}, use_global_device_ids=true, to_apply=%region_16.18 | all-reduce | flops 1024 | bytes 8192 | tf_op jit(solution)/shard_map/psum | solution.py:18
  105.3 14.4 %all-reduce.6 = (f32[512]{0:T(512)S(1)}, f32[512]{0:T(512)S(1)}) all-reduce(f32[512]{0:T(512)S(1)} %get-tuple-element.105, f32[512]{0:T(512)S(1)} %get-tuple-element.106), channel_id=1, replica_groups=mesh['dp_0'=4,'dp_1'=2,'bucket_0'=4,'bucket_1'=8] {'bucket_1'}, use_global_device_ids=true, to_apply=%region_17.19 | all-reduce | flops 1024 | bytes 8192 | tf_op jit(solution)/shard_map/psum | solution.py:18
  123.6 7.7 %all-reduce.9 = (f32[512]{0:T(512)S(1)}, f32[512]{0:T(512)S(1)}) all-reduce(f32[512]{0:T(512)S(1)} %get-tuple-element.43, f32[512]{0:T(512)S(1)} %get-tuple-element.42), channel_id=1, replica_groups=mesh['dp_0'=4,'dp_1'=2,'bucket_0'=4,'bucket_1'=8] {'dp_0'}, use_global_device_ids=true, to_apply=%region_24.26 | all-reduce | flops 1024 | bytes 8192 | tf_op jit(solution)/shard_map/psum | solution.py:18
  133.8 8.8 %all-reduce.7 = (f32[512]{0:T(512)S(1)}, f32[512]{0:T(512)S(1)}) all-reduce(f32[512]{0:T(512)S(1)} %get-tuple-element.111, f32[512]{0:T(512)S(1)} %get-tuple-element.112), channel_id=1, replica_groups=mesh['dp_0'=4,'dp_1'=2,'bucket_0'=4,'bucket_1'=8] {'bucket_0'}, use_global_device_ids=true, to_apply=%region_26.28 | all-reduce | flops 1024 | bytes 8192 | tf_op jit(solution)/shard_map/psum | solution.py:18
  142.6 15.9 %all-reduce.5 = (f32[512]{0:T(512)S(1)}, f32[512]{0:T(512)S(1)}) all-reduce(f32[512]{0:T(512)S(1)} %get-tuple-element.103, f32[512]{0:T(512)S(1)} %get-tuple-element.104), channel_id=1, replica_groups=mesh['dp_0'=4,'dp_1'=2,'bucket_0'=4,'bucket_1'=8] {'bucket_1'}, use_global_device_ids=true, to_apply=%region_27.29 | all-reduce | flops 1024 | bytes 8192 | tf_op jit(solution)/shard_map/psum | solution.py:18
  158.5 7.0 %multiply_reduce_fusion.4 = (f32[512]{0:T(512)S(1)}, f32[512]{0:T(512)S(1)}, f32[512]{0:T(512)S(1)}, f32[512]{0:T(512)S(1)}, f32[512]{0:T(512)S(1)}, /*index=5*/f32[512]{0:T(512)S(1)}, f32[768,512]{1,0:T(8,128)S(1)}) fusion(pred[768]{0:T(1024)(128)(4,1)S(1)} %get-tuple-element.48, bf16[1,768,512]{2,1,0:T(8,128)(2,1)} %copy-done.3, ...), kind=kLoop, calls=%fused_computation.76 | loop fusion | flops 11793408 | bytes 5532160 | tf_op jit(solution)/shard_map/reduce_sum | solution.py:77
  181.2 16.6 %reduce-scatter.17.cloned.1.call-done = f32[128,31]{0,1:T(8,128)} async-done(((f32[512,31]{0,1:T(8,128)}), f32[128,31]{0,1:T(8,128)}) %reduce-scatter.17.cloned.1.call-update) | async-done | bytes 15888 | tf_op jit(solution)/shard_map/reduce_scatter | solution.py:23
  199.3 12.0 %fusion.34 = (bf16[768,512]{1,0:T(8,128)(2,1)}, f32[1,768,512]{2,1,0:T(8,128)}) fusion(f32[768,1024]{1,0:T(8,128)} %copy-done.1, f32[512]{0:T(512)S(1)} %bitcast.278, pred[768]{0:T(1024)(128)(4,1)S(1)} %get-tuple-element.44, f32[512]{0:T(512)S(1)} %bitcast.280, pred[768]{0:T(1024)(128)(4,1)S(1)} %get-tuple-element.53, f32[512]{0:T(512)S(1)} %bitcast.284, ...), kind=kLoop, calls=%fused_computation.47 | loop fusion | flops 37748736 | bytes 7164416 | tf_op jit(solution)/shard_map/convert
  211.4 15.0 %reduce-scatter.13.cloned.1.call-done = f32[128,512]{1,0:T(8,128)} async-done(((f32[512,512]{1,0:T(8,128)}), f32[128,512]{1,0:T(8,128)}) %reduce-scatter.13.cloned.1.call-update) | async-done | bytes 262160 | tf_op jit(solution)/shard_map/reduce_scatter | solution.py:23
  239.9 8.5 %all-reduce.3 = f32[512]{0:T(512)S(1)} all-reduce(f32[512]{0:T(512)S(1)} %get-tuple-element.9), channel_id=8, replica_groups=mesh['dp_0'=4,'dp_1'=2,'bucket_0'=4,'bucket_1'=8] {'bucket_0'}, use_global_device_ids=true, to_apply=%region_71.73.clone | all-reduce | flops 512 | bytes 4096
  248.5 16.1 %all-reduce.4 = bf16[128]{0:T(256)(128)(2,1)S(1)} all-reduce(f32[128]{0:T(128)S(1)} %dynamic-slice.1), channel_id=9, replica_groups=mesh['dp_0'=4,'dp_1'=2,'bucket_0'=4,'bucket_1'=8] {'bucket_1'}, use_global_device_ids=true, to_apply=%region_72.74.clone | all-reduce | flops 128 | bytes 768
  280.3 5.4 %gather_fusion.1 = bf16[1536,512]{1,0:T(8,128)(2,1)} fusion(bf16[768,512]{1,0:T(8,128)(2,1)S(1)} %copy.66, s32[2048]{0:T(1024)S(1)} %pad_clamp_fusion), kind=kCustom, calls=%fused_computation.3 | custom fusion | bytes 3151872 | tf_op jit(solution)/shard_map/jit(_take)/gather | solution.py:180
  285.7 17.3 %reduce-scatter.15.cloned.1.call-done = f32[16,512]{1,0:T(8,128)} async-done(((f32[128,512]{1,0:T(8,128)}), f32[16,512]{1,0:T(8,128)}) %reduce-scatter.15.cloned.1.call-update) | async-done | bytes 32784 | tf_op jit(solution)/shard_map/reduce_scatter | solution.py:23
  314.8 8.1 %all-to-all-start.1 = ((bf16[32,1,48,512]{3,2,1,0:T(8,128)(2,1)}), bf16[32,1,48,512]{3,2,1,0:T(8,128)(2,1)S(1)}, u32[]{:S(2)}, u32[]{:S(2)}) async-start(bf16[32,1,48,512]{3,2,1,0:T(8,128)(2,1)} %select_select_fusion), calls=%async_computation.1 | async-start | bytes 3145728 | tf_op jit(solution)/shard_map/all_to_all | solution.py:181
  323.0 27.1 %reduce-scatter.9.cloned.1.call-done = f32[128,1024]{1,0:T(8,128)} async-done(((f32[512,1024]{1,0:T(8,128)}), f32[128,1024]{1,0:T(8,128)}) %reduce-scatter.9.cloned.1.call-update) | async-done | bytes 524304 | tf_op jit(solution)/shard_map/reduce_scatter | solution.py:23
  354.7 7.4 %all-to-all-done.1 = bf16[32,1,48,512]{3,2,1,0:T(8,128)(2,1)S(1)} async-done(((bf16[32,1,48,512]{3,2,1,0:T(8,128)(2,1)}), bf16[32,1,48,512]{3,2,1,0:T(8,128)(2,1)S(1)}, u32[]{:S(2)}, u32[]{:S(2)}) %all-to-all-start.1) | async-done | bytes 1572896 | tf_op jit(solution)/shard_map/all_to_all | solution.py:181
  363.9 26.1 %reduce-scatter.11.cloned.1.call-done = f32[16,1024]{1,0:T(8,128)} async-done(((f32[128,1024]{1,0:T(8,128)}), f32[16,1024]{1,0:T(8,128)}) %reduce-scatter.11.cloned.1.call-update) | async-done | bytes 65552 | tf_op jit(solution)/shard_map/reduce_scatter | solution.py:23
  398.6 4.8 %all-to-all-done.2 = bf16[8,16,1024]{2,1,0:T(8,128)(2,1)S(1)} async-done(((bf16[8,16,1024]{2,1,0:T(8,128)(2,1)}), bf16[8,16,1024]{2,1,0:T(8,128)(2,1)S(1)}, u32[]{:S(2)}, u32[]{:S(2)}) %all-to-all-start.2) | async-done | bytes 262176 | tf_op jit(solution)/shard_map/all_to_all | solution.py:29
  (163 shorter events, 100.3 us)
Async XLA Ops:
  13.2 11.4 %copy-start.11 = (s32[1,1024]{1,0:T(1,128)S(1)}, s32[1,1024]{1,0:T(1,128)}, u32[]{:S(2)}) copy-start(s32[1,1024]{1,0:T(1,128)} %param.14) | copy-start | bytes 12292
  13.2 11.6 %copy-start.12 = (s32[1,1024]{1,0:T(1,128)S(1)}, s32[1,1024]{1,0:T(1,128)}, u32[]{:S(2)}) copy-start(s32[1,1024]{1,0:T(1,128)} %param.13) | copy-start | bytes 12292
  13.2 35.3 %copy-start.10 = (f32[512,31]{0,1:T(8,128)S(1)}, f32[512,31]{0,1:T(8,128)}, u32[]{:S(2)}) copy-start(f32[512,31]{0,1:T(8,128)} %param.18) | copy-start | bytes 190468
  13.2 50.4 %all-to-all-start = ((bf16[32,1,48,512]{3,2,1,0:T(8,128)(2,1)}), bf16[32,1,48,512]{3,2,1,0:T(8,128)(2,1)S(1)}, u32[]{:S(2)}, u32[]{:S(2)}) async-start(bf16[32,1,48,512]{3,2,1,0:T(8,128)(2,1)} %select_bitcast_fusion), calls=%async_computation | async-start | bytes 3145728 | tf_op jit(solution)/shard_map/all_to_all | solution.py:112
  24.5 173.3 %reduce-scatter.17.cloned.1.call-start = ((), (), s32[]{:S(2)}) async-start(), calls=%async_computation.16 | async-start | bytes 81920 | tf_op jit(solution)/shard_map/reduce_scatter | solution.py:23
  71.5 11.5 %copy-start.3 = (bf16[1,768,512]{2,1,0:T(8,128)(2,1)}, bf16[1,768,512]{2,1,0:T(8,128)(2,1)S(1)}, u32[]{:S(2)}) copy-start(bf16[1,768,512]{2,1,0:T(8,128)(2,1)S(1)} %fusion.96) | copy-start | bytes 2359300
  83.1 40.6 %copy-start.5 = (f32[1,768,512]{2,1,0:T(8,128)}, f32[1,768,512]{2,1,0:T(8,128)S(1)}, u32[]{:S(2)}) copy-start(f32[1,768,512]{2,1,0:T(8,128)S(1)} %get-tuple-element.119) | copy-start | bytes 4718596
  83.1 36.6 %copy-start.14 = (f32[512]{0:T(512)S(1)}, f32[512]{0:T(512)}, u32[]{:S(2)}) copy-start(f32[512]{0:T(512)} %param.19) | copy-start | bytes 6148
  83.1 36.6 %copy-start.20 = (f32[512]{0:T(512)S(1)}, f32[512]{0:T(512)}, u32[]{:S(2)}) copy-start(f32[512]{0:T(512)} %param.20) | copy-start | bytes 6148
  158.5 7.1 %copy-start.15 = (f32[512]{0:T(512)}, f32[512]{0:T(512)S(1)}, u32[]{:S(2)}) copy-start(f32[512]{0:T(512)S(1)} %get-tuple-element.99) | copy-start | bytes 6148
  158.5 7.1 %copy-start.16 = (f32[512]{0:T(512)}, f32[512]{0:T(512)S(1)}, u32[]{:S(2)}) copy-start(f32[512]{0:T(512)S(1)} %get-tuple-element.100) | copy-start | bytes 6148
  158.5 7.1 %copy-start.4 = (bf16[1,768,512]{2,1,0:T(8,128)(2,1)S(1)}, bf16[1,768,512]{2,1,0:T(8,128)(2,1)}, u32[]{:S(2)}) copy-start(bf16[1,768,512]{2,1,0:T(8,128)(2,1)} %copy-done.3) | copy-start | bytes 2359300
  170.2 4.8 %copy-start.2 = (f32[768,1024]{1,0:T(8,128)S(1)}, f32[768,1024]{1,0:T(8,128)}, u32[]{:S(2)}) copy-start(f32[768,1024]{1,0:T(8,128)} %copy-done.1) | copy-start | bytes 9437188
  178.1 48.2 %reduce-scatter.13.cloned.1.call-start = ((), (), s32[]{:S(2)}) async-start(), calls=%async_computation.14 | async-start | bytes 1310720 | tf_op jit(solution)/shard_map/reduce_scatter | solution.py:23
  181.2 88.4 %reduce-scatter.19.cloned.1.call-start = ((), (), s32[]{:S(2)}) async-start(), calls=%async_computation.17 | async-start | bytes 73728 | tf_op jit(solution)/shard_map/reduce_scatter | solution.py:23
  199.3 103.7 %reduce-scatter.15.cloned.1.call-start = ((), (), s32[]{:S(2)}) async-start(), calls=%async_computation.15 | async-start | bytes 294912 | tf_op jit(solution)/shard_map/reduce_scatter | solution.py:23
  226.4 123.7 %reduce-scatter.9.cloned.1.call-start = ((), (), s32[]{:S(2)}) async-start(), calls=%async_computation.12 | async-start | bytes 2621440 | tf_op jit(solution)/shard_map/reduce_scatter | solution.py:23
  265.3 9.5 %all-to-all-start.5 = ((bf16[8,1,16]{2,1,0:T(2,128)(2,1)}), bf16[8,1,16]{2,1,0:T(2,128)(2,1)S(1)}, u32[]{:S(2)}, u32[]{:S(2)}) async-start(bf16[8,1,16]{2,1,0:T(2,128)(2,1)} %broadcast_in_dim.783), calls=%async_computation.10 | async-start | bytes 8192 | tf_op jit(solution)/shard_map/all_to_all | solution.py:29
  274.8 29.0 %all-to-all-start.4 = ((bf16[8,2,248]{2,1,0:T(2,128)(2,1)}), bf16[8,2,248]{2,1,0:T(2,128)(2,1)S(1)}, u32[]{:S(2)}, u32[]{:S(2)}) async-start(bf16[8,2,248]{2,1,0:T(2,128)(2,1)} %reshape.824), calls=%async_computation.9 | async-start | bytes 16384 | tf_op jit(solution)/shard_map/all_to_all | solution.py:29
  304.4 10.4 %all-to-all-start.3 = ((bf16[8,16,512]{2,1,0:T(8,128)(2,1)}), bf16[8,16,512]{2,1,0:T(8,128)(2,1)S(1)}, u32[]{:S(2)}, u32[]{:S(2)}) async-start(bf16[8,16,512]{2,1,0:T(8,128)(2,1)} %broadcast_in_dim.781), calls=%async_computation.7 | async-start | bytes 262144 | tf_op jit(solution)/shard_map/all_to_all | solution.py:29
  311.3 38.8 %copy-start.18 = (s32[32]{0:T(128)S(1)}, s32[32]{0:T(128)}, u32[]{:S(2)}) copy-start(s32[32]{0:T(128)} %copy-done.17) | copy-start | bytes 388
  314.8 47.3 %all-to-all-start.1 = ((bf16[32,1,48,512]{3,2,1,0:T(8,128)(2,1)}), bf16[32,1,48,512]{3,2,1,0:T(8,128)(2,1)S(1)}, u32[]{:S(2)}, u32[]{:S(2)}) async-start(bf16[32,1,48,512]{3,2,1,0:T(8,128)(2,1)} %select_select_fusion), calls=%async_computation.1 | async-start | bytes 3145728 | tf_op jit(solution)/shard_map/all_to_all | solution.py:181
  322.9 67.0 %reduce-scatter.11.cloned.1.call-start = ((), (), s32[]{:S(2)}) async-start(), calls=%async_computation.13 | async-start | bytes 589824 | tf_op jit(solution)/shard_map/reduce_scatter | solution.py:23
  391.5 11.8 %all-to-all-start.2 = ((bf16[8,16,1024]{2,1,0:T(8,128)(2,1)}), bf16[8,16,1024]{2,1,0:T(8,128)(2,1)S(1)}, u32[]{:S(2)}, u32[]{:S(2)}) async-start(bf16[8,16,1024]{2,1,0:T(8,128)(2,1)} %broadcast_in_dim.780), calls=%async_computation.4 | async-start | bytes 524288 | tf_op jit(solution)/shard_map/all_to_all | solution.py:29
  (11 other events, 23.4 us)
Sparse Core Ops, SparseCore 0:
  178.3 19.5 reduce-scatter.16
  200.5 25.7 reduce-scatter.12
  229.4 35.5 reduce-scatter.18
  267.6 35.3 reduce-scatter.14
  305.4 44.6 reduce-scatter.8
  352.6 37.3 reduce-scatter.10
where the time goes:
time: 414 us; the launch traced here: 411 us
  waiting for transfers between devices  137 us (33%)
  blocking collectives  95.8 us (23%)
  other arithmetic  81.7 us (20%)
  starting transfers between devices  35.8 us (9%)
  local copies, waits for them, and re-layouts  27.9 us (7%)
  matrix products  16.9 us (4%)
  between operations  16 us (4%)
    reduce_scatter x6, waiting for transfers between devices, scatter_axes(): value = lax.psum_scatter(value, axis, scatter_dimension=dim, tiled=True)  102 us
    psum x8, blocking collectives, by_axis(): return functools.reduce(lax.psum, axes, value)  71.2 us
    unnamed x2, blocking collectives  24.6 us
    reduce_sum x6, other arithmetic, conv_backward(): grad_cols.append(jnp.sum(shifted * grad_conv, axis=(0, 1)))  17 us
    all_to_all x4, starting transfers between devices, sent_to_all(): return lax.all_to_all(copies, axis, split_axis=0, concat_axis=0, tiled=True)  16.2 us
    and x1, other arithmetic, local(): work_frames = jnp.take(incoming_rows, packed_source, axis=0)  15.7 us
    another operation x4, other arithmetic  15.3 us
    all_to_all x1, waiting for transfers between devices, local(): lax.all_to_all(outgoing, BUCKET, split_axis=0, concat_axis=0, tiled=True)  15.1 us
  transfers between devices with their start and end apart: 12, of which 10 were waited for; matrix products, arithmetic and copies ran while one was open for 18% of the time, Pallas kernels for 0%

commit v1 on v0

v1 whole, which is shorter than its diff:
```python
import functools
import math

import jax
import jax.numpy as jnp
import numpy as np
from jax import lax
from jax.experimental import pallas as pl
from jax.experimental.pallas import tpu as pltpu
from jax.sharding import Mesh
from jax.sharding import PartitionSpec as P

BUCKET = ("x", "z")
DP = ("y", "c")
EVERY = ("y", "c", "x", "z")
FIRST = ("c", "z")
SECOND = ("y", "x")

EPSILON = 1e-05
SPAN = 48
POINTS = 64
HALF = POINTS // 2
PER_DFT = 4
PER_STEP = 8
VMEM_LIMIT = 40 * 2**20

F32 = jnp.float32
BF16 = jnp.bfloat16


def dot(a, b, dims=((1,), (0,)), precision=None):
    return lax.dot_general(a, b, (dims, ((), ())), preferred_element_type=F32, precision=precision)


def tables(taps):
    f = np.arange(HALF)[:, None]
    t = np.arange(SPAN)[None, :]
    angle = 2 * np.pi * f * t / POINTS
    real = np.cos(angle) * math.sqrt(2 / POINTS)
    imag = -np.sin(angle) * math.sqrt(2 / POINTS)
    real[0] = math.sqrt(1 / POINTS)
    imag[0] = math.sqrt(1 / POINTS) * (-1.0) ** np.arange(SPAN)
    block = np.zeros((2 * HALF * PER_DFT, SPAN * PER_DFT))
    for u in range(PER_DFT):
        block[u * HALF : (u + 1) * HALF, u * SPAN : (u + 1) * SPAN] = real
        block[(PER_DFT + u) * HALF : (PER_DFT + u + 1) * HALF, u * SPAN : (u + 1) * SPAN] = imag
    lag = np.arange(taps)[None, :] - taps // 2
    turn = 2 * np.pi * f * lag / POINTS
    cos, sin = np.cos(turn), np.sin(turn)
    cos_last = cos.copy()
    cos_last[0] = np.cos(np.pi * lag[0])
    taps_to = np.concatenate([cos, sin, cos_last], axis=0)
    back = np.zeros((2 * HALF + 8, 128))
    back[:HALF, :taps] = cos
    back[HALF : 2 * HALF, :taps] = -sin
    back[HALF, :taps] = np.cos(np.pi * lag[0])
    back[2 * HALF :, taps] = 1.0
    high = block.astype(jnp.bfloat16)
    low = (block - high.astype(np.float64)).astype(jnp.bfloat16)
    return (
        high,
        low,
        np.ascontiguousarray(high.T),
        np.ascontiguousarray(low.T),
        taps_to.astype(np.float32),
        back.astype(np.float32),
    )


def masked(value, lens):
    t = lax.broadcasted_iota(jnp.int32, (SPAN, value.shape[1]), 0)
    return jnp.concatenate(
        [
            jnp.where(t < n, value[u * SPAN : (u + 1) * SPAN], jnp.zeros((), value.dtype))
            for u, n in enumerate(lens)
        ],
        axis=0,
    )


def folded(value):
    return jnp.sum(value.reshape(-1, 8, value.shape[1]), axis=0)


def as_tile(first, second):
    rows = [v[:, k * 128 : (k + 1) * 128] for v in (first, second) for k in range(4)]
    return jnp.concatenate(rows, axis=0)


def from_tile(tile):
    rows = [tile[k : k + 1] for k in range(8)]
    return (jnp.concatenate(rows[:4], axis=1), jnp.concatenate(rows[4:], axis=1))


def normalize(x, gain):
    centred = x - jnp.mean(x, axis=1, keepdims=True)
    inverse = lax.rsqrt(jnp.mean(centred * centred, axis=1, keepdims=True) + EPSILON)
    normed = centred * inverse
    return (normed * gain).astype(BF16), normed, inverse


def spread(wf, part):
    rows = wf[part * HALF : (part + 1) * HALF]
    return jnp.concatenate([rows] * PER_DFT, axis=0)


def unpack_kernel(lens_ref, upstream_ref, out_ref, wide):
    rows = upstream_ref.shape[0]
    wide[:rows, :] = upstream_ref[...].astype(F32)
    wide[rows:, :] = jnp.zeros((8, wide.shape[1]), F32)
    count = out_ref.shape[0] // SPAN

    def step(i, start):
        base = pl.multiple_of(start // 8 * 8, 8)
        window = pltpu.roll(wide[pl.ds(base, SPAN + 8), :], SPAN + 8 - start % 8, 0)
        out_ref[pl.ds(pl.multiple_of(i * SPAN, 16), SPAN), :] = window[:SPAN].astype(BF16)
        return start + lens_ref[i]

    lax.fori_loop(0, count, step, jnp.int32(0))


def pack_kernel(lens_ref, got_ref, out_ref, wide):
    count = got_ref.shape[0] // SPAN
    top = lax.broadcasted_iota(jnp.int32, (8, got_ref.shape[1]), 0)

    def step(i, start):
        base = pl.multiple_of(start // 8 * 8, 8)
        rows = got_ref[pl.ds(pl.multiple_of(i * SPAN, 16), SPAN), :].astype(F32)
        window = jnp.concatenate([rows, jnp.zeros((8, rows.shape[1]), F32)], axis=0)
        window = pltpu.roll(window, start % 8, 0)
        kept = jnp.where(top < start % 8, wide[pl.ds(base, 8), :], window[:8])
        wide[pl.ds(base, 8), :] = kept
        wide[pl.ds(base + 8, SPAN), :] = window[8:]
        return start + lens_ref[i]

    lax.fori_loop(0, count, step, jnp.int32(0))
    out_ref[...] = wide[: out_ref.shape[0], :].astype(BF16)


def step_lens(lens_ref):
    return [lens_ref[pl.program_id(0) * PER_STEP + u] for u in range(PER_STEP)]


def slot_rows(slots_ref, u):
    slot = slots_ref[pl.program_id(0) * PER_STEP + u]
    return pl.ds(pl.multiple_of(slot * SPAN, 16), SPAN)


def forward_kernel(
    lens_ref, slots_ref, frames_ref, gain_ref, win_ref, qh_ref, ql_ref, ih_ref, il_ref, to_ref, wdw_ref,
    lin_ref, sig_ref, freq_ref, conv_ref, wf_ref, stats_ref, acc,
):
    step = pl.program_id(0)

    @pl.when(step == 0)
    def _():
        wf_ref[...] = dot(to_ref[...], wdw_ref[...], ((1,), (1,)), lax.Precision.HIGHEST)
        acc[...] = jnp.zeros_like(acc)

    d = frames_ref.shape[1]
    lens = step_lens(lens_ref)
    x = jnp.concatenate([frames_ref[slot_rows(slots_ref, u), :] for u in range(PER_STEP)], axis=0)
    h, _, _ = normalize(x.astype(F32), gain_ref[...])
    a = dot(h, win_ref[...])
    lin = a[:, :d]
    sig = jax.nn.sigmoid(a[:, d:])
    lin_ref[...] = lin.astype(BF16)
    sig_ref[...] = sig.astype(BF16)
    gated = masked(lin * sig, lens).astype(BF16)
    wa, wb, wl = (spread(wf_ref[...], k) for k in range(3))
    for b in range(PER_STEP // PER_DFT):
        rows = slice(b * SPAN * PER_DFT, (b + 1) * SPAN * PER_DFT)
        part = gated[rows]
        spec = dot(qh_ref[...], part) + dot(ql_ref[...], part)
        freq_ref[b * POINTS * PER_DFT : (b + 1) * POINTS * PER_DFT, :] = spec.astype(BF16)
        re, im = spec[: HALF * PER_DFT], spec[HALF * PER_DFT :]
        turned = jnp.concatenate([re * wa - im * wb, im * wl + re * wb], axis=0)
        high = turned.astype(BF16)
        low = (turned - high.astype(F32)).astype(BF16)
        conv = dot(ih_ref[...], high) + dot(il_ref[...], high) + dot(ih_ref[...], low)
        conv_ref[rows, :] = conv
        live = masked(conv, lens[b * PER_DFT : (b + 1) * PER_DFT])
        acc[0] += folded(live)
        acc[1] += folded(live * live)

    @pl.when(step == pl.num_programs(0) - 1)
    def _():
        sums = [jnp.sum(acc[k], axis=0, keepdims=True) for k in range(2)]
        stats_ref[...] = jnp.broadcast_to(as_tile(*sums)[None], stats_ref.shape)


def relay_kernel(got_ref, out_ref):
    out_ref[...] = jnp.broadcast_to(jnp.sum(got_ref[...], axis=0)[None], out_ref.shape)


def bn_terms(stats, gain_ref, total):
    first, second = from_tile(jnp.sum(stats, axis=0))
    centre = first / total
    inverse = lax.rsqrt(second / total - centre * centre + EPSILON)
    return centre, inverse


def middle_kernel(
    total, lens_ref, conv_ref, dy_ref, stats_ref, gain_ref, bias_ref, wout_ref,
    out_ref, gbn_ref, gwout_ref, sums_ref, acc, sw_all, dy_all,
):
    step = pl.program_id(0)

    @pl.when(step == 0)
    def _():
        acc[...] = jnp.zeros_like(acc)

    centre, inverse = bn_terms(stats_ref[...], gain_ref, total)
    normed = (conv_ref[...] - centre) * inverse
    value = normed * gain_ref[...] + bias_ref[...]
    sig = jax.nn.sigmoid(value)
    swished = (value * sig).astype(BF16)
    out_ref[...] = dot(swished, wout_ref[...]).astype(BF16)
    dy = masked(dy_ref[...].astype(F32), step_lens(lens_ref)).astype(BF16)
    rows = pl.ds(pl.multiple_of(step * PER_STEP * SPAN, 16), PER_STEP * SPAN)
    sw_all[rows, :] = swished
    dy_all[rows, :] = dy
    grad = dot(dy, wout_ref[...], ((1,), (1,))) * (sig * (1.0 + value * (1.0 - sig)))
    gbn_ref[...] = grad
    acc[0] += folded(grad)
    acc[1] += folded(grad * normed)

    @pl.when(step == pl.num_programs(0) - 1)
    def _():
        sums = [jnp.sum(acc[k], axis=0, keepdims=True) for k in range(2)]
        sums_ref[...] = jnp.broadcast_to(as_tile(*sums)[None], sums_ref.shape)
        gwout_ref[...] = dot(sw_all[...], dy_all[...], ((0,), (0,))).astype(BF16)


def backward_kernel(
    total, lens_ref, slots_ref, frames_ref, lin_ref, sig_ref, freq_ref, conv_ref, gbn_ref, wf_ref, stats_ref, sums_ref,
    bn_gain_ref, gain_ref, win_ref, qh_ref, ih_ref, back_ref,
    gframes_ref, gwin_ref, small_ref, bias_ref, bn_out_ref, acc, h_all, ga_all,
):
    step = pl.program_id(0)

    @pl.when(step == 0)
    def _():
        acc[...] = jnp.zeros_like(acc)

    lens = step_lens(lens_ref)
    centre, inverse = bn_terms(stats_ref[...], None, total)
    bias_total, gain_total = from_tile(jnp.sum(sums_ref[...], axis=0))
    bias_ref[...] = bias_total
    bn_out_ref[...] = gain_total
    normed_bn = (conv_ref[...] - centre) * inverse
    scale = bn_gain_ref[...] * inverse
    grad_conv = scale * (gbn_ref[...] - bias_total / total - normed_bn * (gain_total / total))
    grad_conv = masked(grad_conv, lens).astype(BF16)
    wa, wb, wl = (spread(wf_ref[...], k) for k in range(3))
    n = HALF * PER_DFT
    edge = lax.broadcasted_iota(jnp.int32, (n, wa.shape[1]), 0) % HALF == 0
    parts = []
    for b in range(PER_STEP // PER_DFT):
        rows = slice(b * SPAN * PER_DFT, (b + 1) * SPAN * PER_DFT)
        spec = dot(qh_ref[...], grad_conv[rows])
        re, im = spec[:n], spec[n:]
        own = freq_ref[b * 2 * n : (b + 1) * 2 * n, :].astype(F32)
        own_re, own_im = own[:n], own[n:]
        both = im * own_im
        corr_re = re * own_re + jnp.where(edge, 0.0, both)
        corr_im = jnp.where(edge, both, re * own_im - im * own_re)
        acc[0:HALF] += jnp.sum(corr_re.reshape(PER_DFT, HALF, -1), axis=0)
        acc[HALF : 2 * HALF] += jnp.sum(corr_im.reshape(PER_DFT, HALF, -1), axis=0)
        turned = jnp.concatenate([re * wa + im * wb, im * wl - re * wb], axis=0).astype(BF16)
        parts.append(dot(ih_ref[...], turned))
    grad_gated = masked(jnp.concatenate(parts, axis=0), lens)
    lin = lin_ref[...].astype(F32)
    sig = sig_ref[...].astype(F32)
    first = grad_gated * sig
    grad_a = jnp.concatenate([first, first * lin * (1.0 - sig)], axis=1).astype(BF16)
    grad_h = dot(grad_a, win_ref[...], ((1,), (1,)))
    x = jnp.concatenate([frames_ref[slot_rows(slots_ref, u), :] for u in range(PER_STEP)], axis=0)
    gain = gain_ref[...]
    h, normed, inv = normalize(x.astype(F32), gain)
    rows = pl.ds(pl.multiple_of(step * PER_STEP * SPAN, 16), PER_STEP * SPAN)
    h_all[rows, :] = h
    ga_all[rows, :] = grad_a
    acc[2 * HALF :] += folded(grad_h * normed)
    scaled = grad_h * gain
    inner = jnp.mean(scaled * normed, axis=1, keepdims=True)
    grad_x = inv * (scaled - jnp.mean(scaled, axis=1, keepdims=True) - normed * inner)
    grad_x = masked(grad_x, lens).astype(BF16)
    for u in range(PER_STEP):
        gframes_ref[slot_rows(slots_ref, u), :] = grad_x[u * SPAN : (u + 1) * SPAN]

    @pl.when(step == pl.num_programs(0) - 1)
    def _():
        gwin_ref[...] = dot(h_all[...], ga_all[...], ((0,), (0,))).astype(BF16)
        small_ref[...] = dot(acc[...], back_ref[...], ((0,), (0,)), lax.Precision.HIGHEST).astype(BF16)


SMEM = pl.BlockSpec(memory_space=pltpu.SMEM)


def whole(shape):
    return pl.BlockSpec(shape, lambda i: (0,) * len(shape))


def rows_of(shape, steps):
    return pl.BlockSpec((shape[0] // steps, shape[1]), lambda i: (i, 0))


def params():
    return pltpu.CompilerParams(dimension_semantics=("arbitrary",), vmem_limit_bytes=VMEM_LIMIT)


def sds(shape, dtype):
    return jax.ShapeDtypeStruct(shape, dtype)


def unpack(lens, upstream, rows):
    return pl.pallas_call(
        unpack_kernel,
        out_shape=sds((rows, upstream.shape[1]), BF16),
        in_specs=[SMEM, pl.BlockSpec(memory_space=pltpu.VMEM)],
        out_specs=pl.BlockSpec(memory_space=pltpu.VMEM),
        scratch_shapes=[pltpu.VMEM((upstream.shape[0] + 8, upstream.shape[1]), F32)],
        compiler_params=pltpu.CompilerParams(vmem_limit_bytes=VMEM_LIMIT),
        name="unpack",
    )(lens, upstream)


def pack(lens, got, rows):
    return pl.pallas_call(
        pack_kernel,
        out_shape=sds((rows, got.shape[1]), BF16),
        in_specs=[SMEM, pl.BlockSpec(memory_space=pltpu.VMEM)],
        out_specs=pl.BlockSpec(memory_space=pltpu.VMEM),
        scratch_shapes=[pltpu.VMEM((rows + 8, got.shape[1]), F32)],
        compiler_params=pltpu.CompilerParams(vmem_limit_bytes=VMEM_LIMIT),
        name="pack",
    )(lens, got)


def forward(lens, slots, frames, gain, w_in, w_dw, tabs, copies):
    high, low, high_t, low_t, taps_to, _ = tabs
    rows, d = frames.shape
    steps = rows // (SPAN * PER_STEP)
    freq = (rows // SPAN * POINTS, d)
    return pl.pallas_call(
        forward_kernel,
        grid=(steps,),
        out_shape=(
            sds((rows, d), BF16),
            sds((rows, d), BF16),
            sds(freq, BF16),
            sds((rows, d), F32),
            sds((3 * HALF, d), F32),
            sds((copies, 8, 128), F32),
        ),
        in_specs=[SMEM, SMEM, whole(frames.shape), whole(gain.shape), whole(w_in.shape)]
        + [whole(v.shape) for v in (high, low, high_t, low_t, taps_to, w_dw)],
        out_specs=(
            rows_of((rows, d), steps),
            rows_of((rows, d), steps),
            rows_of(freq, steps),
            rows_of((rows, d), steps),
            whole((3 * HALF, d)),
            whole((copies, 8, 128)),
        ),
        scratch_shapes=[pltpu.VMEM((2, 8, d), F32)],
        compiler_params=params(),
        name="forward",
    )(lens, slots, frames, gain, w_in, high, low, high_t, low_t, taps_to, w_dw)


def relay(got, copies):
    return pl.pallas_call(
        relay_kernel,
        out_shape=sds((copies, 8, 128), F32),
        in_specs=[pl.BlockSpec(memory_space=pltpu.VMEM)],
        out_specs=pl.BlockSpec(memory_space=pltpu.VMEM),
        name="relay",
    )(got)


def middle(total, lens, conv, dy, stats, bn_gain, bn_bias, w_out, copies):
    rows, d = conv.shape
    steps = rows // (SPAN * PER_STEP)
    part = rows_of((rows, d), steps)
    return pl.pallas_call(
        functools.partial(middle_kernel, total),
        grid=(steps,),
        out_shape=(
            sds((rows, d), BF16),
            sds((rows, d), F32),
            sds((d, d), BF16),
            sds((copies, 8, 128), F32),
        ),
        in_specs=[SMEM, part, part] + [whole(v.shape) for v in (stats, bn_gain, bn_bias, w_out)],
        out_specs=(part, part, whole((d, d)), whole((copies, 8, 128))),
        scratch_shapes=[pltpu.VMEM((2, 8, d), F32), pltpu.VMEM((rows, d), BF16), pltpu.VMEM((rows, d), BF16)],
        compiler_params=params(),
        name="middle",
    )(lens, conv, dy, stats, bn_gain, bn_bias, w_out)


def backward(total, lens, slots, frames, lin, sig, freq, conv, gbn, wf, stats, sums, bn_gain, gain, w_in, tabs):
    high, _, high_t, _, _, back = tabs
    rows, d = frames.shape
    steps = rows // (SPAN * PER_STEP)
    part = rows_of((rows, d), steps)
    return pl.pallas_call(
        functools.partial(backward_kernel, total),
        grid=(steps,),
        out_shape=(
            sds((rows, d), BF16),
            sds((d, 2 * d), BF16),
            sds((d, 128), BF16),
            sds((1, d), F32),
            sds((1, d), F32),
        ),
        in_specs=[SMEM, SMEM, whole(frames.shape), part, part, rows_of(freq.shape, steps), part, part]
        + [whole(v.shape) for v in (wf, stats, sums, bn_gain, gain, w_in, high, high_t, back)],
        out_specs=(whole((rows, d)), whole((d, 2 * d)), whole((d, 128)), whole((1, d)), whole((1, d))),
        scratch_shapes=[
            pltpu.VMEM((2 * HALF + 8, d), F32),
            pltpu.VMEM((rows, d), BF16),
            pltpu.VMEM((rows, 2 * d), BF16),
        ],
        compiler_params=params(),
        name="backward",
    )(lens, slots, frames, lin, sig, freq, conv, gbn, wf, stats, sums, bn_gain, gain, w_in, high, high_t, back)


def swapped(value, axes):
    return lax.all_to_all(value, axes, split_axis=0, concat_axis=0, tiled=True)


def to_everyone(tiles):
    return swapped(relay(swapped(tiles, FIRST), lax.axis_size(SECOND)), SECOND)


def local(frames, lengths, owners, upstream, ln_gain, w_in, w_dw, bn_gain, bn_bias, w_out):
    loaders = lax.axis_size(BUCKET)
    me = lax.axis_index(BUCKET)
    d = frames.shape[1]
    rows = frames.shape[0]
    taps = w_dw.shape[1]
    total = float(upstream.shape[0] * loaders * lax.axis_size(DP))
    lens_all = lengths.reshape(loaders, loaders)
    dest_all = owners.reshape(loaders, loaders)
    got_lens = jnp.sum(jnp.where(dest_all == me, lens_all, 0), axis=1)
    mine = lax.dynamic_index_in_dim(lens_all, me, 0, keepdims=False)
    to = lax.dynamic_index_in_dim(dest_all, me, 0, keepdims=False)
    ids = jnp.arange(loaders, dtype=jnp.int32)
    hit = to[None, :] == ids[:, None]
    lens = jnp.sum(jnp.where(hit, mine[None, :], 0), axis=1)
    slots = jnp.sum(jnp.where(hit, ids[None, :], 0), axis=1)
    tabs = tuple(jnp.asarray(v) for v in tables(taps))
    gain, bn_gain, bn_bias = (v.reshape(1, d) for v in (ln_gain, bn_gain, bn_bias))

    dy = unpack(got_lens, upstream, rows)
    dy = swapped(dy.reshape(loaders, SPAN, d), BUCKET).reshape(rows, d)
    lin, sig, freq, conv, wf, stats = forward(
        lens, slots, frames, gain, w_in, w_dw, tabs, lax.axis_size(FIRST)
    )
    stats = to_everyone(stats)
    out, gbn, gwout, sums = middle(total, lens, conv, dy, stats, bn_gain, bn_bias, w_out, lax.axis_size(FIRST))
    sums = to_everyone(sums)
    out = swapped(out.reshape(loaders, SPAN, d), BUCKET).reshape(rows, d)
    gframes, gwin, small, bias_total, gain_total = backward(
        total, lens, slots, frames, lin, sig, freq, conv, gbn, wf, stats, sums, bn_gain, gain, w_in, tabs
    )
    share = d // loaders
    grads = jnp.concatenate([gwin, gwout, small], axis=1)
    grads = swapped(grads.reshape(loaders, share, -1), BUCKET)
    grads = jnp.sum(grads.astype(F32), axis=0).astype(BF16)
    grads = swapped(jnp.broadcast_to(grads, (lax.axis_size(DP), *grads.shape)), DP)
    grads = jnp.sum(grads.astype(F32), axis=0)
    out_frames = pack(got_lens, out, upstream.shape[0])
    return (
        out_frames,
        gframes,
        grads[:, : 2 * d],
        grads[:, 2 * d : 3 * d],
        grads[:, 3 * d : 3 * d + taps],
        grads[:, 3 * d + taps],
        gain_total.reshape(d),
        bias_total.reshape(d),
    )


def solution(mesh):
    torus = Mesh(mesh.devices.reshape(4, 2, 4, 8), ("y", "c", "x", "z"))
    in_specs = (P(EVERY, None), P(DP, None), P(DP, None), P(EVERY, None)) + (P(),) * 6
    out_specs = (P(EVERY, None), P(EVERY, None), P(BUCKET, None), P(BUCKET, None), P(BUCKET, None), P(BUCKET), P(), P())
    return jax.shard_map(local, mesh=torus, in_specs=in_specs, out_specs=out_specs, check_vma=False)
```

time: 414 us -> 261 us (0.63)
  waiting for transfers between devices: 137 us -> 48.3 us
  other arithmetic: 81.7 us -> 3.35 us
  Pallas kernels: 0 us -> 33.6 us
  blocking collectives: 95.8 us -> 128 us
  starting transfers between devices: 35.8 us -> 15.5 us
  matrix products: 16.9 us -> 0 us
  between operations: 16 us -> 0.83 us
    all_to_all x0 -> x5, blocking collectives: none -> 128 us  [swapped(): return lax.all_to_all(value, axes, split_axis=0, concat_axis=0, tiled=True)]
    reduce_scatter x6 -> x0, waiting for transfers between devices: 102 us -> none  [scatter_axes(): value = lax.psum_scatter(value, axis, scatter_dimension=dim, tiled=True)]
    psum x8 -> x0, blocking collectives: 71.2 us -> none  [by_axis(): return functools.reduce(lax.psum, axes, value)]
    pallas_call x0 -> x7, Pallas kernels: none -> 33.6 us  [the longest x1 12.1 us: backward(): pl.pallas_call(functools.partial(backward_kernel, total), grid=(steps,),...]
    reduce_sum x16 -> x4, other arithmetic: 30.6 us -> 0.53 us  [the longest x1 0.25 us: local(): grads = jnp.sum(grads.astype(F32), axis=0).astype(BF16)]
    unnamed x2 -> x0, blocking collectives: 24.6 us -> none
    all_to_all x6 -> x3, starting transfers between devices: 35.6 us -> 15.5 us  [swapped(): return lax.all_to_all(value, axes, split_axis=0, concat_axis=0, tiled=True)]
    unnamed x54 -> x62, local copies, waits for them, and re-layouts: 7.74 us -> 26.3 us
  transfers between devices with their start and end apart: 12 -> 3, of which waited for: 10 -> 3; matrix products, arithmetic and copies ran while one was open for 18% -> 0% of each run, Pallas kernels for 0% -> 2%
where the time goes in v1:
time: 261 us; the launch traced here: 259 us
  blocking collectives  128 us (49%)
  waiting for transfers between devices  48.3 us (19%)
  Pallas kernels  33.6 us (13%)
  local copies, waits for them, and re-layouts  29.8 us (11%)
  starting transfers between devices  15.5 us (6%)
  other arithmetic  3.35 us (1%)
    all_to_all x5, blocking collectives, swapped(): return lax.all_to_all(value, axes, split_axis=0, concat_axis=0, tiled=True)  128 us
    all_to_all x3, waiting for transfers between devices, swapped(): return lax.all_to_all(value, axes, split_axis=0, concat_axis=0, tiled=True)  48.3 us
    unnamed x62, local copies, waits for them, and re-layouts  26.3 us
    all_to_all x3, starting transfers between devices, swapped(): return lax.all_to_all(value, axes, split_axis=0, concat_axis=0, tiled=True)  15.5 us
    pallas_call x1, Pallas kernels, backward(): pl.pallas_call(functools.partial(backward_kernel, total), grid=(steps,),...  12.1 us
    pallas_call x1, Pallas kernels, forward(): pl.pallas_call(forward_kernel, grid=(steps,), out_shape=(sds((rows, d), B...  8.69 us
    pallas_call x1, Pallas kernels, middle(): pl.pallas_call(functools.partial(middle_kernel, total), grid=(steps,), ou...  5.44 us
  transfers between devices with their start and end apart: 3, of which 3 were waited for; matrix products, arithmetic and copies ran while one was open for 0% of the time, Pallas kernels for 2%

profile of v1, /device:TPU:32, one launch (start us, length us, event | category | flops | bytes accessed | tf_op | source)
XLA Modules:
  0.0 259.1 jit_solution(17187889634874419509)
XLA Ops:
  5.1 1.4 copy-done
  12.8 8.7 %forward.1 = (bf16[1536,512]{1,0:T(8,128)(2,1)S(1)}, bf16[1536,512]{1,0:T(8,128)(2,1)S(1)}, bf16[2048,512]{1,0:T(8,128)(2,1)S(1)}, f32[1536,512]{1,0:T(8,128)S(1...) custom-call(s32[32]{0:T(128)S(1)} %get-tuple-element.39.lens_ref, s32[32]{0:T(128)S(1)} %get-tuple-element.38.slots_ref, ...), custom_call_target="tpu_custom_call" | custom-call | tf_op jit(solution)/shard_map/forward/pallas_call | solution.py:346
  25.9 15.5 %all_to_all.40.got_ref = f32[16,8,128]{2,1,0:T(8,128)} all-to-all(f32[16,8,128]{2,1,0:T(8,128)S(1)} %get-tuple-element.24), channel_id=1, replica_groups=mesh['y'=4,'c'=2,'x'=4,'z'=8] {'c','z'}, dimensions={0} | all-to-all | bytes 131072 | tf_op jit(solution)/shard_map/all_to_all | solution.py:433
  41.4 1.5 relay.2
  42.9 7.0 %all-to-all-start.2 = ((f32[16,8,128]{2,1,0:T(8,128)}), f32[16,8,128]{2,1,0:T(8,128)S(1)}, u32[]{:S(2)}, u32[]{:S(2)}) async-start(f32[16,8,128]{2,1,0:T(8,128)} %relay.2), calls=%async_computation.2 | async-start | bytes 131072 | tf_op jit(solution)/shard_map/all_to_all | solution.py:433
  51.2 1.7 unpack.1
  54.1 3.5 %all-to-all-done.2.stats_ref = f32[16,8,128]{2,1,0:T(8,128)S(1)} async-done(((f32[16,8,128]{2,1,0:T(8,128)}), f32[16,8,128]{2,1,0:T(8,128)S(1)}, u32[]{:S(2)}, u32[]{:S(2)}) %all-to-all-start.2) | async-done | bytes 65568 | tf_op jit(solution)/shard_map/all_to_all | solution.py:433
  57.6 43.7 %all_to_all.41 = bf16[32,48,512]{2,1,0:T(8,128)(2,1)S(1)} all-to-all(bf16[32,48,512]{2,1,0:T(8,128)(2,1)} %bitcast.15), channel_id=1, replica_groups=mesh['y'=4,'c'=2,'x'=4,'z'=8] {'x','z'}, dimensions={0} | all-to-all | bytes 3145728 | tf_op jit(solution)/shard_map/all_to_all | solution.py:433
  101.3 5.4 %middle.1 = (bf16[1536,512]{1,0:T(8,128)(2,1)}, f32[1536,512]{1,0:T(8,128)S(1)}, bf16[512,512]{1,0:T(8,128)(2,1)S(1)}, f32[16,8,128]{2,1,0:T(8,128)S(1)}) custom-call(s32[32]{0:T(128)S(1)} %get-tuple-element.39.lens_ref, f32[1536,512]{1,0:T(8,128)S(1)} %get-tuple-element.23.conv_ref, bf16[1536,512]{1,0:T(8,128)(2,1)S(1)} %bitcast.16, ...), custom_call_target="tpu_custom_call" | custom-call | tf_op jit(solution)/shard_map/middle/pallas_call | solution.py:387
  106.8 1.6 copy-done.5
  109.2 10.8 %all_to_all.42.got_ref = f32[16,8,128]{2,1,0:T(8,128)} all-to-all(f32[16,8,128]{2,1,0:T(8,128)S(1)} %get-tuple-element.31), channel_id=1, replica_groups=mesh['y'=4,'c'=2,'x'=4,'z'=8] {'c','z'}, dimensions={0} | all-to-all | bytes 131072 | tf_op jit(solution)/shard_map/all_to_all | solution.py:433
  120.0 1.5 relay.3
  121.5 11.9 %all_to_all.43.sums_ref = f32[16,8,128]{2,1,0:T(8,128)S(1)} all-to-all(f32[16,8,128]{2,1,0:T(8,128)} %relay.3), channel_id=1, replica_groups=mesh['y'=4,'c'=2,'x'=4,'z'=8] {'y','x'}, dimensions={0} | all-to-all | bytes 131072 | tf_op jit(solution)/shard_map/all_to_all | solution.py:433
  133.4 1.4 copy-done.1
  136.0 1.6 copy-done.7
  137.6 1.4 copy-done.9
  139.0 1.4 copy-done.11
  141.4 12.1 %backward.1 = (bf16[1536,512]{1,0:T(8,128)(2,1)}, bf16[512,1024]{1,0:T(8,128)(2,1)S(1)}, bf16[512,128]{1,0:T(8,128)(2,1)S(1)}, f32[1,512]{1,0:T(1,128)}, f32[1,512]{1,0:T(1,128)}) custom-call(s32[32]{0:T(128)S(1)} %get-tuple-element.39.lens_ref, s32[32]{0:T(128)S(1)} %get-tuple-element.38.slots_ref, bf16[1536,512]{1,0:T(8,128)(2,1)S(1)} %copy-done.1, ...), custom_call_target="tpu_custom_call" | custom-call | tf_op jit(solution)/shard_map/backward/pallas_call | solution.py:409
  153.6 45.9 %all_to_all.44 = bf16[32,16,1664]{2,1,0:T(8,128)(2,1)S(1)} all-to-all(bf16[32,16,1664]{2,1,0:T(8,128)(2,1)S(1)} %bitcast.22), channel_id=1, replica_groups=mesh['y'=4,'c'=2,'x'=4,'z'=8] {'x','z'}, dimensions={0} | all-to-all | bytes 3407872 | tf_op jit(solution)/shard_map/all_to_all | solution.py:433
  199.5 5.0 %all-to-all-start.3 = ((bf16[32,48,512]{2,1,0:T(8,128)(2,1)}), bf16[32,48,512]{2,1,0:T(8,128)(2,1)S(1)}, u32[]{:S(2)}, u32[]{:S(2)}) async-start(bf16[32,48,512]{2,1,0:T(8,128)(2,1)} %bitcast.7), calls=%async_computation.3 | async-start | bytes 3145728 | tf_op jit(solution)/shard_map/all_to_all | solution.py:433
  204.8 38.2 %all-to-all-done.3 = bf16[32,48,512]{2,1,0:T(8,128)(2,1)S(1)} async-done(((bf16[32,48,512]{2,1,0:T(8,128)(2,1)}), bf16[32,48,512]{2,1,0:T(8,128)(2,1)S(1)}, u32[]{:S(2)}, u32[]{:S(2)}) %all-to-all-start.3) | async-done | bytes 1572896 | tf_op jit(solution)/shard_map/all_to_all | solution.py:433
  243.8 3.5 %all-to-all-start.7 = ((bf16[8,16,1664]{2,1,0:T(8,128)(2,1)}), bf16[8,16,1664]{2,1,0:T(8,128)(2,1)S(1)}, u32[]{:S(2)}, u32[]{:S(2)}) async-start(bf16[8,16,1664]{2,1,0:T(8,128)(2,1)} %broadcast_in_dim.33), calls=%async_computation.7 | async-start | bytes 851968 | tf_op jit(solution)/shard_map/all_to_all | solution.py:433
  247.3 2.6 %pack.1 = bf16[768,512]{1,0:T(8,128)(2,1)} custom-call(s32[32]{0:T(128)S(1)} %select_reduce_fusion.2.lens_ref, bf16[1536,512]{1,0:T(8,128)(2,1)S(1)} %bitcast.14), custom_call_target="tpu_custom_call" | custom-call | tf_op jit(solution)/shard_map/pack/pallas_call | solution.py:330
  249.9 6.6 %all-to-all-done.7 = bf16[8,16,1664]{2,1,0:T(8,128)(2,1)S(1)} async-done(((bf16[8,16,1664]{2,1,0:T(8,128)(2,1)}), bf16[8,16,1664]{2,1,0:T(8,128)(2,1)S(1)}, u32[]{:S(2)}, u32[]{:S(2)}) %all-to-all-start.7) | async-done | bytes 426016 | tf_op jit(solution)/shard_map/all_to_all | solution.py:433
  (71 shorter events, 24.3 us)
Async XLA Ops:
  5.1 1.4 copy-start
  6.5 1.2 copy-start.3
  21.5 1.4 copy-start.6
  22.9 1.2 copy-start.8
  24.0 1.2 copy-start.10
  42.9 14.7 %all-to-all-start.2 = ((f32[16,8,128]{2,1,0:T(8,128)}), f32[16,8,128]{2,1,0:T(8,128)S(1)}, u32[]{:S(2)}, u32[]{:S(2)}) async-start(f32[16,8,128]{2,1,0:T(8,128)} %relay.2), calls=%async_computation.2 | async-start | bytes 131072 | tf_op jit(solution)/shard_map/all_to_all | solution.py:433
  50.0 1.1 copy-start.12
  52.9 1.1 copy-start.2
  54.1 47.2 %copy-start.26 = (f32[512]{0:T(512)S(1)}, f32[512]{0:T(512)}, u32[]{:S(2)}) copy-start(f32[512]{0:T(512)} %param.23) | copy-start | bytes 6148
  54.1 47.2 %copy-start.29 = (f32[512]{0:T(512)S(1)}, f32[512]{0:T(512)}, u32[]{:S(2)}) copy-start(f32[512]{0:T(512)} %param.24) | copy-start | bytes 6148
  57.6 43.7 %copy-start.15 = (bf16[512,512]{1,0:T(8,128)(2,1)S(1)}, bf16[512,512]{1,0:T(8,128)(2,1)}, u32[]{:S(2)}) copy-start(bf16[512,512]{1,0:T(8,128)(2,1)} %wout_ref.1) | copy-start | bytes 1572868
  101.3 32.1 %copy-start.14 = (bf16[256,192]{1,0:T(8,128)(2,1)S(1)}, bf16[256,192]{1,0:T(8,128)(2,1)}, u32[]{:S(2)}) copy-start(bf16[256,192]{1,0:T(8,128)(2,1)} %constant.35.clone.qh_ref) | copy-start | bytes 294916
  101.3 32.1 %copy-start.19 = (bf16[192,256]{1,0:T(8,128)(2,1)S(1)}, bf16[192,256]{1,0:T(8,128)(2,1)}, u32[]{:S(2)}) copy-start(bf16[192,256]{1,0:T(8,128)(2,1)} %constant.37.clone.ih_ref) | copy-start | bytes 294916
  101.3 32.1 %copy-start.25 = (f32[72,128]{1,0:T(8,128)S(1)}, f32[72,128]{1,0:T(8,128)}, u32[]{:S(2)}) copy-start(f32[72,128]{1,0:T(8,128)} %constant.40.clone.back_ref) | copy-start | bytes 110596
  101.3 32.1 %copy-start.28 = (f32[512]{0:T(512)S(1)}, f32[512]{0:T(512)}, u32[]{:S(2)}) copy-start(f32[512]{0:T(512)} %param.20) | copy-start | bytes 6148
  106.8 1.7 copy-start.5
  133.4 1.4 copy-start.1
  134.8 1.2 copy-start.4
  136.0 1.6 copy-start.7
  137.6 1.4 copy-start.9
  139.0 1.4 copy-start.11
  141.4 12.1 %copy-start.17 = (bf16[512,512]{1,0:T(8,128)(2,1)S(1)}, bf16[512,512]{1,0:T(8,128)(2,1)}, u32[]{:S(2)}) copy-start(bf16[512,512]{1,0:T(8,128)(2,1)} %copy-done.16) | copy-start | bytes 1572868
  199.5 43.5 %all-to-all-start.3 = ((bf16[32,48,512]{2,1,0:T(8,128)(2,1)}), bf16[32,48,512]{2,1,0:T(8,128)(2,1)S(1)}, u32[]{:S(2)}, u32[]{:S(2)}) async-start(bf16[32,48,512]{2,1,0:T(8,128)(2,1)} %bitcast.7), calls=%async_computation.3 | async-start | bytes 3145728 | tf_op jit(solution)/shard_map/all_to_all | solution.py:433
  243.8 12.7 %all-to-all-start.7 = ((bf16[8,16,1664]{2,1,0:T(8,128)(2,1)}), bf16[8,16,1664]{2,1,0:T(8,128)(2,1)S(1)}, u32[]{:S(2)}, u32[]{:S(2)}) async-start(bf16[8,16,1664]{2,1,0:T(8,128)(2,1)} %broadcast_in_dim.33), calls=%async_computation.7 | async-start | bytes 851968 | tf_op jit(solution)/shard_map/all_to_all | solution.py:433
  (9 other events, 7.5 us)

commit v2 on v1

--- a/solution.py
+++ b/solution.py
@@ -13,8 +13,7 @@
 BUCKET = ("x", "z")
 DP = ("y", "c")
 EVERY = ("y", "c", "x", "z")
-FIRST = ("c", "z")
-SECOND = ("y", "x")
+
 
 EPSILON = 1e-05
 SPAN = 48
@@ -22,7 +21,7 @@
 HALF = POINTS // 2
 PER_DFT = 4
 PER_STEP = 8
-VMEM_LIMIT = 40 * 2**20
+VMEM_LIMIT = 60 * 2**20
 
 F32 = jnp.float32
 BF16 = jnp.bfloat16
@@ -186,15 +185,11 @@
     @pl.when(step == pl.num_programs(0) - 1)
     def _():
         sums = [jnp.sum(acc[k], axis=0, keepdims=True) for k in range(2)]
-        stats_ref[...] = jnp.broadcast_to(as_tile(*sums)[None], stats_ref.shape)
-
-
-def relay_kernel(got_ref, out_ref):
-    out_ref[...] = jnp.broadcast_to(jnp.sum(got_ref[...], axis=0)[None], out_ref.shape)
+        stats_ref[...] = as_tile(*sums)
 
 
 def bn_terms(stats, gain_ref, total):
-    first, second = from_tile(jnp.sum(stats, axis=0))
+    first, second = from_tile(stats)
     centre = first / total
     inverse = lax.rsqrt(second / total - centre * centre + EPSILON)
     return centre, inverse
@@ -228,7 +223,7 @@
     @pl.when(step == pl.num_programs(0) - 1)
     def _():
         sums = [jnp.sum(acc[k], axis=0, keepdims=True) for k in range(2)]
-        sums_ref[...] = jnp.broadcast_to(as_tile(*sums)[None], sums_ref.shape)
+        sums_ref[...] = as_tile(*sums)
         gwout_ref[...] = dot(sw_all[...], dy_all[...], ((0,), (0,))).astype(BF16)
 
 
@@ -245,7 +240,7 @@
 
     lens = step_lens(lens_ref)
     centre, inverse = bn_terms(stats_ref[...], None, total)
-    bias_total, gain_total = from_tile(jnp.sum(sums_ref[...], axis=0))
+    bias_total, gain_total = from_tile(sums_ref[...])
     bias_ref[...] = bias_total
     bn_out_ref[...] = gain_total
     normed_bn = (conv_ref[...] - centre) * inverse
@@ -306,6 +301,10 @@
     return pl.BlockSpec((shape[0] // steps, shape[1]), lambda i: (i, 0))
 
 
+def cost(flops, moved):
+    return pl.CostEstimate(flops=int(flops), bytes_accessed=int(moved), transcendentals=0)
+
+
 def params():
     return pltpu.CompilerParams(dimension_semantics=("arbitrary",), vmem_limit_bytes=VMEM_LIMIT)
 
@@ -323,6 +322,7 @@
         scratch_shapes=[pltpu.VMEM((upstream.shape[0] + 8, upstream.shape[1]), F32)],
         compiler_params=pltpu.CompilerParams(vmem_limit_bytes=VMEM_LIMIT),
         name="unpack",
+        cost_estimate=cost(1e9, 3 * rows * upstream.shape[1]),
     )(lens, upstream)
 
 
@@ -335,10 +335,11 @@
         scratch_shapes=[pltpu.VMEM((rows + 8, got.shape[1]), F32)],
         compiler_params=pltpu.CompilerParams(vmem_limit_bytes=VMEM_LIMIT),
         name="pack",
+        cost_estimate=cost(2e9, 6 * rows * got.shape[1]),
     )(lens, got)
 
 
-def forward(lens, slots, frames, gain, w_in, w_dw, tabs, copies):
+def forward(lens, slots, frames, gain, w_in, w_dw, tabs):
     high, low, high_t, low_t, taps_to, _ = tabs
     rows, d = frames.shape
     steps = rows // (SPAN * PER_STEP)
@@ -352,7 +353,7 @@
             sds(freq, BF16),
             sds((rows, d), F32),
             sds((3 * HALF, d), F32),
-            sds((copies, 8, 128), F32),
+            sds((8, 128), F32),
         ),
         in_specs=[SMEM, SMEM, whole(frames.shape), whole(gain.shape), whole(w_in.shape)]
         + [whole(v.shape) for v in (high, low, high_t, low_t, taps_to, w_dw)],
@@ -362,25 +363,16 @@
             rows_of(freq, steps),
             rows_of((rows, d), steps),
             whole((3 * HALF, d)),
-            whole((copies, 8, 128)),
+            whole((8, 128)),
         ),
         scratch_shapes=[pltpu.VMEM((2, 8, d), F32)],
         compiler_params=params(),
         name="forward",
+        cost_estimate=cost(10e9, 16 * rows * d),
     )(lens, slots, frames, gain, w_in, high, low, high_t, low_t, taps_to, w_dw)
 
 
-def relay(got, copies):
-    return pl.pallas_call(
-        relay_kernel,
-        out_shape=sds((copies, 8, 128), F32),
-        in_specs=[pl.BlockSpec(memory_space=pltpu.VMEM)],
-        out_specs=pl.BlockSpec(memory_space=pltpu.VMEM),
-        name="relay",
-    )(got)
-
-
-def middle(total, lens, conv, dy, stats, bn_gain, bn_bias, w_out, copies):
+def middle(total, lens, conv, dy, stats, bn_gain, bn_bias, w_out):
     rows, d = conv.shape
     steps = rows // (SPAN * PER_STEP)
     part = rows_of((rows, d), steps)
@@ -391,13 +383,14 @@
             sds((rows, d), BF16),
             sds((rows, d), F32),
             sds((d, d), BF16),
-            sds((copies, 8, 128), F32),
+            sds((8, 128), F32),
         ),
         in_specs=[SMEM, part, part] + [whole(v.shape) for v in (stats, bn_gain, bn_bias, w_out)],
-        out_specs=(part, part, whole((d, d)), whole((copies, 8, 128))),
+        out_specs=(part, part, whole((d, d)), whole((8, 128))),
         scratch_shapes=[pltpu.VMEM((2, 8, d), F32), pltpu.VMEM((rows, d), BF16), pltpu.VMEM((rows, d), BF16)],
         compiler_params=params(),
         name="middle",
+        cost_estimate=cost(5e9, 12 * rows * d),
     )(lens, conv, dy, stats, bn_gain, bn_bias, w_out)
 
 
@@ -426,6 +419,7 @@
         ],
         compiler_params=params(),
         name="backward",
+        cost_estimate=cost(12e9, 18 * rows * d),
     )(lens, slots, frames, lin, sig, freq, conv, gbn, wf, stats, sums, bn_gain, gain, w_in, high, high_t, back)
 
 
@@ -433,8 +427,23 @@
     return lax.all_to_all(value, axes, split_axis=0, concat_axis=0, tiled=True)
 
 
-def to_everyone(tiles):
-    return swapped(relay(swapped(tiles, FIRST), lax.axis_size(SECOND)), SECOND)
+def to_everyone(tile):
+    return functools.reduce(lax.psum, ("c", "y", "x", "z"), tile)
+
+
+def sum_of_rows(blocks, ahead):
+    pair = lax.axis_size("c")
+    core = lax.axis_index("c")
+    count, share, width = blocks.shape
+    halves = blocks.reshape(count, pair, share // pair, width)
+    theirs = lax.dynamic_index_in_dim(halves, 1 - core, 1, keepdims=False)
+    own = lax.dynamic_index_in_dim(halves, core, 1, keepdims=False)
+    got = lax.ppermute(theirs, "c", [(0, 1), (1, 0)])
+    both = (own.astype(F32) + got.astype(F32)).astype(BF16)
+    both, ahead = lax.optimization_barrier((both, ahead))
+    mine = jnp.sum(swapped(both, BUCKET).astype(F32), axis=0).astype(BF16)
+    every = swapped(jnp.broadcast_to(mine, (lax.axis_size(DP), *mine.shape)), DP).astype(F32)
+    return jnp.sum(every.reshape(-1, pair, share // pair, width), axis=0).reshape(share, width), ahead
 
 
 def local(frames, lengths, owners, upstream, ln_gain, w_in, w_dw, bn_gain, bn_bias, w_out):
@@ -458,11 +467,9 @@
 
     dy = unpack(got_lens, upstream, rows)
     dy = swapped(dy.reshape(loaders, SPAN, d), BUCKET).reshape(rows, d)
-    lin, sig, freq, conv, wf, stats = forward(
-        lens, slots, frames, gain, w_in, w_dw, tabs, lax.axis_size(FIRST)
-    )
+    lin, sig, freq, conv, wf, stats = forward(lens, slots, frames, gain, w_in, w_dw, tabs)
     stats = to_everyone(stats)
-    out, gbn, gwout, sums = middle(total, lens, conv, dy, stats, bn_gain, bn_bias, w_out, lax.axis_size(FIRST))
+    out, gbn, gwout, sums = middle(total, lens, conv, dy, stats, bn_gain, bn_bias, w_out)
     sums = to_everyone(sums)
     out = swapped(out.reshape(loaders, SPAN, d), BUCKET).reshape(rows, d)
     gframes, gwin, small, bias_total, gain_total = backward(
@@ -470,10 +477,7 @@
     )
     share = d // loaders
     grads = jnp.concatenate([gwin, gwout, small], axis=1)
-    grads = swapped(grads.reshape(loaders, share, -1), BUCKET)
-    grads = jnp.sum(grads.astype(F32), axis=0).astype(BF16)
-    grads = swapped(jnp.broadcast_to(grads, (lax.axis_size(DP), *grads.shape)), DP)
-    grads = jnp.sum(grads.astype(F32), axis=0)
+    grads, out = sum_of_rows(grads.reshape(loaders, share, -1), out)
     out_frames = pack(got_lens, out, upstream.shape[0])
     return (
         out_frames,

time: 261 us -> 195 us (0.75)
  waiting for transfers between devices: 48.3 us -> 5.8 us
  local copies, waits for them, and re-layouts: 29.8 us -> 5.97 us
  blocking collectives: 128 us -> 114 us
  Pallas kernels: 33.6 us -> 40.9 us
  starting transfers between devices: 15.5 us -> 20.9 us
    all_to_all x5 -> x1, blocking collectives: 128 us -> 34.9 us  [swapped(): return lax.all_to_all(value, axes, split_axis=0, concat_axis=0, tiled=True)]
    psum x0 -> x8, blocking collectives: none -> 79.3 us  [to_everyone(): return functools.reduce(lax.psum, ('c', 'y', 'x', 'z'), tile)]
    all_to_all x3, waiting for transfers between devices: 48.3 us -> 3.43 us  [swapped(): return lax.all_to_all(value, axes, split_axis=0, concat_axis=0, tiled=True)]
    unnamed x62 -> x10, local copies, waits for them, and re-layouts: 26.3 us -> 2.52 us
    all_to_all x3, starting transfers between devices: 15.5 us -> 20.8 us  [swapped(): return lax.all_to_all(value, axes, split_axis=0, concat_axis=0, tiled=True)]
    pallas_call x1, Pallas kernels: 8.69 us -> 11.7 us  [forward(): pl.pallas_call(forward_kernel, grid=(steps,), out_shape=(sds((rows, d), B...]
    pallas_call x2 -> x0, Pallas kernels: 2.98 us -> none  [relay(): pl.pallas_call(relay_kernel, out_shape=sds((copies, 8, 128), F32), in_spe...]
  transfers between devices with their start and end apart: 3 -> 4, of which waited for: 3 -> 2; matrix products, arithmetic and copies ran while one was open for 0% -> 2% of each run, Pallas kernels for 2% -> 15%
where the time goes in v2:
time: 195 us; the launch traced here: 194 us
  blocking collectives  114 us (58%)
  Pallas kernels  40.9 us (21%)
  starting transfers between devices  20.9 us (11%)
  local copies, waits for them, and re-layouts  5.97 us (3%)
  other arithmetic  5.82 us (3%)
  waiting for transfers between devices  5.8 us (3%)
    psum x8, blocking collectives, to_everyone(): return functools.reduce(lax.psum, ('c', 'y', 'x', 'z'), tile)  79.3 us
    all_to_all x1, blocking collectives, swapped(): return lax.all_to_all(value, axes, split_axis=0, concat_axis=0, tiled=True)  34.9 us
    all_to_all x3, starting transfers between devices, swapped(): return lax.all_to_all(value, axes, split_axis=0, concat_axis=0, tiled=True)  20.8 us
    pallas_call x1, Pallas kernels, backward(): pl.pallas_call(functools.partial(backward_kernel, total), grid=(steps,),...  14.4 us
    pallas_call x1, Pallas kernels, forward(): pl.pallas_call(forward_kernel, grid=(steps,), out_shape=(sds((rows, d), B...  11.7 us
    pallas_call x1, Pallas kernels, middle(): pl.pallas_call(functools.partial(middle_kernel, total), grid=(steps,), ou...  7.74 us
  transfers between devices with their start and end apart: 4, of which 2 were waited for; matrix products, arithmetic and copies ran while one was open for 2% of the time, Pallas kernels for 15%

profile of v2, /device:TPU:32, one launch (start us, length us, event | category | flops | bytes accessed | tf_op | source)
XLA Modules:
  0.0 194.3 jit_solution(14510179001862643261)
XLA Ops:
  1.2 1.3 reduce.10
  2.6 1.3 reduce.9
  4.6 3.5 %unpack.1 = bf16[1536,512]{1,0:T(8,128)(2,1)} custom-call(s32[32]{0:T(128)} %select_reduce_fusion.2.lens_ref, bf16[768,512]{1,0:T(8,128)(2,1)} %upstream_ref.1), custom_call_target="tpu_custom_call" | custom-call | flops 1000000000 | bytes 2359296 | tf_op jit(solution)/shard_map/unpack/pallas_call | solution.py:317
  8.1 11.3 %all-to-all-start = ((bf16[32,48,512]{2,1,0:T(8,128)(2,1)}), bf16[32,48,512]{2,1,0:T(8,128)(2,1)S(1)}, u32[]{:S(2)}, u32[]{:S(2)}) async-start(bf16[32,48,512]{2,1,0:T(8,128)(2,1)} %bitcast.26), calls=%async_computation | async-start | bytes 3145728 | tf_op jit(solution)/shard_map/all_to_all | solution.py:427
  19.5 0.8 copy.26.wdw_ref
  21.0 11.7 %forward.1 = (bf16[1536,512]{1,0:T(8,128)(2,1)}, bf16[1536,512]{1,0:T(8,128)(2,1)}, bf16[2048,512]{1,0:T(8,128)(2,1)}, f32[1536,512]{1,0:T(8,128)}, f32[96,512]{1,0:T(8,128)}, /*index=5*/f32[8,128]{1,0:T(8,128)}) custom-call(s32[32]{0:T(128)} %get-tuple-element.43.lens_ref, s32[32]{0:T(128)} %get-tuple-element.42.slots_ref, bf16[1536,512]{1,0:T(8,128)(2,1)} %frames_ref.3, ...), custom_call_target="tpu_custom_call" | custom-call | flops 10000000000 | bytes 12582912 | tf_op jit(solution)/shard_map/forward/pallas_call | solution.py:347
  32.7 2.6 %psum.56 = f32[8,128]{1,0:T(8,128)S(1)} all-reduce(f32[8,128]{1,0:T(8,128)} %get-tuple-element.29), channel_id=1, replica_groups=mesh['y'=4,'c'=2,'x'=4,'z'=8] {'c'}, use_global_device_ids=true, to_apply=%region_3.4 | all-reduce | flops 1024 | bytes 8192 | tf_op jit(solution)/shard_map/psum | solution.py:431
  35.3 10.7 %psum.57 = f32[8,128]{1,0:T(8,128)S(1)} all-reduce(f32[8,128]{1,0:T(8,128)S(1)} %psum.56), channel_id=1, replica_groups=mesh['y'=4,'c'=2,'x'=4,'z'=8] {'y'}, use_global_device_ids=true, to_apply=%region_4.5 | all-reduce | flops 1024 | bytes 8192 | tf_op jit(solution)/shard_map/psum | solution.py:431
  46.0 10.5 %psum.58 = f32[8,128]{1,0:T(8,128)S(1)} all-reduce(f32[8,128]{1,0:T(8,128)S(1)} %psum.57), channel_id=1, replica_groups=mesh['y'=4,'c'=2,'x'=4,'z'=8] {'x'}, use_global_device_ids=true, to_apply=%region_5.6 | all-reduce | flops 1024 | bytes 8192 | tf_op jit(solution)/shard_map/psum | solution.py:431
  56.5 17.0 %psum.59.stats_ref = f32[8,128]{1,0:T(8,128)} all-reduce(f32[8,128]{1,0:T(8,128)S(1)} %psum.58), channel_id=1, replica_groups=mesh['y'=4,'c'=2,'x'=4,'z'=8] {'z'}, use_global_device_ids=true, to_apply=%region_6.7 | all-reduce | flops 1024 | bytes 8192 | tf_op jit(solution)/shard_map/psum | solution.py:431
  73.5 1.1 copy-done
  74.6 7.7 %middle.1 = (bf16[1536,512]{1,0:T(8,128)(2,1)}, f32[1536,512]{1,0:T(8,128)}, bf16[512,512]{1,0:T(8,128)(2,1)}, f32[8,128]{1,0:T(8,128)}) custom-call(s32[32]{0:T(128)} %get-tuple-element.43.lens_ref, f32[1536,512]{1,0:T(8,128)} %get-tuple-element.28.conv_ref, bf16[1536,512]{1,0:T(8,128)(2,1)} %bitcast.25, f32[8,128]{1,0:T(8,128)} %psum.59.stats_ref, ...), custom_call_target="tpu_custom_call" | custom-call | flops 5000000000 | bytes 9437184 | tf_op jit(solution)/shard_map/middle/pallas_call | solution.py:379
  82.4 6.1 %all-to-all-start.1 = ((bf16[32,48,512]{2,1,0:T(8,128)(2,1)}), bf16[32,48,512]{2,1,0:T(8,128)(2,1)}, u32[]{:S(2)}, u32[]{:S(2)}) async-start(bf16[32,48,512]{2,1,0:T(8,128)(2,1)} %bitcast.24), calls=%async_computation.1 | async-start | bytes 3145728 | tf_op jit(solution)/shard_map/all_to_all | solution.py:427
  88.5 2.5 %psum.60 = f32[8,128]{1,0:T(8,128)S(1)} all-reduce(f32[8,128]{1,0:T(8,128)S(1)} %copy-done.3), channel_id=1, replica_groups=mesh['y'=4,'c'=2,'x'=4,'z'=8] {'c'}, use_global_device_ids=true, to_apply=%region_7.8 | all-reduce | flops 1024 | bytes 8192 | tf_op jit(solution)/shard_map/psum | solution.py:431
  91.0 7.7 %psum.61 = f32[8,128]{1,0:T(8,128)S(1)} all-reduce(f32[8,128]{1,0:T(8,128)S(1)} %psum.60), channel_id=1, replica_groups=mesh['y'=4,'c'=2,'x'=4,'z'=8] {'y'}, use_global_device_ids=true, to_apply=%region_8.9 | all-reduce | flops 1024 | bytes 8192 | tf_op jit(solution)/shard_map/psum | solution.py:431
  98.7 10.5 %psum.62 = f32[8,128]{1,0:T(8,128)S(1)} all-reduce(f32[8,128]{1,0:T(8,128)S(1)} %psum.61), channel_id=1, replica_groups=mesh['y'=4,'c'=2,'x'=4,'z'=8] {'x'}, use_global_device_ids=true, to_apply=%region_9.10 | all-reduce | flops 1024 | bytes 8192 | tf_op jit(solution)/shard_map/psum | solution.py:431
  109.1 17.9 %psum.63.sums_ref = f32[8,128]{1,0:T(8,128)} all-reduce(f32[8,128]{1,0:T(8,128)S(1)} %psum.62), channel_id=1, replica_groups=mesh['y'=4,'c'=2,'x'=4,'z'=8] {'z'}, use_global_device_ids=true, to_apply=%region_10.11 | all-reduce | flops 1024 | bytes 8192 | tf_op jit(solution)/shard_map/psum | solution.py:431
  127.1 14.4 %backward.1 = (bf16[1536,512]{1,0:T(8,128)(2,1)}, bf16[512,1024]{1,0:T(8,128)(2,1)}, bf16[512,128]{1,0:T(8,128)(2,1)}, f32[1,512]{1,0:T(1,128)}, f32[1,512]{1,0:T(1,128)}) custom-call(s32[32]{0:T(128)} %get-tuple-element.43.lens_ref, s32[32]{0:T(128)} %get-tuple-element.42.slots_ref, bf16[1536,512]{1,0:T(8,128)(2,1)} %frames_ref.3, ...), custom_call_target="tpu_custom_call" | custom-call | flops 12000000000 | bytes 14155776 | tf_op jit(solution)/shard_map/backward/pallas_call | solution.py:402
  141.5 1.4 pad_maximum_fusion
  143.1 2.4 %collective-permute-done = bf16[32,8,1664]{2,1,0:T(8,128)(2,1)S(1)} collective-permute-done((bf16[32,8,1664]{2,1,0:T(8,128)(2,1)S(1)}, bf16[32,8,1664]{2,1,0:T(8,128)(2,1)S(1)}, u32[]{:S(2)}, u32[]{:S(2)}) %collective-permute-start) | collective-permute-done | bytes 852000 | tf_op jit(solution)/shard_map/ppermute | solution.py:441
  145.7 34.9 %all_to_all.20 = bf16[32,8,1664]{2,1,0:T(8,128)(2,1)S(1)} all-to-all(bf16[32,8,1664]{2,1,0:T(8,128)(2,1)S(1)} %fusion), channel_id=1, replica_groups=mesh['y'=4,'c'=2,'x'=4,'z'=8] {'x','z'}, dimensions={0} | all-to-all | bytes 1703936 | tf_op jit(solution)/shard_map/all_to_all | solution.py:427
  181.4 3.4 %all-to-all-start.3 = ((bf16[8,8,1664]{2,1,0:T(8,128)(2,1)}), bf16[8,8,1664]{2,1,0:T(8,128)(2,1)S(1)}, u32[]{:S(2)}, u32[]{:S(2)}) async-start(bf16[8,8,1664]{2,1,0:T(8,128)(2,1)} %broadcast_in_dim.33), calls=%async_computation.3 | async-start | bytes 425984 | tf_op jit(solution)/shard_map/all_to_all | solution.py:427
  184.8 3.5 %pack.1 = bf16[768,512]{1,0:T(8,128)(2,1)} custom-call(s32[32]{0:T(128)} %select_reduce_fusion.2.lens_ref, bf16[1536,512]{1,0:T(8,128)(2,1)} %bitcast.11.got_ref), custom_call_target="tpu_custom_call" | custom-call | flops 2000000000 | bytes 2359296 | tf_op jit(solution)/shard_map/pack/pallas_call | solution.py:330
  188.3 3.4 %all-to-all-done.3 = bf16[8,8,1664]{2,1,0:T(8,128)(2,1)S(1)} async-done(((bf16[8,8,1664]{2,1,0:T(8,128)(2,1)}), bf16[8,8,1664]{2,1,0:T(8,128)(2,1)S(1)}, u32[]{:S(2)}, u32[]{:S(2)}) %all-to-all-start.3) | async-done | bytes 213024 | tf_op jit(solution)/shard_map/all_to_all | solution.py:427
  (25 shorter events, 5.8 us)
Async XLA Ops:
  8.1 11.3 %copy-start.2 = (f32[512,31]{0,1:T(8,128)S(1)}, f32[512,31]{0,1:T(8,128)}, u32[]{:S(2)}) copy-start(f32[512,31]{0,1:T(8,128)} %param.22) | copy-start | bytes 190468
  8.1 65.4 %all-to-all-start = ((bf16[32,48,512]{2,1,0:T(8,128)(2,1)}), bf16[32,48,512]{2,1,0:T(8,128)(2,1)S(1)}, u32[]{:S(2)}, u32[]{:S(2)}) async-start(bf16[32,48,512]{2,1,0:T(8,128)(2,1)} %bitcast.26), calls=%async_computation | async-start | bytes 3145728 | tf_op jit(solution)/shard_map/all_to_all | solution.py:427
  73.5 1.1 copy-start
  82.4 6.1 %copy-start.3 = (f32[8,128]{1,0:T(8,128)S(1)}, f32[8,128]{1,0:T(8,128)}, u32[]{:S(2)}) copy-start(f32[8,128]{1,0:T(8,128)} %get-tuple-element.32) | copy-start | bytes 12292
  82.4 63.3 %all-to-all-start.1 = ((bf16[32,48,512]{2,1,0:T(8,128)(2,1)}), bf16[32,48,512]{2,1,0:T(8,128)(2,1)}, u32[]{:S(2)}, u32[]{:S(2)}) async-start(bf16[32,48,512]{2,1,0:T(8,128)(2,1)} %bitcast.24), calls=%async_computation.1 | async-start | bytes 3145728 | tf_op jit(solution)/shard_map/all_to_all | solution.py:427
  127.1 14.4 %copy-start.1 = (bf16[512,512]{1,0:T(8,128)(2,1)S(1)}, bf16[512,512]{1,0:T(8,128)(2,1)}, u32[]{:S(2)}) copy-start(bf16[512,512]{1,0:T(8,128)(2,1)} %get-tuple-element.34) | copy-start | bytes 1572868
  143.0 2.5 %collective-permute-start = (bf16[32,8,1664]{2,1,0:T(8,128)(2,1)S(1)}, bf16[32,8,1664]{2,1,0:T(8,128)(2,1)S(1)}, u32[]{:S(2)}, u32[]{:S(2)}) collective-permute-start(bf16[32,8,1664]{2,1,0:T(8,128)(2,1)S(1)} %dynamic-slice_bitcast_fusion), channel_id=1, source_target_pairs={{0,32},{32,0},{1,33},{33,1},{2,34},{34,2},{3,35},{35,3},{4,36},{36... | collective-permute-start | bytes 2555912 | tf_op jit(solution)/shard_map/ppermute | solution.py:441
  181.4 10.3 %all-to-all-start.3 = ((bf16[8,8,1664]{2,1,0:T(8,128)(2,1)}), bf16[8,8,1664]{2,1,0:T(8,128)(2,1)S(1)}, u32[]{:S(2)}, u32[]{:S(2)}) async-start(bf16[8,8,1664]{2,1,0:T(8,128)(2,1)} %broadcast_in_dim.33), calls=%async_computation.3 | async-start | bytes 425984 | tf_op jit(solution)/shard_map/all_to_all | solution.py:427

commit v3 on v2

v3 whole, which is shorter than its diff:
```python
import functools
import math

import jax
import jax.numpy as jnp
import numpy as np
from jax import lax
from jax.experimental import pallas as pl
from jax.experimental.pallas import tpu as pltpu
from jax.sharding import Mesh
from jax.sharding import PartitionSpec as P

BUCKET = ("x", "z")
DP = ("y", "c")
EVERY = ("y", "c", "x", "z")


EPSILON = 1e-05
SPAN = 48
POINTS = 64
HALF = POINTS // 2
PER_DFT = 4
PER_STEP = 8
VMEM_LIMIT = 60 * 2**20

F32 = jnp.float32
BF16 = jnp.bfloat16


def dot(a, b, dims=((1,), (0,)), precision=None):
    return lax.dot_general(a, b, (dims, ((), ())), preferred_element_type=F32, precision=precision)


def tables(taps):
    f = np.arange(HALF)[:, None]
    t = np.arange(SPAN)[None, :]
    angle = 2 * np.pi * f * t / POINTS
    real = np.cos(angle) * math.sqrt(2 / POINTS)
    imag = -np.sin(angle) * math.sqrt(2 / POINTS)
    real[0] = math.sqrt(1 / POINTS)
    imag[0] = math.sqrt(1 / POINTS) * (-1.0) ** np.arange(SPAN)
    block = np.zeros((2 * HALF * PER_DFT, SPAN * PER_DFT))
    for u in range(PER_DFT):
        block[u * HALF : (u + 1) * HALF, u * SPAN : (u + 1) * SPAN] = real
        block[(PER_DFT + u) * HALF : (PER_DFT + u + 1) * HALF, u * SPAN : (u + 1) * SPAN] = imag
    lag = np.arange(taps)[None, :] - taps // 2
    turn = 2 * np.pi * f * lag / POINTS
    cos, sin = np.cos(turn), np.sin(turn)
    cos_last = cos.copy()
    cos_last[0] = np.cos(np.pi * lag[0])
    taps_to = np.concatenate([cos, sin, cos_last], axis=0)
    back = np.zeros((2 * HALF, 128))
    back[:HALF, :taps] = cos
    back[HALF : 2 * HALF, :taps] = -sin
    back[HALF, :taps] = np.cos(np.pi * lag[0])
    high = block.astype(jnp.bfloat16)
    low = (block - high.astype(np.float64)).astype(jnp.bfloat16)
    return (
        high,
        low,
        np.ascontiguousarray(high.T),
        np.ascontiguousarray(low.T),
        taps_to.astype(np.float32),
        back.astype(np.float32),
    )


def masked(value, lens):
    t = lax.broadcasted_iota(jnp.int32, (SPAN, value.shape[1]), 0)
    return jnp.concatenate(
        [
            jnp.where(t < n, value[u * SPAN : (u + 1) * SPAN], jnp.zeros((), value.dtype))
            for u, n in enumerate(lens)
        ],
        axis=0,
    )


def folded(value):
    return jnp.sum(value.reshape(-1, 8, value.shape[1]), axis=0)


def as_tile(first, second):
    rows = [v[:, k * 128 : (k + 1) * 128] for v in (first, second) for k in range(4)]
    return jnp.concatenate(rows, axis=0)


def from_tile(tile):
    rows = [tile[k : k + 1] for k in range(8)]
    return (jnp.concatenate(rows[:4], axis=1), jnp.concatenate(rows[4:], axis=1))


def normalize(x, gain):
    centred = x - jnp.mean(x, axis=1, keepdims=True)
    inverse = lax.rsqrt(jnp.mean(centred * centred, axis=1, keepdims=True) + EPSILON)
    normed = centred * inverse
    return (normed * gain).astype(BF16), normed, inverse


def spread(wf, part):
    rows = wf[part * HALF : (part + 1) * HALF]
    return jnp.concatenate([rows] * PER_DFT, axis=0)


def unpack_kernel(lengths_ref, owners_ref, upstream_ref, out_ref, table_ref, wide, lens_all, dest_all, table, sem):
    loaders = lens_all.shape[0]
    me = lax.axis_index(BUCKET)
    for k in range(loaders):
        lens_all[k : k + 1, :] = lengths_ref[:, k * loaders : (k + 1) * loaders]
        dest_all[k : k + 1, :] = owners_ref[:, k * loaders : (k + 1) * loaders]
    got = jnp.sum(jnp.where(dest_all[...] == me, lens_all[...], 0), axis=1, keepdims=True)
    square = (loaders, loaders)
    hit = dest_all[pl.ds(me, 1), :] == lax.broadcasted_iota(jnp.int32, square, 0)
    lens = jnp.sum(jnp.where(hit, lens_all[pl.ds(me, 1), :], 0), axis=1, keepdims=True)
    slots = jnp.sum(jnp.where(hit, lax.broadcasted_iota(jnp.int32, square, 1), 0), axis=1, keepdims=True)
    column = lax.broadcasted_iota(jnp.int32, table_ref.shape, 1)
    table_ref[...] = jnp.where(column == 0, got, jnp.where(column == 1, lens, slots))
    copy = pltpu.make_async_copy(table_ref, table, sem)
    copy.start()
    rows = upstream_ref.shape[0]
    wide[:rows, :] = upstream_ref[...].astype(F32)
    wide[rows:, :] = jnp.zeros((8, wide.shape[1]), F32)
    copy.wait()

    def step(i, start):
        base = pl.multiple_of(start // 8 * 8, 8)
        window = pltpu.roll(wide[pl.ds(base, SPAN + 8), :], SPAN + 8 - start % 8, 0)
        out_ref[pl.ds(pl.multiple_of(i * SPAN, 16), SPAN), :] = window[:SPAN].astype(BF16)
        return start + table[i, 0]

    lax.fori_loop(0, loaders, step, jnp.int32(0))


def pack_kernel(table_ref, got_ref, out_ref, wide):
    count = got_ref.shape[0] // SPAN
    top = lax.broadcasted_iota(jnp.int32, (8, got_ref.shape[1]), 0)

    def step(i, start):
        base = pl.multiple_of(start // 8 * 8, 8)
        rows = got_ref[pl.ds(pl.multiple_of(i * SPAN, 16), SPAN), :].astype(F32)
        window = jnp.concatenate([rows, jnp.zeros((8, rows.shape[1]), F32)], axis=0)
        window = pltpu.roll(window, start % 8, 0)
        kept = jnp.where(top < start % 8, wide[pl.ds(base, 8), :], window[:8])
        wide[pl.ds(base, 8), :] = kept
        wide[pl.ds(base + 8, SPAN), :] = window[8:]
        return start + table_ref[i, 0]

    lax.fori_loop(0, count, step, jnp.int32(0))
    out_ref[...] = wide[: out_ref.shape[0], :].astype(BF16)


def step_lens(table_ref):
    return [table_ref[pl.program_id(0) * PER_STEP + u, 1] for u in range(PER_STEP)]


def slot_rows(table_ref, u):
    slot = table_ref[pl.program_id(0) * PER_STEP + u, 2]
    return pl.ds(pl.multiple_of(slot * SPAN, 16), SPAN)


def forward_kernel(
    table_ref, frames_ref, gain_ref, win_ref, qh_ref, ql_ref, ih_ref, il_ref, to_ref, wdw_ref,
    h_ref, lin_ref, sig_ref, freq_ref, conv_ref, wf_ref, stats_ref, acc,
):
    step = pl.program_id(0)

    @pl.when(step == 0)
    def _():
        wf_ref[...] = dot(to_ref[...], wdw_ref[...], ((1,), (1,)), lax.Precision.HIGHEST)
        acc[...] = jnp.zeros_like(acc)

    d = frames_ref.shape[1]
    lens = step_lens(table_ref)
    x = jnp.concatenate([frames_ref[slot_rows(table_ref, u), :] for u in range(PER_STEP)], axis=0)
    h, _, _ = normalize(x.astype(F32), gain_ref[...])
    h_ref[...] = h
    a = dot(h, win_ref[...])
    lin = a[:, :d]
    sig = jax.nn.sigmoid(a[:, d:])
    lin_ref[...] = lin.astype(BF16)
    sig_ref[...] = sig.astype(BF16)
    gated = masked(lin * sig, lens).astype(BF16)
    wa, wb, wl = (spread(wf_ref[...], k) for k in range(3))
    for b in range(PER_STEP // PER_DFT):
        rows = slice(b * SPAN * PER_DFT, (b + 1) * SPAN * PER_DFT)
        part = gated[rows]
        spec = dot(qh_ref[...], part) + dot(ql_ref[...], part)
        freq_ref[b * POINTS * PER_DFT : (b + 1) * POINTS * PER_DFT, :] = spec.astype(BF16)
        re, im = spec[: HALF * PER_DFT], spec[HALF * PER_DFT :]
        turned = jnp.concatenate([re * wa - im * wb, im * wl + re * wb], axis=0)
        high = turned.astype(BF16)
        low = (turned - high.astype(F32)).astype(BF16)
        conv = dot(ih_ref[...], high) + dot(il_ref[...], high) + dot(ih_ref[...], low)
        conv_ref[rows, :] = conv
        live = masked(conv, lens[b * PER_DFT : (b + 1) * PER_DFT])
        acc[0] += folded(live)
        acc[1] += folded(live * live)

    @pl.when(step == pl.num_programs(0) - 1)
    def _():
        sums = [jnp.sum(acc[k], axis=0, keepdims=True) for k in range(2)]
        stats_ref[...] = as_tile(*sums)


def split(value, theirs_ref, own_ref):
    blocks = value.reshape(-1, 2, 8, value.shape[1])
    first = lax.axis_index("c") == 0
    low, high = blocks[:, 0], blocks[:, 1]
    theirs_ref[...] = jnp.where(first, high, low).reshape(theirs_ref.shape).astype(BF16)
    own_ref[...] = jnp.where(first, low, high).reshape(own_ref.shape).astype(BF16)


def bn_terms(stats, total):
    first, second = from_tile(stats)
    centre = first / total
    inverse = lax.rsqrt(second / total - centre * centre + EPSILON)
    return centre, inverse


def middle_kernel(
    total, table_ref, conv_ref, dy_ref, stats_ref, gain_ref, bias_ref, wout_ref,
    out_ref, gbn_ref, theirs_ref, own_ref, sums_ref, moments_ref, acc, sw_all, dy_all,
):
    step = pl.program_id(0)

    @pl.when(step == 0)
    def _():
        acc[...] = jnp.zeros_like(acc)
        moments_ref[...] = jnp.sum(stats_ref[...], axis=0)

    centre, inverse = bn_terms(moments_ref[...], total)
    normed = (conv_ref[...] - centre) * inverse
    value = normed * gain_ref[...] + bias_ref[...]
    sig = jax.nn.sigmoid(value)
    swished = (value * sig).astype(BF16)
    out_ref[...] = dot(swished, wout_ref[...]).astype(BF16)
    dy = masked(dy_ref[...].astype(F32), step_lens(table_ref)).astype(BF16)
    rows = pl.ds(pl.multiple_of(step * PER_STEP * SPAN, 16), PER_STEP * SPAN)
    sw_all[rows, :] = swished
    dy_all[rows, :] = dy
    grad = dot(dy, wout_ref[...], ((1,), (1,))) * (sig * (1.0 + value * (1.0 - sig)))
    gbn_ref[...] = grad
    acc[0] += folded(grad)
    acc[1] += folded(grad * normed)

    @pl.when(step == pl.num_programs(0) - 1)
    def _():
        sums = [jnp.sum(acc[k], axis=0, keepdims=True) for k in range(2)]
        sums_ref[...] = as_tile(*sums)
        split(dot(sw_all[...], dy_all[...], ((0,), (0,))), theirs_ref, own_ref)


def backward_kernel(
    total, table_ref, h_ref, lin_ref, sig_ref, freq_ref, conv_ref, gbn_ref, wf_ref, stats_ref, sums_ref,
    bn_gain_ref, theirs_in, own_in, qh_ref, ih_ref, back_ref,
    grad_a_ref, theirs_ref, own_ref, bias_ref, bn_out_ref, acc, h_all, ga_all,
):
    step = pl.program_id(0)

    @pl.when(step == 0)
    def _():
        acc[...] = jnp.zeros_like(acc)

    lens = step_lens(table_ref)
    centre, inverse = bn_terms(stats_ref[...], total)
    bias_total, gain_total = from_tile(sums_ref[...])
    bias_ref[...] = bias_total
    bn_out_ref[...] = gain_total
    normed_bn = (conv_ref[...] - centre) * inverse
    scale = bn_gain_ref[...] * inverse
    grad_conv = scale * (gbn_ref[...] - bias_total / total - normed_bn * (gain_total / total))
    grad_conv = masked(grad_conv, lens).astype(BF16)
    wa, wb, wl = (spread(wf_ref[...], k) for k in range(3))
    n = HALF * PER_DFT
    edge = lax.broadcasted_iota(jnp.int32, (n, wa.shape[1]), 0) % HALF == 0
    parts = []
    for b in range(PER_STEP // PER_DFT):
        rows = slice(b * SPAN * PER_DFT, (b + 1) * SPAN * PER_DFT)
        spec = dot(qh_ref[...], grad_conv[rows])
        re, im = spec[:n], spec[n:]
        own = freq_ref[b * 2 * n : (b + 1) * 2 * n, :].astype(F32)
        own_re, own_im = own[:n], own[n:]
        both = im * own_im
        corr_re = re * own_re + jnp.where(edge, 0.0, both)
        corr_im = jnp.where(edge, both, re * own_im - im * own_re)
        acc[:HALF] += jnp.sum(corr_re.reshape(PER_DFT, HALF, -1), axis=0)
        acc[HALF:] += jnp.sum(corr_im.reshape(PER_DFT, HALF, -1), axis=0)
        turned = jnp.concatenate([re * wa + im * wb, im * wl - re * wb], axis=0).astype(BF16)
        parts.append(dot(ih_ref[...], turned))
    grad_gated = masked(jnp.concatenate(parts, axis=0), lens)
    lin = lin_ref[...].astype(F32)
    sig = sig_ref[...].astype(F32)
    first = grad_gated * sig
    grad_a = jnp.concatenate([first, first * lin * (1.0 - sig)], axis=1).astype(BF16)
    grad_a_ref[...] = grad_a
    rows = pl.ds(pl.multiple_of(step * PER_STEP * SPAN, 16), PER_STEP * SPAN)
    h_all[rows, :] = h_ref[...]
    ga_all[rows, :] = grad_a

    @pl.when(step == pl.num_programs(0) - 1)
    def _():
        d = h_all.shape[1]
        gwin, gwout, taps = slice(0, 2 * d), slice(2 * d, 3 * d), slice(3 * d, theirs_ref.shape[1])
        theirs_ref[:, gwout] = theirs_in[...]
        own_ref[:, gwout] = own_in[...]
        small = dot(acc[...], back_ref[...], ((0,), (0,)), lax.Precision.HIGHEST)
        split(small, theirs_ref.at[:, taps], own_ref.at[:, taps])
        split(dot(h_all[...], ga_all[...], ((0,), (0,))), theirs_ref.at[:, gwin], own_ref.at[:, gwin])


def inputs_kernel(table_ref, frames_ref, grad_a_ref, gain_ref, win_ref, gframes_ref):
    grad_h = dot(grad_a_ref[...], win_ref[...], ((1,), (1,)))
    x = jnp.concatenate([frames_ref[slot_rows(table_ref, u), :] for u in range(PER_STEP)], axis=0)
    gain = gain_ref[...]
    _, normed, inv = normalize(x.astype(F32), gain)
    scaled = grad_h * gain
    inner = jnp.mean(scaled * normed, axis=1, keepdims=True)
    grad_x = inv * (scaled - jnp.mean(scaled, axis=1, keepdims=True) - normed * inner)
    grad_x = masked(grad_x, step_lens(table_ref)).astype(BF16)
    for u in range(PER_STEP):
        gframes_ref[slot_rows(table_ref, u), :] = grad_x[u * SPAN : (u + 1) * SPAN]


def finish_kernel(every_ref, w_ref, gain_ref, gwin_ref, gwout_ref, gwdw_ref, gln_ref):
    count = every_ref.shape[0]
    halves = [sum(every_ref[k].astype(F32) for k in range(core, count, 2)) for core in range(2)]
    rows = jnp.concatenate(halves, axis=0)
    d = gwout_ref.shape[1]
    gwin = rows[:, : 2 * d]
    gwin_ref[...] = gwin
    gwout_ref[...] = rows[:, 2 * d : 3 * d]
    gwdw_ref[...] = rows[:, 3 * d : 3 * d + gwdw_ref.shape[1]]
    ones = jnp.ones((8, 2 * d), F32)
    dots = dot(ones, gwin * w_ref[...].astype(F32), ((1,), (1,)), lax.Precision.HIGHEST)
    gln_ref[...] = dots[:1] / gain_ref[...]


SMEM = pl.BlockSpec(memory_space=pltpu.SMEM)


def whole(shape):
    return pl.BlockSpec(shape, lambda i: (0,) * len(shape))


def rows_of(shape, steps):
    return pl.BlockSpec((shape[0] // steps, shape[1]), lambda i: (i, 0))


def cost(flops, moved):
    return pl.CostEstimate(flops=int(flops), bytes_accessed=int(moved), transcendentals=0)


def params():
    return pltpu.CompilerParams(dimension_semantics=("arbitrary",), vmem_limit_bytes=VMEM_LIMIT)


def sds(shape, dtype):
    return jax.ShapeDtypeStruct(shape, dtype)


def unpack(lengths, owners, upstream, loaders):
    rows, d = upstream.shape
    vmem = pl.BlockSpec(memory_space=pltpu.VMEM)
    return pl.pallas_call(
        unpack_kernel,
        out_shape=(sds((loaders * SPAN, d), BF16), sds((loaders, 128), jnp.int32)),
        in_specs=[vmem] * 3,
        out_specs=(vmem, vmem),
        scratch_shapes=[
            pltpu.VMEM((rows + 8, d), F32),
            pltpu.VMEM((loaders, loaders), jnp.int32),
            pltpu.VMEM((loaders, loaders), jnp.int32),
            pltpu.SMEM((loaders, 128), jnp.int32),
            pltpu.SemaphoreType.DMA,
        ],
        compiler_params=pltpu.CompilerParams(vmem_limit_bytes=VMEM_LIMIT),
        name="unpack",
        cost_estimate=cost(1e9, 6 * rows * d),
    )(lengths, owners, upstream)


def pack(table, got, rows):
    return pl.pallas_call(
        pack_kernel,
        out_shape=sds((rows, got.shape[1]), BF16),
        in_specs=[SMEM, pl.BlockSpec(memory_space=pltpu.VMEM)],
        out_specs=pl.BlockSpec(memory_space=pltpu.VMEM),
        scratch_shapes=[pltpu.VMEM((rows + 8, got.shape[1]), F32)],
        compiler_params=pltpu.CompilerParams(vmem_limit_bytes=VMEM_LIMIT),
        name="pack",
        cost_estimate=cost(2e9, 6 * rows * got.shape[1]),
    )(table, got)


def forward(table, frames, gain, w_in, w_dw, tabs):
    high, low, high_t, low_t, taps_to, _ = tabs
    rows, d = frames.shape
    steps = rows // (SPAN * PER_STEP)
    freq = (rows // SPAN * POINTS, d)
    return pl.pallas_call(
        forward_kernel,
        grid=(steps,),
        out_shape=(
            sds((rows, d), BF16),
            sds((rows, d), BF16),
            sds((rows, d), BF16),
            sds(freq, BF16),
            sds((rows, d), F32),
            sds((3 * HALF, d), F32),
            sds((8, 128), F32),
        ),
        in_specs=[SMEM, whole(frames.shape), whole(gain.shape), whole(w_in.shape)]
        + [whole(v.shape) for v in (high, low, high_t, low_t, taps_to, w_dw)],
        out_specs=(
            rows_of((rows, d), steps),
            rows_of((rows, d), steps),
            rows_of((rows, d), steps),
            rows_of(freq, steps),
            rows_of((rows, d), steps),
            whole((3 * HALF, d)),
            whole((8, 128)),
        ),
        scratch_shapes=[pltpu.VMEM((2, 8, d), F32)],
        compiler_params=params(),
        name="forward",
        cost_estimate=cost(10e9, 16 * rows * d),
    )(table, frames, gain, w_in, high, low, high_t, low_t, taps_to, w_dw)


def middle(total, table, conv, dy, stats, bn_gain, bn_bias, w_out):
    rows, d = conv.shape
    steps = rows // (SPAN * PER_STEP)
    part = rows_of((rows, d), steps)
    return pl.pallas_call(
        functools.partial(middle_kernel, total),
        grid=(steps,),
        out_shape=(
            sds((rows, d), BF16),
            sds((rows, d), F32),
            sds((d // 2, d), BF16),
            sds((d // 2, d), BF16),
            sds((8, 128), F32),
            sds((8, 128), F32),
        ),
        in_specs=[SMEM, part, part] + [whole(v.shape) for v in (stats, bn_gain, bn_bias, w_out)],
        out_specs=(part, part, whole((d // 2, d)), whole((d // 2, d)), whole((8, 128)), whole((8, 128))),
        scratch_shapes=[pltpu.VMEM((2, 8, d), F32), pltpu.VMEM((rows, d), BF16), pltpu.VMEM((rows, d), BF16)],
        compiler_params=params(),
        name="middle",
        cost_estimate=cost(5e9, 12 * rows * d),
    )(table, conv, dy, stats, bn_gain, bn_bias, w_out)


def backward(total, table, h, lin, sig, freq, conv, gbn, wf, stats, sums, bn_gain, theirs, own, tabs):
    high, _, high_t, _, _, back = tabs
    rows, d = h.shape
    width = 3 * d + back.shape[1]
    steps = rows // (SPAN * PER_STEP)
    part = rows_of((rows, d), steps)
    return pl.pallas_call(
        functools.partial(backward_kernel, total),
        grid=(steps,),
        out_shape=(
            sds((rows, 2 * d), BF16),
            sds((d // 2, width), BF16),
            sds((d // 2, width), BF16),
            sds((1, d), F32),
            sds((1, d), F32),
        ),
        in_specs=[SMEM, part, part, part, rows_of(freq.shape, steps), part, part]
        + [whole(v.shape) for v in (wf, stats, sums, bn_gain, theirs, own, high, high_t, back)],
        out_specs=(
            rows_of((rows, 2 * d), steps),
            whole((d // 2, width)),
            whole((d // 2, width)),
            whole((1, d)),
            whole((1, d)),
        ),
        scratch_shapes=[
            pltpu.VMEM((2 * HALF, d), F32),
            pltpu.VMEM((rows, d), BF16),
            pltpu.VMEM((rows, 2 * d), BF16),
        ],
        compiler_params=params(),
        name="backward",
        cost_estimate=cost(8e9, 18 * rows * d),
    )(table, h, lin, sig, freq, conv, gbn, wf, stats, sums, bn_gain, theirs, own, high, high_t, back)


def inputs_back(table, frames, grad_a, gain, w_in):
    rows, d = frames.shape
    steps = rows // (SPAN * PER_STEP)
    return pl.pallas_call(
        inputs_kernel,
        grid=(steps,),
        out_shape=sds((rows, d), BF16),
        in_specs=[SMEM, whole(frames.shape), rows_of(grad_a.shape, steps), whole(gain.shape), whole(w_in.shape)],
        out_specs=whole((rows, d)),
        compiler_params=params(),
        name="inputs_back",
        cost_estimate=cost(6e9, 12 * rows * d),
    )(table, frames, grad_a, gain, w_in)


def finish(every, w_rows, gain_rows, taps):
    share, width = w_rows.shape
    d = width // 2
    vmem = pl.BlockSpec(memory_space=pltpu.VMEM)
    return pl.pallas_call(
        finish_kernel,
        out_shape=(sds((share, width), F32), sds((share, d), F32), sds((share, taps), F32), sds((1, share), F32)),
        in_specs=[vmem] * 3,
        out_specs=(vmem,) * 4,
        compiler_params=pltpu.CompilerParams(vmem_limit_bytes=VMEM_LIMIT),
        name="finish",
    )(every, w_rows, gain_rows)


def swapped(value, axes):
    return lax.all_to_all(value, axes, split_axis=0, concat_axis=0, tiled=True)


def to_everyone(tile):
    return functools.reduce(lax.psum, ("c", "y", "x", "z"), tile)


def sum_of_rows(theirs, own, loaders, ahead):
    got = lax.ppermute(theirs, "c", [(0, 1), (1, 0)])
    both = (own.astype(F32) + got.astype(F32)).astype(BF16).reshape(loaders, -1, own.shape[1])
    both, ahead = lax.optimization_barrier((both, ahead))
    mine = jnp.sum(swapped(both, BUCKET).astype(F32), axis=0).astype(BF16)
    return swapped(jnp.broadcast_to(mine, (lax.axis_size(DP), *mine.shape)), DP), ahead


def local(frames, lengths, owners, upstream, ln_gain, w_in, w_dw, bn_gain, bn_bias, w_out):
    loaders = lax.axis_size(BUCKET)
    me = lax.axis_index(BUCKET)
    rows, d = frames.shape
    taps = w_dw.shape[1]
    share = d // loaders
    total = float(upstream.shape[0] * loaders * lax.axis_size(DP))
    tabs = tuple(jnp.asarray(v) for v in tables(taps))
    w_rows = lax.dynamic_slice_in_dim(w_in, me * share, share, 0)
    gain_rows = lax.dynamic_slice_in_dim(ln_gain, me * share, share, 0).reshape(1, share)
    gain, bn_gain, bn_bias = (v.reshape(1, d) for v in (ln_gain, bn_gain, bn_bias))

    dy, table = unpack(lengths, owners, upstream, loaders)
    dy = swapped(dy.reshape(loaders, SPAN, d), BUCKET).reshape(rows, d)
    h, lin, sig, freq, conv, wf, stats = forward(table, frames, gain, w_in, w_dw, tabs)
    stats = lax.psum(lax.psum(stats, "c"), "y")
    stats, dy = lax.optimization_barrier((stats, dy))
    stats = swapped(jnp.broadcast_to(stats, (loaders, *stats.shape)), BUCKET)
    out, gbn, theirs, own, sums, stats = middle(total, table, conv, dy, stats, bn_gain, bn_bias, w_out)
    sums = to_everyone(sums)
    out = swapped(out.reshape(loaders, SPAN, d), BUCKET).reshape(rows, d)
    grad_a, theirs, own, bias_total, gain_total = backward(
        total, table, h, lin, sig, freq, conv, gbn, wf, stats, sums, bn_gain, theirs, own, tabs
    )
    every, out = sum_of_rows(theirs, own, loaders, out)
    gframes = inputs_back(table, frames, grad_a, gain, w_in)
    out_frames = pack(table, out, upstream.shape[0])
    gwin, gwout, gwdw, gln = finish(every, w_rows, gain_rows, taps)
    return (
        out_frames,
        gframes,
        gwin,
        gwout,
        gwdw,
        gln.reshape(share),
        gain_total.reshape(d),
        bias_total.reshape(d),
    )


def solution(mesh):
    torus = Mesh(mesh.devices.reshape(4, 2, 4, 8), ("y", "c", "x", "z"))
    in_specs = (P(EVERY, None), P(DP, None), P(DP, None), P(EVERY, None)) + (P(),) * 6
    out_specs = (P(EVERY, None), P(EVERY, None), P(BUCKET, None), P(BUCKET, None), P(BUCKET, None), P(BUCKET), P(), P())
    return jax.shard_map(local, mesh=torus, in_specs=in_specs, out_specs=out_specs, check_vma=False)
```

time: 195 us -> 195 us (level)
  blocking collectives: 114 us -> 71.8 us
  waiting for transfers between devices: 5.8 us -> 34.5 us
  starting transfers between devices: 20.9 us -> 31.1 us
  Pallas kernels: 40.9 us -> 48.1 us
  other arithmetic: 5.82 us -> 2.45 us
    psum x8 -> x4, blocking collectives: 79.3 us -> 43.1 us  [to_everyone(): return functools.reduce(lax.psum, ('c', 'y', 'x', 'z'), tile)]
    all_to_all x3 -> x4, waiting for transfers between devices: 3.43 us -> 31.9 us  [swapped(): return lax.all_to_all(value, axes, split_axis=0, concat_axis=0, tiled=True)]
    all_to_all x1, blocking collectives: 34.9 us -> 15.5 us  [swapped(): return lax.all_to_all(value, axes, split_axis=0, concat_axis=0, tiled=True)]
    psum x0 -> x2, blocking collectives: none -> 13.3 us  [local(): stats = lax.psum(lax.psum(stats, 'c'), 'y')]
    all_to_all x3 -> x4, starting transfers between devices: 20.8 us -> 31 us  [swapped(): return lax.all_to_all(value, axes, split_axis=0, concat_axis=0, tiled=True)]
    pallas_call x1 -> x3, Pallas kernels: 3.5 us -> 13 us  [the longest x1 6.79 us: inputs_back(): pl.pallas_call(inputs_kernel, grid=(steps,), out_shape=sds((rows, d), BF1...]
    unnamed x2 -> x0, other arithmetic: 2.69 us -> none
    slice x4 -> x0, local copies, waits for them, and re-layouts: 2.54 us -> none  [the longest x1 0.69 us: local(): grads[:, 3 * d + taps]]
  transfers between devices with their start and end apart: 4 -> 5, of which waited for: 2 -> 4; matrix products, arithmetic and copies ran while one was open for 2% -> 3% of each run, Pallas kernels for 15% -> 18%
where the time goes in v3:
time: 195 us; the launch traced here: 194 us
  blocking collectives  71.8 us (37%)
  Pallas kernels  48.1 us (25%)
  waiting for transfers between devices  34.5 us (18%)
  starting transfers between devices  31.1 us (16%)
  local copies, waits for them, and re-layouts  4.93 us (3%)
  other arithmetic  2.45 us (1%)
    psum x4, blocking collectives, to_everyone(): return functools.reduce(lax.psum, ('c', 'y', 'x', 'z'), tile)  43.1 us
    all_to_all x4, waiting for transfers between devices, swapped(): return lax.all_to_all(value, axes, split_axis=0, concat_axis=0, tiled=True)  31.9 us
    all_to_all x4, starting transfers between devices, swapped(): return lax.all_to_all(value, axes, split_axis=0, concat_axis=0, tiled=True)  31 us
    all_to_all x1, blocking collectives, swapped(): return lax.all_to_all(value, axes, split_axis=0, concat_axis=0, tiled=True)  15.5 us
    psum x2, blocking collectives, local(): stats = lax.psum(lax.psum(stats, 'c'), 'y')  13.3 us
    pallas_call x1, Pallas kernels, backward(): pl.pallas_call(functools.partial(backward_kernel, total), grid=(steps,),...  12 us
    pallas_call x1, Pallas kernels, forward(): pl.pallas_call(forward_kernel, grid=(steps,), out_shape=(sds((rows, d), B...  11.8 us
    pallas_call x1, Pallas kernels, middle(): pl.pallas_call(functools.partial(middle_kernel, total), grid=(steps,), ou...  7.78 us
  transfers between devices with their start and end apart: 5, of which 4 were waited for; matrix products, arithmetic and copies ran while one was open for 3% of the time, Pallas kernels for 18%

profile of v3, /device:TPU:32, one launch (start us, length us, event | category | flops | bytes accessed | tf_op | source)
XLA Modules:
  0.0 193.6 jit_solution(15966924443299757284)
XLA Ops:
  0.6 4.5 %unpack.1 = (bf16[1536,512]{1,0:T(8,128)(2,1)}, s32[32,128]{1,0:T(8,128)}) custom-call(s32[1,1024]{1,0:T(1,128)} %lengths_ref.1, s32[1,1024]{1,0:T(1,128)} %owners_ref.1, bf16[768,512]{1,0:T(8,128)(2,1)} %upstream_ref.1), custom_call_target="tpu_custom_call" | custom-call | flops 1000000000 | bytes 2359296 | tf_op jit(solution)/shard_map/unpack/pallas_call | solution.py:364
  5.2 11.3 %all-to-all-start = ((bf16[32,48,512]{2,1,0:T(8,128)(2,1)}), bf16[32,48,512]{2,1,0:T(8,128)(2,1)S(1)}, u32[]{:S(2)}, u32[]{:S(2)}) async-start(bf16[32,48,512]{2,1,0:T(8,128)(2,1)} %bitcast.17), calls=%async_computation | async-start | bytes 3145728 | tf_op jit(solution)/shard_map/all_to_all | solution.py:520
  17.4 11.8 %forward.1 = (bf16[1536,512]{1,0:T(8,128)(2,1)}, bf16[1536,512]{1,0:T(8,128)(2,1)}, bf16[1536,512]{1,0:T(8,128)(2,1)}, bf16[2048,512]{1,0:T(8,128)(2,1)}, f32[15...) custom-call(s32[32,128]{1,0:T(8,128)} %get-tuple-element.36.table_ref, bf16[1536,512]{1,0:T(8,128)(2,1)} %frames_ref.3, ...), custom_call_target="tpu_custom_call" | custom-call | flops 10000000000 | bytes 12582912 | tf_op jit(solution)/shard_map/forward/pallas_call | solution.py:400
  29.2 2.6 %psum.42 = f32[8,128]{1,0:T(8,128)S(1)} all-reduce(f32[8,128]{1,0:T(8,128)} %get-tuple-element.42), channel_id=1, replica_groups=mesh['y'=4,'c'=2,'x'=4,'z'=8] {'c'}, use_global_device_ids=true, to_apply=%region_0.0 | all-reduce | flops 1024 | bytes 8192 | tf_op jit(solution)/shard_map/psum | solution.py:550
  31.8 10.7 %psum.43 = f32[8,128]{1,0:T(8,128)S(1)} all-reduce(f32[8,128]{1,0:T(8,128)S(1)} %psum.42), channel_id=1, replica_groups=mesh['y'=4,'c'=2,'x'=4,'z'=8] {'y'}, use_global_device_ids=true, to_apply=%region_1.0 | all-reduce | flops 1024 | bytes 8192 | tf_op jit(solution)/shard_map/psum | solution.py:550
  42.5 13.1 %all-to-all-done = bf16[32,48,512]{2,1,0:T(8,128)(2,1)S(1)} async-done(((bf16[32,48,512]{2,1,0:T(8,128)(2,1)}), bf16[32,48,512]{2,1,0:T(8,128)(2,1)S(1)}, u32[]{:S(2)}, u32[]{:S(2)}) %all-to-all-start) | async-done | bytes 1572896 | tf_op jit(solution)/shard_map/all_to_all | solution.py:520
  55.6 15.5 %all_to_all.25.stats_ref = f32[32,8,128]{2,1,0:T(8,128)} all-to-all(f32[32,8,128]{2,1,0:T(8,128)S(1)} %broadcast_in_dim.6), channel_id=1, replica_groups=mesh['y'=4,'c'=2,'x'=4,'z'=8] {'x','z'}, dimensions={0} | all-to-all | bytes 262144 | tf_op jit(solution)/shard_map/all_to_all | solution.py:520
  71.1 7.8 %middle.1 = (bf16[1536,512]{1,0:T(8,128)(2,1)}, f32[1536,512]{1,0:T(8,128)}, bf16[256,512]{1,0:T(8,128)(2,1)}, bf16[256,512]{1,0:T(8,128)(2,1)}, f32[8,128]{1,0:T(8,128)}, /*index=5*/f32[8,128]{1,0:T(8,128)}) custom-call(s32[32,128]{1,0:T(8,128)} %get-tuple-element.36.table_ref, f32[1536,512]{1,0:T(8,128)} %get-tuple-element.41.conv_ref, ...), custom_call_target="tpu_custom_call" | custom-call | flops 5000000000 | bytes 9437184 | tf_op jit(solution)/shard_map/middle/pallas_call | solution.py:434
  78.9 4.5 %all-to-all-start.2 = ((bf16[32,48,512]{2,1,0:T(8,128)(2,1)}), bf16[32,48,512]{2,1,0:T(8,128)(2,1)S(1)}, u32[]{:S(2)}, u32[]{:S(2)}) async-start(bf16[32,48,512]{2,1,0:T(8,128)(2,1)} %bitcast.15), calls=%async_computation.2 | async-start | bytes 3145728 | tf_op jit(solution)/shard_map/all_to_all | solution.py:520
  83.5 2.5 %psum.44 = f32[8,128]{1,0:T(8,128)S(1)} all-reduce(f32[8,128]{1,0:T(8,128)S(1)} %copy-done.4), channel_id=1, replica_groups=mesh['y'=4,'c'=2,'x'=4,'z'=8] {'c'}, use_global_device_ids=true, to_apply=%region_2.0 | all-reduce | flops 1024 | bytes 8192 | tf_op jit(solution)/shard_map/psum | solution.py:524
  86.0 10.7 %psum.45 = f32[8,128]{1,0:T(8,128)S(1)} all-reduce(f32[8,128]{1,0:T(8,128)S(1)} %psum.44), channel_id=1, replica_groups=mesh['y'=4,'c'=2,'x'=4,'z'=8] {'y'}, use_global_device_ids=true, to_apply=%region_3.0 | all-reduce | flops 1024 | bytes 8192 | tf_op jit(solution)/shard_map/psum | solution.py:524
  96.7 11.0 %psum.46 = f32[8,128]{1,0:T(8,128)S(1)} all-reduce(f32[8,128]{1,0:T(8,128)S(1)} %psum.45), channel_id=1, replica_groups=mesh['y'=4,'c'=2,'x'=4,'z'=8] {'x'}, use_global_device_ids=true, to_apply=%region_4.0 | all-reduce | flops 1024 | bytes 8192 | tf_op jit(solution)/shard_map/psum | solution.py:524
  107.6 18.9 %psum.47.sums_ref = f32[8,128]{1,0:T(8,128)} all-reduce(f32[8,128]{1,0:T(8,128)S(1)} %psum.46), channel_id=1, replica_groups=mesh['y'=4,'c'=2,'x'=4,'z'=8] {'z'}, use_global_device_ids=true, to_apply=%region_5.0 | all-reduce | flops 1024 | bytes 8192 | tf_op jit(solution)/shard_map/psum | solution.py:524
  126.5 12.0 %backward.1 = (bf16[1536,1024]{1,0:T(8,128)(2,1)}, bf16[256,1664]{1,0:T(8,128)(2,1)}, bf16[256,1664]{1,0:T(8,128)(2,1)}, f32[1,512]{1,0:T(1,128)}, f32[1,512]{1,0:T(1,128)}) custom-call(s32[32,128]{1,0:T(8,128)} %get-tuple-element.36.table_ref, bf16[1536,512]{1,0:T(8,128)(2,1)} %get-tuple-element.37.h_ref, bf16[1536,512]{1,0:T(8,128)(2,1)} %get-tuple-element.38.lin_ref, ...), custom_call_target="tpu_custom_call" | custom-call | flops 8000000000 | bytes 14155776 | tf_op jit(solution)/shard_map/backward/pallas_call | solution.py:460
  138.6 2.6 %collective-permute-done = bf16[256,1664]{1,0:T(8,128)(2,1)S(1)} collective-permute-done((bf16[256,1664]{1,0:T(8,128)(2,1)}, bf16[256,1664]{1,0:T(8,128)(2,1)S(1)}, u32[]{:S(2)}, u32[]{:S(2)}) %collective-permute-start) | collective-permute-done | bytes 852000 | tf_op jit(solution)/shard_map/ppermute | solution.py:528
  141.2 2.3 %fusion = bf16[32,8,1664]{2,1,0:T(8,128)(2,1)} fusion(bf16[256,1664]{1,0:T(8,128)(2,1)S(1)} %collective-permute-done, bf16[256,1664]{1,0:T(8,128)(2,1)} %get-tuple-element.52), kind=kLoop, calls=%fused_computation.1 | loop fusion | flops 1703936 | bytes 2555904 | tf_op jit(solution)/shard_map/reshape | solution.py:529
  143.5 10.7 %all-to-all-start.3 = ((bf16[32,8,1664]{2,1,0:T(8,128)(2,1)}), bf16[32,8,1664]{2,1,0:T(8,128)(2,1)S(1)}, u32[]{:S(2)}, u32[]{:S(2)}) async-start(bf16[32,8,1664]{2,1,0:T(8,128)(2,1)} %fusion), calls=%async_computation.3 | async-start | bytes 1703936 | tf_op jit(solution)/shard_map/all_to_all | solution.py:520
  155.5 1.4 constant_dynamic-slice_fusion.w_ref
  156.9 6.8 %inputs_back.1 = bf16[1536,512]{1,0:T(8,128)(2,1)} custom-call(s32[32,128]{1,0:T(8,128)} %get-tuple-element.36.table_ref, bf16[1536,512]{1,0:T(8,128)(2,1)} %frames_ref.3, bf16[1536,1024]{1,0:T(8,128)(2,1)} %get-tuple-element.56.grad_a_ref, f32[1,512]{1,0:T(1,128)} %bitcast.22, bf16[512,1024]{1,0:T(8,128)(2,1)} %win_ref.3), custom_call_target="tpu_custom_call" | custom-call | flops 6000000000 | bytes 9437184 | tf_op jit(solution)/shard_map/inputs_back/pallas_call | solution.py:493
  163.7 15.3 %all-to-all-done.3 = bf16[32,8,1664]{2,1,0:T(8,128)(2,1)S(1)} async-done(((bf16[32,8,1664]{2,1,0:T(8,128)(2,1)}), bf16[32,8,1664]{2,1,0:T(8,128)(2,1)S(1)}, u32[]{:S(2)}, u32[]{:S(2)}) %all-to-all-start.3) | async-done | bytes 852000 | tf_op jit(solution)/shard_map/all_to_all | solution.py:520
  179.8 4.5 %all-to-all-start.4 = ((bf16[8,8,1664]{2,1,0:T(8,128)(2,1)}), bf16[8,8,1664]{2,1,0:T(8,128)(2,1)S(1)}, u32[]{:S(2)}, u32[]{:S(2)}) async-start(bf16[8,8,1664]{2,1,0:T(8,128)(2,1)} %broadcast_in_dim.7), calls=%async_computation.4 | async-start | bytes 425984 | tf_op jit(solution)/shard_map/all_to_all | solution.py:520
  184.2 3.5 %pack.1 = bf16[768,512]{1,0:T(8,128)(2,1)} custom-call(s32[32,128]{1,0:T(8,128)} %get-tuple-element.36.table_ref, bf16[1536,512]{1,0:T(8,128)(2,1)} %bitcast.14), custom_call_target="tpu_custom_call" | custom-call | flops 2000000000 | bytes 2359296 | tf_op jit(solution)/shard_map/pack/pallas_call | solution.py:383
  187.7 3.5 %all-to-all-done.4.every_ref = bf16[8,8,1664]{2,1,0:T(8,128)(2,1)S(1)} async-done(((bf16[8,8,1664]{2,1,0:T(8,128)(2,1)}), bf16[8,8,1664]{2,1,0:T(8,128)(2,1)S(1)}, u32[]{:S(2)}, u32[]{:S(2)}) %all-to-all-start.4) | async-done | bytes 213024 | tf_op jit(solution)/shard_map/all_to_all | solution.py:520
  191.9 1.7 finish.1
  (17 shorter events, 3.8 us)
Async XLA Ops:
  5.2 11.4 %copy-start.3 = (f32[512,31]{0,1:T(8,128)S(1)}, f32[512,31]{0,1:T(8,128)}, u32[]{:S(2)}) copy-start(f32[512,31]{0,1:T(8,128)} %param.22) | copy-start | bytes 190468
  5.2 50.4 %all-to-all-start = ((bf16[32,48,512]{2,1,0:T(8,128)(2,1)}), bf16[32,48,512]{2,1,0:T(8,128)(2,1)S(1)}, u32[]{:S(2)}, u32[]{:S(2)}) async-start(bf16[32,48,512]{2,1,0:T(8,128)(2,1)} %bitcast.17), calls=%async_computation | async-start | bytes 3145728 | tf_op jit(solution)/shard_map/all_to_all | solution.py:520
  55.6 15.5 %copy-start.1 = (bf16[32,48,512]{2,1,0:T(8,128)(2,1)}, bf16[32,48,512]{2,1,0:T(8,128)(2,1)S(1)}, u32[]{:S(2)}) copy-start(bf16[32,48,512]{2,1,0:T(8,128)(2,1)S(1)} %all-to-all-done) | copy-start | bytes 4718596
  78.9 4.6 %copy-start.4 = (f32[8,128]{1,0:T(8,128)S(1)}, f32[8,128]{1,0:T(8,128)}, u32[]{:S(2)}) copy-start(f32[8,128]{1,0:T(8,128)} %get-tuple-element.49) | copy-start | bytes 12292
  78.9 64.6 %all-to-all-start.2 = ((bf16[32,48,512]{2,1,0:T(8,128)(2,1)}), bf16[32,48,512]{2,1,0:T(8,128)(2,1)S(1)}, u32[]{:S(2)}, u32[]{:S(2)}) async-start(bf16[32,48,512]{2,1,0:T(8,128)(2,1)} %bitcast.15), calls=%async_computation.2 | async-start | bytes 3145728 | tf_op jit(solution)/shard_map/all_to_all | solution.py:520
  138.5 2.7 %collective-permute-start = (bf16[256,1664]{1,0:T(8,128)(2,1)}, bf16[256,1664]{1,0:T(8,128)(2,1)S(1)}, u32[]{:S(2)}, u32[]{:S(2)}) collective-permute-start(bf16[256,1664]{1,0:T(8,128)(2,1)} %get-tuple-element.53), channel_id=1, source_target_pairs={{0,32},{32,0},{1,33},{33,1},{2,34},{34,2},{3,35},{35,3},{4,36},{36... | collective-permute-start | bytes 2555912 | tf_op jit(solution)/shard_map/ppermute | solution.py:528
  143.5 20.2 %copy-start = (bf16[32,48,512]{2,1,0:T(8,128)(2,1)}, bf16[32,48,512]{2,1,0:T(8,128)(2,1)S(1)}, u32[]{:S(2)}) copy-start(bf16[32,48,512]{2,1,0:T(8,128)(2,1)S(1)} %all-to-all-done.2) | copy-start | bytes 4718596
  143.5 35.4 %all-to-all-start.3 = ((bf16[32,8,1664]{2,1,0:T(8,128)(2,1)}), bf16[32,8,1664]{2,1,0:T(8,128)(2,1)S(1)}, u32[]{:S(2)}, u32[]{:S(2)}) async-start(bf16[32,8,1664]{2,1,0:T(8,128)(2,1)} %fusion), calls=%async_computation.3 | async-start | bytes 1703936 | tf_op jit(solution)/shard_map/all_to_all | solution.py:520
  179.8 11.5 %all-to-all-start.4 = ((bf16[8,8,1664]{2,1,0:T(8,128)(2,1)}), bf16[8,8,1664]{2,1,0:T(8,128)(2,1)S(1)}, u32[]{:S(2)}, u32[]{:S(2)}) async-start(bf16[8,8,1664]{2,1,0:T(8,128)(2,1)} %broadcast_in_dim.7), calls=%async_computation.4 | async-start | bytes 425984 | tf_op jit(solution)/shard_map/all_to_all | solution.py:520
  191.3 0.7 copy-start.2

commit v4 on v3

--- a/solution.py
+++ b/solution.py
@@ -17,6 +17,7 @@
 
 EPSILON = 1e-05
 SPAN = 48
+BLOCK = 64
 POINTS = 64
 HALF = POINTS // 2
 PER_DFT = 4
@@ -131,13 +132,14 @@
     lax.fori_loop(0, loaders, step, jnp.int32(0))
 
 
-def pack_kernel(table_ref, got_ref, out_ref, wide):
-    count = got_ref.shape[0] // SPAN
+def pack_kernel(table_ref, got_ref, out_ref, gwout_ref, wide):
+    count = got_ref.shape[0] // BLOCK
+    share = gwout_ref.shape[0]
     top = lax.broadcasted_iota(jnp.int32, (8, got_ref.shape[1]), 0)
 
     def step(i, start):
         base = pl.multiple_of(start // 8 * 8, 8)
-        rows = got_ref[pl.ds(pl.multiple_of(i * SPAN, 16), SPAN), :].astype(F32)
+        rows = got_ref[pl.ds(pl.multiple_of(i * BLOCK, 16), SPAN), :].astype(F32)
         window = jnp.concatenate([rows, jnp.zeros((8, rows.shape[1]), F32)], axis=0)
         window = pltpu.roll(window, start % 8, 0)
         kept = jnp.where(top < start % 8, wide[pl.ds(base, 8), :], window[:8])
@@ -147,6 +149,8 @@
 
     lax.fori_loop(0, count, step, jnp.int32(0))
     out_ref[...] = wide[: out_ref.shape[0], :].astype(BF16)
+    parts = [got_ref[k * BLOCK + SPAN : k * BLOCK + SPAN + share, :].astype(F32) for k in range(count)]
+    gwout_ref[...] = sum(parts).astype(BF16)
 
 
 def step_lens(table_ref):
@@ -219,7 +223,7 @@
 
 def middle_kernel(
     total, table_ref, conv_ref, dy_ref, stats_ref, gain_ref, bias_ref, wout_ref,
-    out_ref, gbn_ref, theirs_ref, own_ref, sums_ref, moments_ref, acc, sw_all, dy_all,
+    out_ref, gbn_ref, sums_ref, moments_ref, acc, sw_all, dy_all,
 ):
     step = pl.program_id(0)
 
@@ -233,7 +237,10 @@
     value = normed * gain_ref[...] + bias_ref[...]
     sig = jax.nn.sigmoid(value)
     swished = (value * sig).astype(BF16)
-    out_ref[...] = dot(swished, wout_ref[...]).astype(BF16)
+    out = dot(swished, wout_ref[...]).astype(BF16)
+    for u in range(PER_STEP):
+        slot = pl.multiple_of((step * PER_STEP + u) * BLOCK, BLOCK)
+        out_ref[pl.ds(slot, SPAN), :] = out[u * SPAN : (u + 1) * SPAN]
     dy = masked(dy_ref[...].astype(F32), step_lens(table_ref)).astype(BF16)
     rows = pl.ds(pl.multiple_of(step * PER_STEP * SPAN, 16), PER_STEP * SPAN)
     sw_all[rows, :] = swished
@@ -247,12 +254,16 @@
     def _():
         sums = [jnp.sum(acc[k], axis=0, keepdims=True) for k in range(2)]
         sums_ref[...] = as_tile(*sums)
-        split(dot(sw_all[...], dy_all[...], ((0,), (0,))), theirs_ref, own_ref)
+        gwout = dot(sw_all[...], dy_all[...], ((0,), (0,))).astype(BF16)
+        count = out_ref.shape[0] // BLOCK
+        share = gwout.shape[0] // count
+        for k in range(count):
+            out_ref[k * BLOCK + SPAN : k * BLOCK + SPAN + share, :] = gwout[k * share : (k + 1) * share]
 
 
 def backward_kernel(
     total, table_ref, h_ref, lin_ref, sig_ref, freq_ref, conv_ref, gbn_ref, wf_ref, stats_ref, sums_ref,
-    bn_gain_ref, theirs_in, own_in, qh_ref, ih_ref, back_ref,
+    bn_gain_ref, qh_ref, ih_ref, back_ref,
     grad_a_ref, theirs_ref, own_ref, bias_ref, bn_out_ref, acc, h_all, ga_all,
 ):
     step = pl.program_id(0)
@@ -300,9 +311,7 @@
     @pl.when(step == pl.num_programs(0) - 1)
     def _():
         d = h_all.shape[1]
-        gwin, gwout, taps = slice(0, 2 * d), slice(2 * d, 3 * d), slice(3 * d, theirs_ref.shape[1])
-        theirs_ref[:, gwout] = theirs_in[...]
-        own_ref[:, gwout] = own_in[...]
+        gwin, taps = slice(0, 2 * d), slice(2 * d, theirs_ref.shape[1])
         small = dot(acc[...], back_ref[...], ((0,), (0,)), lax.Precision.HIGHEST)
         split(small, theirs_ref.at[:, taps], own_ref.at[:, taps])
         split(dot(h_all[...], ga_all[...], ((0,), (0,))), theirs_ref.at[:, gwin], own_ref.at[:, gwin])
@@ -321,15 +330,27 @@
         gframes_ref[slot_rows(table_ref, u), :] = grad_x[u * SPAN : (u + 1) * SPAN]
 
 
+def collect_kernel(got_ref, gwout_ref, out_ref):
+    total = got_ref[0].astype(F32)
+    for k in range(1, got_ref.shape[0]):
+        total += got_ref[k].astype(F32)
+    high, low = gwout_ref[:8].astype(F32), gwout_ref[8:].astype(F32)
+    rows = jnp.concatenate([total, high, low], axis=1).astype(BF16)
+    for k in range(out_ref.shape[0]):
+        out_ref[k] = rows
+
+
 def finish_kernel(every_ref, w_ref, gain_ref, gwin_ref, gwout_ref, gwdw_ref, gln_ref):
     count = every_ref.shape[0]
-    halves = [sum(every_ref[k].astype(F32) for k in range(core, count, 2)) for core in range(2)]
+    d = gwout_ref.shape[1]
+    width = 2 * d + 128
+    halves = [sum(every_ref[k, :, :width].astype(F32) for k in range(core, count, 2)) for core in range(2)]
     rows = jnp.concatenate(halves, axis=0)
-    d = gwout_ref.shape[1]
     gwin = rows[:, : 2 * d]
     gwin_ref[...] = gwin
-    gwout_ref[...] = rows[:, 2 * d : 3 * d]
-    gwdw_ref[...] = rows[:, 3 * d : 3 * d + gwdw_ref.shape[1]]
+    gwdw_ref[...] = rows[:, 2 * d : 2 * d + gwdw_ref.shape[1]]
+    out = sum(every_ref[k, :, width:].astype(F32) for k in range(count))
+    gwout_ref[...] = jnp.concatenate([out[:, :d], out[:, d:]], axis=0)
     ones = jnp.ones((8, 2 * d), F32)
     dots = dot(ones, gwin * w_ref[...].astype(F32), ((1,), (1,)), lax.Precision.HIGHEST)
     gln_ref[...] = dots[:1] / gain_ref[...]
@@ -380,15 +401,18 @@
 
 
 def pack(table, got, rows):
+    d = got.shape[1]
+    share = d * BLOCK // got.shape[0]
+    vmem = pl.BlockSpec(memory_space=pltpu.VMEM)
     return pl.pallas_call(
         pack_kernel,
-        out_shape=sds((rows, got.shape[1]), BF16),
-        in_specs=[SMEM, pl.BlockSpec(memory_space=pltpu.VMEM)],
-        out_specs=pl.BlockSpec(memory_space=pltpu.VMEM),
-        scratch_shapes=[pltpu.VMEM((rows + 8, got.shape[1]), F32)],
+        out_shape=(sds((rows, d), BF16), sds((share, d), BF16)),
+        in_specs=[SMEM, vmem],
+        out_specs=(vmem, vmem),
+        scratch_shapes=[pltpu.VMEM((rows + 8, d), F32)],
         compiler_params=pltpu.CompilerParams(vmem_limit_bytes=VMEM_LIMIT),
         name="pack",
-        cost_estimate=cost(2e9, 6 * rows * got.shape[1]),
+        cost_estimate=cost(2e9, 6 * rows * d),
     )(table, got)
 
 
@@ -435,15 +459,13 @@
         functools.partial(middle_kernel, total),
         grid=(steps,),
         out_shape=(
-            sds((rows, d), BF16),
+            sds((rows // SPAN * BLOCK, d), BF16),
             sds((rows, d), F32),
-            sds((d // 2, d), BF16),
-            sds((d // 2, d), BF16),
             sds((8, 128), F32),
             sds((8, 128), F32),
         ),
         in_specs=[SMEM, part, part] + [whole(v.shape) for v in (stats, bn_gain, bn_bias, w_out)],
-        out_specs=(part, part, whole((d // 2, d)), whole((d // 2, d)), whole((8, 128)), whole((8, 128))),
+        out_specs=(whole((rows // SPAN * BLOCK, d)), part, whole((8, 128)), whole((8, 128))),
         scratch_shapes=[pltpu.VMEM((2, 8, d), F32), pltpu.VMEM((rows, d), BF16), pltpu.VMEM((rows, d), BF16)],
         compiler_params=params(),
         name="middle",
@@ -451,10 +473,10 @@
     )(table, conv, dy, stats, bn_gain, bn_bias, w_out)
 
 
-def backward(total, table, h, lin, sig, freq, conv, gbn, wf, stats, sums, bn_gain, theirs, own, tabs):
+def backward(total, table, h, lin, sig, freq, conv, gbn, wf, stats, sums, bn_gain, tabs):
     high, _, high_t, _, _, back = tabs
     rows, d = h.shape
-    width = 3 * d + back.shape[1]
+    width = 2 * d + back.shape[1]
     steps = rows // (SPAN * PER_STEP)
     part = rows_of((rows, d), steps)
     return pl.pallas_call(
@@ -468,7 +490,7 @@
             sds((1, d), F32),
         ),
         in_specs=[SMEM, part, part, part, rows_of(freq.shape, steps), part, part]
-        + [whole(v.shape) for v in (wf, stats, sums, bn_gain, theirs, own, high, high_t, back)],
+        + [whole(v.shape) for v in (wf, stats, sums, bn_gain, high, high_t, back)],
         out_specs=(
             rows_of((rows, 2 * d), steps),
             whole((d // 2, width)),
@@ -484,7 +506,7 @@
         compiler_params=params(),
         name="backward",
         cost_estimate=cost(8e9, 18 * rows * d),
-    )(table, h, lin, sig, freq, conv, gbn, wf, stats, sums, bn_gain, theirs, own, high, high_t, back)
+    )(table, h, lin, sig, freq, conv, gbn, wf, stats, sums, bn_gain, high, high_t, back)
 
 
 def inputs_back(table, frames, grad_a, gain, w_in):
@@ -502,6 +524,19 @@
     )(table, frames, grad_a, gain, w_in)
 
 
+def collect(got, gwout, count):
+    _, share, width = got.shape
+    vmem = pl.BlockSpec(memory_space=pltpu.VMEM)
+    return pl.pallas_call(
+        collect_kernel,
+        out_shape=sds((count, share, width + 2 * gwout.shape[1]), BF16),
+        in_specs=[vmem] * 2,
+        out_specs=vmem,
+        compiler_params=pltpu.CompilerParams(vmem_limit_bytes=VMEM_LIMIT),
+        name="collect",
+    )(got, gwout)
+
+
 def finish(every, w_rows, gain_rows, taps):
     share, width = w_rows.shape
     d = width // 2
@@ -524,12 +559,11 @@
     return functools.reduce(lax.psum, ("c", "y", "x", "z"), tile)
 
 
-def sum_of_rows(theirs, own, loaders, ahead):
+def over_bucket(theirs, own, loaders, ahead):
     got = lax.ppermute(theirs, "c", [(0, 1), (1, 0)])
     both = (own.astype(F32) + got.astype(F32)).astype(BF16).reshape(loaders, -1, own.shape[1])
     both, ahead = lax.optimization_barrier((both, ahead))
-    mine = jnp.sum(swapped(both, BUCKET).astype(F32), axis=0).astype(BF16)
-    return swapped(jnp.broadcast_to(mine, (lax.axis_size(DP), *mine.shape)), DP), ahead
+    return swapped(both, BUCKET), ahead
 
 
 def local(frames, lengths, owners, upstream, ln_gain, w_in, w_dw, bn_gain, bn_bias, w_out):
@@ -547,18 +581,20 @@
     dy, table = unpack(lengths, owners, upstream, loaders)
     dy = swapped(dy.reshape(loaders, SPAN, d), BUCKET).reshape(rows, d)
     h, lin, sig, freq, conv, wf, stats = forward(table, frames, gain, w_in, w_dw, tabs)
-    stats = lax.psum(lax.psum(stats, "c"), "y")
+    stats = lax.psum(lax.psum(lax.psum(stats, "c"), "y"), "x")
     stats, dy = lax.optimization_barrier((stats, dy))
-    stats = swapped(jnp.broadcast_to(stats, (loaders, *stats.shape)), BUCKET)
-    out, gbn, theirs, own, sums, stats = middle(total, table, conv, dy, stats, bn_gain, bn_bias, w_out)
+    stats = swapped(jnp.broadcast_to(stats, (lax.axis_size("z"), *stats.shape)), "z")
+    out, gbn, sums, stats = middle(total, table, conv, dy, stats, bn_gain, bn_bias, w_out)
     sums = to_everyone(sums)
-    out = swapped(out.reshape(loaders, SPAN, d), BUCKET).reshape(rows, d)
+    out = swapped(out.reshape(loaders, BLOCK, d), BUCKET).reshape(loaders * BLOCK, d)
     grad_a, theirs, own, bias_total, gain_total = backward(
-        total, table, h, lin, sig, freq, conv, gbn, wf, stats, sums, bn_gain, theirs, own, tabs
+        total, table, h, lin, sig, freq, conv, gbn, wf, stats, sums, bn_gain, tabs
     )
-    every, out = sum_of_rows(theirs, own, loaders, out)
+    got, out = over_bucket(theirs, own, loaders, out)
     gframes = inputs_back(table, frames, grad_a, gain, w_in)
-    out_frames = pack(table, out, upstream.shape[0])
+    out_frames, gwout = pack(table, out, upstream.shape[0])
+    gwout, gframes = lax.optimization_barrier((gwout, gframes))
+    every = swapped(collect(got, gwout, lax.axis_size(DP)), DP)
     gwin, gwout, gwdw, gln = finish(every, w_rows, gain_rows, taps)
     return (
         out_frames,

time: 195 us -> 198 us (1.015)
  blocking collectives: 71.8 us -> 88.6 us
  waiting for transfers between devices: 34.5 us -> 18.5 us
  Pallas kernels: 48.1 us -> 50.2 us
    all_to_all x4, waiting for transfers between devices: 31.9 us -> 16.3 us  [swapped(): return lax.all_to_all(value, axes, split_axis=0, concat_axis=0, tiled=True)]
    psum x4, blocking collectives: 43.1 us -> 53.6 us  [to_everyone(): return functools.reduce(lax.psum, ('c', 'y', 'x', 'z'), tile)]
    psum x2 -> x3, blocking collectives: 13.3 us -> 23.8 us  [local(): stats = lax.psum(lax.psum(lax.psum(stats, 'c'), 'y'), 'x')]
    all_to_all x1, blocking collectives: 15.5 us -> 11.2 us  [swapped(): return lax.all_to_all(value, axes, split_axis=0, concat_axis=0, tiled=True)]
    pallas_call x1 -> x2, Pallas kernels: 3.49 us -> 5.54 us  [the longest x1 3.67 us: pack(): pl.pallas_call(pack_kernel, out_shape=(sds((rows, d), BF16), sds((share,...]
  transfers between devices with their start and end apart: 5 -> 5, of which waited for: 4 -> 4; matrix products, arithmetic and copies ran while one was open for 3% -> 3% of each run, Pallas kernels for 18% -> 17%
where the time goes in v4:
time: 198 us; the launch traced here: 197 us
  blocking collectives  88.6 us (45%)
  Pallas kernels  50.2 us (25%)
  starting transfers between devices  31.6 us (16%)
  waiting for transfers between devices  18.5 us (9%)
  local copies, waits for them, and re-layouts  5.09 us (3%)
  other arithmetic  2.02 us (1%)
    psum x4, blocking collectives, to_everyone(): return functools.reduce(lax.psum, ('c', 'y', 'x', 'z'), tile)  53.6 us
    all_to_all x4, starting transfers between devices, swapped(): return lax.all_to_all(value, axes, split_axis=0, concat_axis=0, tiled=True)  31.5 us
    psum x3, blocking collectives, local(): stats = lax.psum(lax.psum(lax.psum(stats, 'c'), 'y'), 'x')  23.8 us
    all_to_all x4, waiting for transfers between devices, swapped(): return lax.all_to_all(value, axes, split_axis=0, concat_axis=0, tiled=True)  16.3 us
    pallas_call x1, Pallas kernels, forward(): pl.pallas_call(forward_kernel, grid=(steps,), out_shape=(sds((rows, d), B...  11.9 us
    pallas_call x1, Pallas kernels, backward(): pl.pallas_call(functools.partial(backward_kernel, total), grid=(steps,),...  11.6 us
    all_to_all x1, blocking collectives, swapped(): return lax.all_to_all(value, axes, split_axis=0, concat_axis=0, tiled=True)  11.2 us
    pallas_call x1, Pallas kernels, middle(): pl.pallas_call(functools.partial(middle_kernel, total), grid=(steps,), ou...  8.08 us
  transfers between devices with their start and end apart: 5, of which 4 were waited for; matrix products, arithmetic and copies ran while one was open for 3% of the time, Pallas kernels for 17%

profile of v4, /device:TPU:32, one launch (start us, length us, event | category | flops | bytes accessed | tf_op | source)
XLA Modules:
  0.0 196.8 jit_solution(14544443404784933421)
XLA Ops:
  0.6 4.5 %unpack.1 = (bf16[1536,512]{1,0:T(8,128)(2,1)}, s32[32,128]{1,0:T(8,128)}) custom-call(s32[1,1024]{1,0:T(1,128)} %lengths_ref.1, s32[1,1024]{1,0:T(1,128)} %owners_ref.1, bf16[768,512]{1,0:T(8,128)(2,1)} %upstream_ref.1), custom_call_target="tpu_custom_call" | custom-call | flops 1000000000 | bytes 2359296 | tf_op jit(solution)/shard_map/unpack/pallas_call | solution.py:385
  5.2 11.3 %all-to-all-start = ((bf16[32,48,512]{2,1,0:T(8,128)(2,1)}), bf16[32,48,512]{2,1,0:T(8,128)(2,1)S(1)}, u32[]{:S(2)}, u32[]{:S(2)}) async-start(bf16[32,48,512]{2,1,0:T(8,128)(2,1)} %bitcast.17), calls=%async_computation | async-start | bytes 3145728 | tf_op jit(solution)/shard_map/all_to_all | solution.py:555
  17.4 11.9 %forward.1 = (bf16[1536,512]{1,0:T(8,128)(2,1)}, bf16[1536,512]{1,0:T(8,128)(2,1)}, bf16[1536,512]{1,0:T(8,128)(2,1)}, bf16[2048,512]{1,0:T(8,128)(2,1)}, f32[15...) custom-call(s32[32,128]{1,0:T(8,128)} %get-tuple-element.38.table_ref, bf16[1536,512]{1,0:T(8,128)(2,1)} %frames_ref.3, ...), custom_call_target="tpu_custom_call" | custom-call | flops 10000000000 | bytes 12582912 | tf_op jit(solution)/shard_map/forward/pallas_call | solution.py:424
  29.3 2.6 %psum.49 = f32[8,128]{1,0:T(8,128)S(1)} all-reduce(f32[8,128]{1,0:T(8,128)} %get-tuple-element.44), channel_id=1, replica_groups=mesh['y'=4,'c'=2,'x'=4,'z'=8] {'c'}, use_global_device_ids=true, to_apply=%region_0.0 | all-reduce | flops 1024 | bytes 8192 | tf_op jit(solution)/shard_map/psum | solution.py:584
  31.9 10.7 %psum.50 = f32[8,128]{1,0:T(8,128)S(1)} all-reduce(f32[8,128]{1,0:T(8,128)S(1)} %psum.49), channel_id=1, replica_groups=mesh['y'=4,'c'=2,'x'=4,'z'=8] {'y'}, use_global_device_ids=true, to_apply=%region_1.0 | all-reduce | flops 1024 | bytes 8192 | tf_op jit(solution)/shard_map/psum | solution.py:584
  42.6 10.5 %psum.51 = f32[8,128]{1,0:T(8,128)S(1)} all-reduce(f32[8,128]{1,0:T(8,128)S(1)} %psum.50), channel_id=1, replica_groups=mesh['y'=4,'c'=2,'x'=4,'z'=8] {'x'}, use_global_device_ids=true, to_apply=%region_2.0 | all-reduce | flops 1024 | bytes 8192 | tf_op jit(solution)/shard_map/psum | solution.py:584
  53.2 2.5 %all-to-all-done = bf16[32,48,512]{2,1,0:T(8,128)(2,1)S(1)} async-done(((bf16[32,48,512]{2,1,0:T(8,128)(2,1)}), bf16[32,48,512]{2,1,0:T(8,128)(2,1)S(1)}, u32[]{:S(2)}, u32[]{:S(2)}) %all-to-all-start) | async-done | bytes 1572896 | tf_op jit(solution)/shard_map/all_to_all | solution.py:555
  55.6 11.2 %all_to_all.25.stats_ref = f32[8,8,128]{2,1,0:T(8,128)} all-to-all(f32[8,8,128]{2,1,0:T(8,128)S(1)} %broadcast_in_dim.3), channel_id=1, replica_groups=mesh['y'=4,'c'=2,'x'=4,'z'=8] {'z'}, dimensions={0} | all-to-all | bytes 65536 | tf_op jit(solution)/shard_map/all_to_all | solution.py:555
  66.8 8.1 %middle.1 = (bf16[2048,512]{1,0:T(8,128)(2,1)}, f32[1536,512]{1,0:T(8,128)}, f32[8,128]{1,0:T(8,128)}, f32[8,128]{1,0:T(8,128)}) custom-call(s32[32,128]{1,0:T(8,128)} %get-tuple-element.38.table_ref, f32[1536,512]{1,0:T(8,128)} %get-tuple-element.43.conv_ref, bf16[1536,512]{1,0:T(8,128)(2,1)} %bitcast.16, f32[8,8,128]{2,1,0:T(8,128)} %all_to_all.25.stats_ref, ...), custom_call_target="tpu_custom_call" | custom-call | flops 5000000000 | bytes 9437184 | tf_op jit(solution)/shard_map/middle/pallas_call | solution.py:458
  74.9 5.3 %all-to-all-start.2 = ((bf16[32,64,512]{2,1,0:T(8,128)(2,1)}), bf16[32,64,512]{2,1,0:T(8,128)(2,1)S(1)}, u32[]{:S(2)}, u32[]{:S(2)}) async-start(bf16[32,64,512]{2,1,0:T(8,128)(2,1)} %bitcast.15), calls=%async_computation.2 | async-start | bytes 4194304 | tf_op jit(solution)/shard_map/all_to_all | solution.py:555
  80.2 2.5 %psum.52 = f32[8,128]{1,0:T(8,128)S(1)} all-reduce(f32[8,128]{1,0:T(8,128)S(1)} %copy-done.5), channel_id=1, replica_groups=mesh['y'=4,'c'=2,'x'=4,'z'=8] {'c'}, use_global_device_ids=true, to_apply=%region_3.0 | all-reduce | flops 1024 | bytes 8192 | tf_op jit(solution)/shard_map/psum | solution.py:559
  82.7 10.4 %psum.53 = f32[8,128]{1,0:T(8,128)S(1)} all-reduce(f32[8,128]{1,0:T(8,128)S(1)} %psum.52), channel_id=1, replica_groups=mesh['y'=4,'c'=2,'x'=4,'z'=8] {'y'}, use_global_device_ids=true, to_apply=%region_4.0 | all-reduce | flops 1024 | bytes 8192 | tf_op jit(solution)/shard_map/psum | solution.py:559
  93.1 10.7 %psum.54 = f32[8,128]{1,0:T(8,128)S(1)} all-reduce(f32[8,128]{1,0:T(8,128)S(1)} %psum.53), channel_id=1, replica_groups=mesh['y'=4,'c'=2,'x'=4,'z'=8] {'x'}, use_global_device_ids=true, to_apply=%region_5.0 | all-reduce | flops 1024 | bytes 8192 | tf_op jit(solution)/shard_map/psum | solution.py:559
  103.8 30.0 %psum.55.sums_ref = f32[8,128]{1,0:T(8,128)} all-reduce(f32[8,128]{1,0:T(8,128)S(1)} %psum.54), channel_id=1, replica_groups=mesh['y'=4,'c'=2,'x'=4,'z'=8] {'z'}, use_global_device_ids=true, to_apply=%region_6.0 | all-reduce | flops 1024 | bytes 8192 | tf_op jit(solution)/shard_map/psum | solution.py:559
  133.8 11.6 %backward.1 = (bf16[1536,1024]{1,0:T(8,128)(2,1)}, bf16[256,1152]{1,0:T(8,128)(2,1)}, bf16[256,1152]{1,0:T(8,128)(2,1)}, f32[1,512]{1,0:T(1,128)}, f32[1,512]{1,0:T(1,128)}) custom-call(s32[32,128]{1,0:T(8,128)} %get-tuple-element.38.table_ref, bf16[1536,512]{1,0:T(8,128)(2,1)} %get-tuple-element.39.h_ref, bf16[1536,512]{1,0:T(8,128)(2,1)} %get-tuple-element.40.lin_ref, ...), custom_call_target="tpu_custom_call" | custom-call | flops 8000000000 | bytes 14155776 | tf_op jit(solution)/shard_map/backward/pallas_call | solution.py:482
  145.5 2.2 %collective-permute-done = bf16[256,1152]{1,0:T(8,128)(2,1)S(1)} collective-permute-done((bf16[256,1152]{1,0:T(8,128)(2,1)}, bf16[256,1152]{1,0:T(8,128)(2,1)S(1)}, u32[]{:S(2)}, u32[]{:S(2)}) %collective-permute-start) | collective-permute-done | bytes 589856 | tf_op jit(solution)/shard_map/ppermute | solution.py:563
  147.7 2.0 %fusion = bf16[32,8,1152]{2,1,0:T(8,128)(2,1)} fusion(bf16[256,1152]{1,0:T(8,128)(2,1)S(1)} %collective-permute-done, bf16[256,1152]{1,0:T(8,128)(2,1)} %get-tuple-element.52), kind=kLoop, calls=%fused_computation.1 | loop fusion | flops 1179648 | bytes 1769472 | tf_op jit(solution)/shard_map/reshape | solution.py:564
  149.8 10.5 %all-to-all-start.3 = ((bf16[32,8,1152]{2,1,0:T(8,128)(2,1)}), bf16[32,8,1152]{2,1,0:T(8,128)(2,1)S(1)}, u32[]{:S(2)}, u32[]{:S(2)}) async-start(bf16[32,8,1152]{2,1,0:T(8,128)(2,1)} %fusion), calls=%async_computation.3 | async-start | bytes 1179648 | tf_op jit(solution)/shard_map/all_to_all | solution.py:555
  160.2 6.8 %inputs_back.1 = bf16[1536,512]{1,0:T(8,128)(2,1)} custom-call(s32[32,128]{1,0:T(8,128)} %get-tuple-element.38.table_ref, bf16[1536,512]{1,0:T(8,128)(2,1)} %frames_ref.3, bf16[1536,1024]{1,0:T(8,128)(2,1)} %get-tuple-element.58.grad_a_ref, f32[1,512]{1,0:T(1,128)} %bitcast.22, bf16[512,1024]{1,0:T(8,128)(2,1)} %win_ref.3), custom_call_target="tpu_custom_call" | custom-call | flops 6000000000 | bytes 9437184 | tf_op jit(solution)/shard_map/inputs_back/pallas_call | solution.py:515
  167.1 3.7 %pack.1 = (bf16[768,512]{1,0:T(8,128)(2,1)}, bf16[16,512]{1,0:T(8,128)(2,1)}) custom-call(s32[32,128]{1,0:T(8,128)} %get-tuple-element.38.table_ref, bf16[2048,512]{1,0:T(8,128)(2,1)} %bitcast.14), custom_call_target="tpu_custom_call" | custom-call | flops 2000000000 | bytes 2359296 | tf_op jit(solution)/shard_map/pack/pallas_call | solution.py:407
  170.7 8.8 %all-to-all-done.3.got_ref = bf16[32,8,1152]{2,1,0:T(8,128)(2,1)S(1)} async-done(((bf16[32,8,1152]{2,1,0:T(8,128)(2,1)}), bf16[32,8,1152]{2,1,0:T(8,128)(2,1)S(1)}, u32[]{:S(2)}, u32[]{:S(2)}) %all-to-all-start.3) | async-done | bytes 589856 | tf_op jit(solution)/shard_map/all_to_all | solution.py:555
  180.3 1.9 collect.1
  182.2 4.5 %all-to-all-start.4 = ((bf16[8,8,2176]{2,1,0:T(8,128)(2,1)}), bf16[8,8,2176]{2,1,0:T(8,128)(2,1)S(1)}, u32[]{:S(2)}, u32[]{:S(2)}) async-start(bf16[8,8,2176]{2,1,0:T(8,128)(2,1)} %collect.1), calls=%async_computation.4 | async-start | bytes 557056 | tf_op jit(solution)/shard_map/all_to_all | solution.py:555
  189.4 5.0 %all-to-all-done.4.every_ref = bf16[8,8,2176]{2,1,0:T(8,128)(2,1)S(1)} async-done(((bf16[8,8,2176]{2,1,0:T(8,128)(2,1)}), bf16[8,8,2176]{2,1,0:T(8,128)(2,1)S(1)}, u32[]{:S(2)}, u32[]{:S(2)}) %all-to-all-start.4) | async-done | bytes 278560 | tf_op jit(solution)/shard_map/all_to_all | solution.py:555
  (19 shorter events, 6.9 us)
Async XLA Ops:
  5.2 11.4 %copy-start.4 = (f32[512,31]{0,1:T(8,128)S(1)}, f32[512,31]{0,1:T(8,128)}, u32[]{:S(2)}) copy-start(f32[512,31]{0,1:T(8,128)} %param.22) | copy-start | bytes 190468
  5.2 50.4 %all-to-all-start = ((bf16[32,48,512]{2,1,0:T(8,128)(2,1)}), bf16[32,48,512]{2,1,0:T(8,128)(2,1)S(1)}, u32[]{:S(2)}, u32[]{:S(2)}) async-start(bf16[32,48,512]{2,1,0:T(8,128)(2,1)} %bitcast.17), calls=%async_computation | async-start | bytes 3145728 | tf_op jit(solution)/shard_map/all_to_all | solution.py:555
  55.6 11.2 %copy-start.2 = (bf16[32,48,512]{2,1,0:T(8,128)(2,1)}, bf16[32,48,512]{2,1,0:T(8,128)(2,1)S(1)}, u32[]{:S(2)}) copy-start(bf16[32,48,512]{2,1,0:T(8,128)(2,1)S(1)} %all-to-all-done) | copy-start | bytes 4718596
  74.9 5.3 %copy-start.5 = (f32[8,128]{1,0:T(8,128)S(1)}, f32[8,128]{1,0:T(8,128)}, u32[]{:S(2)}) copy-start(f32[8,128]{1,0:T(8,128)} %get-tuple-element.51) | copy-start | bytes 12292
  74.9 74.8 %all-to-all-start.2 = ((bf16[32,64,512]{2,1,0:T(8,128)(2,1)}), bf16[32,64,512]{2,1,0:T(8,128)(2,1)S(1)}, u32[]{:S(2)}, u32[]{:S(2)}) async-start(bf16[32,64,512]{2,1,0:T(8,128)(2,1)} %bitcast.15), calls=%async_computation.2 | async-start | bytes 4194304 | tf_op jit(solution)/shard_map/all_to_all | solution.py:555
  145.4 2.3 %collective-permute-start = (bf16[256,1152]{1,0:T(8,128)(2,1)}, bf16[256,1152]{1,0:T(8,128)(2,1)S(1)}, u32[]{:S(2)}, u32[]{:S(2)}) collective-permute-start(bf16[256,1152]{1,0:T(8,128)(2,1)} %get-tuple-element.53), channel_id=1, source_target_pairs={{0,32},{32,0},{1,33},{33,1},{2,34},{34,2},{3,35},{35,3},{4,36},{36... | collective-permute-start | bytes 1769480 | tf_op jit(solution)/shard_map/ppermute | solution.py:563
  149.8 17.3 %copy-start.1 = (bf16[32,64,512]{2,1,0:T(8,128)(2,1)}, bf16[32,64,512]{2,1,0:T(8,128)(2,1)S(1)}, u32[]{:S(2)}) copy-start(bf16[32,64,512]{2,1,0:T(8,128)(2,1)S(1)} %all-to-all-done.2) | copy-start | bytes 6291460
  149.8 29.7 %all-to-all-start.3 = ((bf16[32,8,1152]{2,1,0:T(8,128)(2,1)}), bf16[32,8,1152]{2,1,0:T(8,128)(2,1)S(1)}, u32[]{:S(2)}, u32[]{:S(2)}) async-start(bf16[32,8,1152]{2,1,0:T(8,128)(2,1)} %fusion), calls=%async_computation.3 | async-start | bytes 1179648 | tf_op jit(solution)/shard_map/all_to_all | solution.py:555
  179.5 0.8 copy-start
  182.2 12.2 %all-to-all-start.4 = ((bf16[8,8,2176]{2,1,0:T(8,128)(2,1)}), bf16[8,8,2176]{2,1,0:T(8,128)(2,1)S(1)}, u32[]{:S(2)}, u32[]{:S(2)}) async-start(bf16[8,8,2176]{2,1,0:T(8,128)(2,1)} %collect.1), calls=%async_computation.4 | async-start | bytes 557056 | tf_op jit(solution)/shard_map/all_to_all | solution.py:555
  194.4 0.7 copy-start.3

commit v5 on v3

--- a/solution.py
+++ b/solution.py
@@ -22,6 +22,7 @@
 PER_DFT = 4
 PER_STEP = 8
 VMEM_LIMIT = 60 * 2**20
+SMALL_LIMIT = 16 * 2**20
 
 F32 = jnp.float32
 BF16 = jnp.bfloat16
@@ -219,7 +220,7 @@
 
 def middle_kernel(
     total, table_ref, conv_ref, dy_ref, stats_ref, gain_ref, bias_ref, wout_ref,
-    out_ref, gbn_ref, theirs_ref, own_ref, sums_ref, moments_ref, acc, sw_all, dy_all,
+    swished_ref, live_dy_ref, gbn_ref, sums_ref, moments_ref, acc,
 ):
     step = pl.program_id(0)
 
@@ -232,12 +233,9 @@
     normed = (conv_ref[...] - centre) * inverse
     value = normed * gain_ref[...] + bias_ref[...]
     sig = jax.nn.sigmoid(value)
-    swished = (value * sig).astype(BF16)
-    out_ref[...] = dot(swished, wout_ref[...]).astype(BF16)
+    swished_ref[...] = (value * sig).astype(BF16)
     dy = masked(dy_ref[...].astype(F32), step_lens(table_ref)).astype(BF16)
-    rows = pl.ds(pl.multiple_of(step * PER_STEP * SPAN, 16), PER_STEP * SPAN)
-    sw_all[rows, :] = swished
-    dy_all[rows, :] = dy
+    live_dy_ref[...] = dy
     grad = dot(dy, wout_ref[...], ((1,), (1,))) * (sig * (1.0 + value * (1.0 - sig)))
     gbn_ref[...] = grad
     acc[0] += folded(grad)
@@ -246,7 +244,18 @@
     @pl.when(step == pl.num_programs(0) - 1)
     def _():
         sums = [jnp.sum(acc[k], axis=0, keepdims=True) for k in range(2)]
-        sums_ref[...] = as_tile(*sums)
+        sums_ref[...] = jnp.broadcast_to(as_tile(*sums)[None], sums_ref.shape)
+
+
+def output_kernel(swished_ref, dy_ref, wout_ref, out_ref, theirs_ref, own_ref, sw_all, dy_all):
+    step = pl.program_id(0)
+    out_ref[...] = dot(swished_ref[...], wout_ref[...]).astype(BF16)
+    rows = pl.ds(pl.multiple_of(step * PER_STEP * SPAN, 16), PER_STEP * SPAN)
+    sw_all[rows, :] = swished_ref[...]
+    dy_all[rows, :] = dy_ref[...]
+
+    @pl.when(step == pl.num_programs(0) - 1)
+    def _():
         split(dot(sw_all[...], dy_all[...], ((0,), (0,))), theirs_ref, own_ref)
 
 
@@ -321,6 +330,14 @@
         gframes_ref[slot_rows(table_ref, u), :] = grad_x[u * SPAN : (u + 1) * SPAN]
 
 
+def collect_kernel(got_ref, out_ref):
+    total = got_ref[0].astype(F32)
+    for k in range(1, got_ref.shape[0]):
+        total += got_ref[k].astype(F32)
+    for k in range(out_ref.shape[0]):
+        out_ref[k] = total.astype(BF16)
+
+
 def finish_kernel(every_ref, w_ref, gain_ref, gwin_ref, gwout_ref, gwdw_ref, gln_ref):
     count = every_ref.shape[0]
     halves = [sum(every_ref[k].astype(F32) for k in range(core, count, 2)) for core in range(2)]
@@ -427,28 +444,46 @@
     )(table, frames, gain, w_in, high, low, high_t, low_t, taps_to, w_dw)
 
 
-def middle(total, table, conv, dy, stats, bn_gain, bn_bias, w_out):
+def middle(total, table, conv, dy, stats, bn_gain, bn_bias, w_out, copies):
     rows, d = conv.shape
     steps = rows // (SPAN * PER_STEP)
     part = rows_of((rows, d), steps)
+    tiles = (copies, 8, 128)
     return pl.pallas_call(
         functools.partial(middle_kernel, total),
         grid=(steps,),
         out_shape=(
             sds((rows, d), BF16),
+            sds((rows, d), BF16),
             sds((rows, d), F32),
-            sds((d // 2, d), BF16),
-            sds((d // 2, d), BF16),
-            sds((8, 128), F32),
+            sds(tiles, F32),
             sds((8, 128), F32),
         ),
         in_specs=[SMEM, part, part] + [whole(v.shape) for v in (stats, bn_gain, bn_bias, w_out)],
-        out_specs=(part, part, whole((d // 2, d)), whole((d // 2, d)), whole((8, 128)), whole((8, 128))),
-        scratch_shapes=[pltpu.VMEM((2, 8, d), F32), pltpu.VMEM((rows, d), BF16), pltpu.VMEM((rows, d), BF16)],
+        out_specs=(part, part, part, whole(tiles), whole((8, 128))),
+        scratch_shapes=[pltpu.VMEM((2, 8, d), F32)],
         compiler_params=params(),
         name="middle",
         cost_estimate=cost(5e9, 12 * rows * d),
     )(table, conv, dy, stats, bn_gain, bn_bias, w_out)
+
+
+def outputs(swished, dy, w_out):
+    rows, d = swished.shape
+    steps = rows // (SPAN * PER_STEP)
+    part = rows_of((rows, d), steps)
+    half = (d // 2, d)
+    return pl.pallas_call(
+        output_kernel,
+        grid=(steps,),
+        out_shape=(sds((rows, d), BF16), sds(half, BF16), sds(half, BF16)),
+        in_specs=[part, part, whole(w_out.shape)],
+        out_specs=(part, whole(half), whole(half)),
+        scratch_shapes=[pltpu.VMEM((rows, d), BF16), pltpu.VMEM((rows, d), BF16)],
+        compiler_params=params(),
+        name="outputs",
+        cost_estimate=cost(4e9, 6 * rows * d),
+    )(swished, dy, w_out)
 
 
 def backward(total, table, h, lin, sig, freq, conv, gbn, wf, stats, sums, bn_gain, theirs, own, tabs):
@@ -502,6 +537,18 @@
     )(table, frames, grad_a, gain, w_in)
 
 
+def collect(got, count):
+    vmem = pl.BlockSpec(memory_space=pltpu.VMEM)
+    return pl.pallas_call(
+        collect_kernel,
+        out_shape=sds((count, *got.shape[1:]), BF16),
+        in_specs=[vmem],
+        out_specs=vmem,
+        compiler_params=pltpu.CompilerParams(vmem_limit_bytes=SMALL_LIMIT),
+        name="collect",
+    )(got)
+
+
 def finish(every, w_rows, gain_rows, taps):
     share, width = w_rows.shape
     d = width // 2
@@ -511,7 +558,7 @@
         out_shape=(sds((share, width), F32), sds((share, d), F32), sds((share, taps), F32), sds((1, share), F32)),
         in_specs=[vmem] * 3,
         out_specs=(vmem,) * 4,
-        compiler_params=pltpu.CompilerParams(vmem_limit_bytes=VMEM_LIMIT),
+        compiler_params=pltpu.CompilerParams(vmem_limit_bytes=SMALL_LIMIT),
         name="finish",
     )(every, w_rows, gain_rows)
 
@@ -520,16 +567,11 @@
     return lax.all_to_all(value, axes, split_axis=0, concat_axis=0, tiled=True)
 
 
-def to_everyone(tile):
-    return functools.reduce(lax.psum, ("c", "y", "x", "z"), tile)
-
-
-def sum_of_rows(theirs, own, loaders, ahead):
+def over_bucket(theirs, own, loaders, ahead):
     got = lax.ppermute(theirs, "c", [(0, 1), (1, 0)])
     both = (own.astype(F32) + got.astype(F32)).astype(BF16).reshape(loaders, -1, own.shape[1])
     both, ahead = lax.optimization_barrier((both, ahead))
-    mine = jnp.sum(swapped(both, BUCKET).astype(F32), axis=0).astype(BF16)
-    return swapped(jnp.broadcast_to(mine, (lax.axis_size(DP), *mine.shape)), DP), ahead
+    return swapped(both, BUCKET), ahead
 
 
 def local(frames, lengths, owners, upstream, ln_gain, w_in, w_dw, bn_gain, bn_bias, w_out):
@@ -547,18 +589,25 @@
     dy, table = unpack(lengths, owners, upstream, loaders)
     dy = swapped(dy.reshape(loaders, SPAN, d), BUCKET).reshape(rows, d)
     h, lin, sig, freq, conv, wf, stats = forward(table, frames, gain, w_in, w_dw, tabs)
-    stats = lax.psum(lax.psum(stats, "c"), "y")
+    stats = lax.psum(lax.psum(lax.psum(stats, "c"), "y"), "x")
     stats, dy = lax.optimization_barrier((stats, dy))
-    stats = swapped(jnp.broadcast_to(stats, (loaders, *stats.shape)), BUCKET)
-    out, gbn, theirs, own, sums, stats = middle(total, table, conv, dy, stats, bn_gain, bn_bias, w_out)
-    sums = to_everyone(sums)
+    stats = swapped(jnp.broadcast_to(stats, (lax.axis_size("z"), *stats.shape)), "z")
+    swished, live_dy, gbn, sums, stats = middle(
+        total, table, conv, dy, stats, bn_gain, bn_bias, w_out, lax.axis_size("z")
+    )
+    sums = jnp.sum(swapped(sums, "z"), axis=0)
+    out, theirs, own = outputs(swished, live_dy, w_out)
+    out, sums = lax.optimization_barrier((out, sums))
     out = swapped(out.reshape(loaders, SPAN, d), BUCKET).reshape(rows, d)
+    sums = functools.reduce(lax.psum, ("c", "y", "x"), sums)
     grad_a, theirs, own, bias_total, gain_total = backward(
         total, table, h, lin, sig, freq, conv, gbn, wf, stats, sums, bn_gain, theirs, own, tabs
     )
-    every, out = sum_of_rows(theirs, own, loaders, out)
+    got, out = over_bucket(theirs, own, loaders, out)
     gframes = inputs_back(table, frames, grad_a, gain, w_in)
     out_frames = pack(table, out, upstream.shape[0])
+    got, gframes, out_frames = lax.optimization_barrier((got, gframes, out_frames))
+    every = swapped(collect(got, lax.axis_size(DP)), DP)
     gwin, gwout, gwdw, gln = finish(every, w_rows, gain_rows, taps)
     return (
         out_frames,

time: 195 us -> 179 us (0.918)
  blocking collectives: 71.8 us -> 59.6 us
  waiting for transfers between devices: 34.5 us -> 25.6 us
  Pallas kernels: 48.1 us -> 52.9 us
  starting transfers between devices: 31.1 us -> 34.7 us
  local copies, waits for them, and re-layouts: 4.93 us -> 2.39 us
    all_to_all x4 -> x5, waiting for transfers between devices: 31.9 us -> 23 us  [swapped(): return lax.all_to_all(value, axes, split_axis=0, concat_axis=0, tiled=True)]
    psum x6, blocking collectives: 56.4 us -> 48.5 us  [the longest x3 24.5 us: local(): sums = functools.reduce(lax.psum, ('c', 'y', 'x'), sums)]
    pallas_call x0 -> x2, Pallas kernels: none -> 6.75 us  [the longest x1 5.95 us: outputs(): pl.pallas_call(output_kernel, grid=(steps,), out_shape=(sds((rows, d), BF...]
    all_to_all x1, blocking collectives: 15.5 us -> 11.1 us  [swapped(): return lax.all_to_all(value, axes, split_axis=0, concat_axis=0, tiled=True)]
    all_to_all x4 -> x5, starting transfers between devices: 31 us -> 34.6 us  [swapped(): return lax.all_to_all(value, axes, split_axis=0, concat_axis=0, tiled=True)]
  transfers between devices with their start and end apart: 5 -> 6, of which waited for: 4 -> 5; matrix products, arithmetic and copies ran while one was open for 3% -> 3% of each run, Pallas kernels for 18% -> 22%
where the time goes in v5:
time: 179 us; the launch traced here: 178 us
  blocking collectives  59.6 us (33%)
  Pallas kernels  52.9 us (30%)
  starting transfers between devices  34.7 us (19%)
  waiting for transfers between devices  25.6 us (14%)
  local copies, waits for them, and re-layouts  2.39 us (1%)
  other arithmetic  2.32 us (1%)
    all_to_all x5, starting transfers between devices, swapped(): return lax.all_to_all(value, axes, split_axis=0, concat_axis=0, tiled=True)  34.6 us
    psum x3, blocking collectives, local(): sums = functools.reduce(lax.psum, ('c', 'y', 'x'), sums)  24.5 us
    psum x3, blocking collectives, local(): stats = lax.psum(lax.psum(lax.psum(stats, 'c'), 'y'), 'x')  23.9 us
    all_to_all x5, waiting for transfers between devices, swapped(): return lax.all_to_all(value, axes, split_axis=0, concat_axis=0, tiled=True)  23 us
    pallas_call x1, Pallas kernels, backward(): pl.pallas_call(functools.partial(backward_kernel, total), grid=(steps,),...  12 us
    pallas_call x1, Pallas kernels, forward(): pl.pallas_call(forward_kernel, grid=(steps,), out_shape=(sds((rows, d), B...  11.8 us
    all_to_all x1, blocking collectives, swapped(): return lax.all_to_all(value, axes, split_axis=0, concat_axis=0, tiled=True)  11.1 us
    pallas_call x1, Pallas kernels, middle(): pl.pallas_call(functools.partial(middle_kernel, total), grid=(steps,), ou...  6.85 us
  transfers between devices with their start and end apart: 6, of which 5 were waited for; matrix products, arithmetic and copies ran while one was open for 3% of the time, Pallas kernels for 22%

profile of v5, /device:TPU:32, one launch (start us, length us, event | category | flops | bytes accessed | tf_op | source)
XLA Modules:
  0.0 178.2 jit_solution(15762876481821778510)
XLA Ops:
  0.6 4.5 %unpack.1 = (bf16[1536,512]{1,0:T(8,128)(2,1)}, s32[32,128]{1,0:T(8,128)}) custom-call(s32[1,1024]{1,0:T(1,128)} %lengths_ref.1, s32[1,1024]{1,0:T(1,128)} %owners_ref.1, bf16[768,512]{1,0:T(8,128)(2,1)} %upstream_ref.1), custom_call_target="tpu_custom_call" | custom-call | flops 1000000000 | bytes 2359296 | tf_op jit(solution)/shard_map/unpack/pallas_call | solution.py:381
  5.2 11.3 %all-to-all-start = ((bf16[32,48,512]{2,1,0:T(8,128)(2,1)}), bf16[32,48,512]{2,1,0:T(8,128)(2,1)S(1)}, u32[]{:S(2)}, u32[]{:S(2)}) async-start(bf16[32,48,512]{2,1,0:T(8,128)(2,1)} %bitcast.17), calls=%async_computation | async-start | bytes 3145728 | tf_op jit(solution)/shard_map/all_to_all | solution.py:567
  17.4 11.8 %forward.1 = (bf16[1536,512]{1,0:T(8,128)(2,1)}, bf16[1536,512]{1,0:T(8,128)(2,1)}, bf16[1536,512]{1,0:T(8,128)(2,1)}, bf16[2048,512]{1,0:T(8,128)(2,1)}, f32[15...) custom-call(s32[32,128]{1,0:T(8,128)} %get-tuple-element.43.table_ref, bf16[1536,512]{1,0:T(8,128)(2,1)} %frames_ref.3, ...), custom_call_target="tpu_custom_call" | custom-call | flops 10000000000 | bytes 12582912 | tf_op jit(solution)/shard_map/forward/pallas_call | solution.py:417
  29.2 2.6 %psum.42 = f32[8,128]{1,0:T(8,128)S(1)} all-reduce(f32[8,128]{1,0:T(8,128)} %get-tuple-element.49), channel_id=1, replica_groups=mesh['y'=4,'c'=2,'x'=4,'z'=8] {'c'}, use_global_device_ids=true, to_apply=%region_0.0 | all-reduce | flops 1024 | bytes 8192 | tf_op jit(solution)/shard_map/psum | solution.py:592
  31.8 10.7 %psum.43 = f32[8,128]{1,0:T(8,128)S(1)} all-reduce(f32[8,128]{1,0:T(8,128)S(1)} %psum.42), channel_id=1, replica_groups=mesh['y'=4,'c'=2,'x'=4,'z'=8] {'y'}, use_global_device_ids=true, to_apply=%region_1.0 | all-reduce | flops 1024 | bytes 8192 | tf_op jit(solution)/shard_map/psum | solution.py:592
  42.5 10.6 %psum.44 = f32[8,128]{1,0:T(8,128)S(1)} all-reduce(f32[8,128]{1,0:T(8,128)S(1)} %psum.43), channel_id=1, replica_groups=mesh['y'=4,'c'=2,'x'=4,'z'=8] {'x'}, use_global_device_ids=true, to_apply=%region_2.0 | all-reduce | flops 1024 | bytes 8192 | tf_op jit(solution)/shard_map/psum | solution.py:592
  53.1 2.5 %all-to-all-done = bf16[32,48,512]{2,1,0:T(8,128)(2,1)S(1)} async-done(((bf16[32,48,512]{2,1,0:T(8,128)(2,1)}), bf16[32,48,512]{2,1,0:T(8,128)(2,1)S(1)}, u32[]{:S(2)}, u32[]{:S(2)}) %all-to-all-start) | async-done | bytes 1572896 | tf_op jit(solution)/shard_map/all_to_all | solution.py:567
  55.6 11.1 %all_to_all.30.stats_ref = f32[8,8,128]{2,1,0:T(8,128)} all-to-all(f32[8,8,128]{2,1,0:T(8,128)S(1)} %broadcast_in_dim.3), channel_id=1, replica_groups=mesh['y'=4,'c'=2,'x'=4,'z'=8] {'z'}, dimensions={0} | all-to-all | bytes 65536 | tf_op jit(solution)/shard_map/all_to_all | solution.py:567
  66.8 6.9 %middle.1 = (bf16[1536,512]{1,0:T(8,128)(2,1)}, bf16[1536,512]{1,0:T(8,128)(2,1)}, f32[1536,512]{1,0:T(8,128)}, f32[8,8,128]{2,1,0:T(8,128)}, f32[8,128]{1,0:T(8,128)}) custom-call(s32[32,128]{1,0:T(8,128)} %get-tuple-element.43.table_ref, f32[1536,512]{1,0:T(8,128)} %get-tuple-element.48.conv_ref, bf16[1536,512]{1,0:T(8,128)(2,1)} %bitcast.16, ...), custom_call_target="tpu_custom_call" | custom-call | flops 5000000000 | bytes 9437184 | tf_op jit(solution)/shard_map/middle/pallas_call | solution.py:452
  73.6 4.7 %all-to-all-start.2 = ((f32[8,8,128]{2,1,0:T(8,128)}), f32[8,8,128]{2,1,0:T(8,128)S(1)}, u32[]{:S(2)}, u32[]{:S(2)}) async-start(f32[8,8,128]{2,1,0:T(8,128)} %get-tuple-element.59), calls=%async_computation.2 | async-start | bytes 65536 | tf_op jit(solution)/shard_map/all_to_all | solution.py:567
  78.3 6.0 %outputs.1 = (bf16[1536,512]{1,0:T(8,128)(2,1)}, bf16[256,512]{1,0:T(8,128)(2,1)}, bf16[256,512]{1,0:T(8,128)(2,1)}) custom-call(bf16[1536,512]{1,0:T(8,128)(2,1)} %get-tuple-element.56.swished_ref, bf16[1536,512]{1,0:T(8,128)(2,1)} %get-tuple-element.57.dy_ref, bf16[512,512]{1,0:T(8,128)(2,1)} %wout_ref.3), custom_call_target="tpu_custom_call" | custom-call | flops 4000000000 | bytes 4718592 | tf_op jit(solution)/shard_map/outputs/pallas_call | solution.py:476
  84.9 7.8 %all-to-all-start.3 = ((bf16[32,48,512]{2,1,0:T(8,128)(2,1)}), bf16[32,48,512]{2,1,0:T(8,128)(2,1)S(1)}, u32[]{:S(2)}, u32[]{:S(2)}) async-start(bf16[32,48,512]{2,1,0:T(8,128)(2,1)} %bitcast.15), calls=%async_computation.3 | async-start | bytes 3145728 | tf_op jit(solution)/shard_map/all_to_all | solution.py:567
  92.7 2.5 %psum.45 = f32[8,128]{1,0:T(8,128)S(1)} all-reduce(f32[8,128]{1,0:T(8,128)S(1)} %reduce_sum.9), channel_id=1, replica_groups=mesh['y'=4,'c'=2,'x'=4,'z'=8] {'c'}, use_global_device_ids=true, to_apply=%region_4.0 | all-reduce | flops 1024 | bytes 8192 | tf_op jit(solution)/shard_map/psum | solution.py:602
  95.2 10.7 %psum.46 = f32[8,128]{1,0:T(8,128)S(1)} all-reduce(f32[8,128]{1,0:T(8,128)S(1)} %psum.45), channel_id=1, replica_groups=mesh['y'=4,'c'=2,'x'=4,'z'=8] {'y'}, use_global_device_ids=true, to_apply=%region_5.0 | all-reduce | flops 1024 | bytes 8192 | tf_op jit(solution)/shard_map/psum | solution.py:602
  105.9 11.3 %psum.47.sums_ref = f32[8,128]{1,0:T(8,128)} all-reduce(f32[8,128]{1,0:T(8,128)S(1)} %psum.46), channel_id=1, replica_groups=mesh['y'=4,'c'=2,'x'=4,'z'=8] {'x'}, use_global_device_ids=true, to_apply=%region_6.0 | all-reduce | flops 1024 | bytes 8192 | tf_op jit(solution)/shard_map/psum | solution.py:602
  117.2 12.0 %backward.1 = (bf16[1536,1024]{1,0:T(8,128)(2,1)}, bf16[256,1664]{1,0:T(8,128)(2,1)}, bf16[256,1664]{1,0:T(8,128)(2,1)}, f32[1,512]{1,0:T(1,128)}, f32[1,512]{1,0:T(1,128)}) custom-call(s32[32,128]{1,0:T(8,128)} %get-tuple-element.43.table_ref, bf16[1536,512]{1,0:T(8,128)(2,1)} %get-tuple-element.44.h_ref, bf16[1536,512]{1,0:T(8,128)(2,1)} %get-tuple-element.45.lin_ref, ...), custom_call_target="tpu_custom_call" | custom-call | flops 8000000000 | bytes 14155776 | tf_op jit(solution)/shard_map/backward/pallas_call | solution.py:495
  129.3 2.6 %collective-permute-done = bf16[256,1664]{1,0:T(8,128)(2,1)S(1)} collective-permute-done((bf16[256,1664]{1,0:T(8,128)(2,1)}, bf16[256,1664]{1,0:T(8,128)(2,1)S(1)}, u32[]{:S(2)}, u32[]{:S(2)}) %collective-permute-start) | collective-permute-done | bytes 852000 | tf_op jit(solution)/shard_map/ppermute | solution.py:571
  131.9 2.3 %fusion = bf16[32,8,1664]{2,1,0:T(8,128)(2,1)} fusion(bf16[256,1664]{1,0:T(8,128)(2,1)S(1)} %collective-permute-done, bf16[256,1664]{1,0:T(8,128)(2,1)} %get-tuple-element.63), kind=kLoop, calls=%fused_computation.1 | loop fusion | flops 1703936 | bytes 2555904 | tf_op jit(solution)/shard_map/reshape | solution.py:572
  134.2 7.4 %all-to-all-start.4 = ((bf16[32,8,1664]{2,1,0:T(8,128)(2,1)}), bf16[32,8,1664]{2,1,0:T(8,128)(2,1)S(1)}, u32[]{:S(2)}, u32[]{:S(2)}) async-start(bf16[32,8,1664]{2,1,0:T(8,128)(2,1)} %fusion), calls=%async_computation.4 | async-start | bytes 1703936 | tf_op jit(solution)/shard_map/all_to_all | solution.py:567
  141.6 6.8 %inputs_back.1 = bf16[1536,512]{1,0:T(8,128)(2,1)} custom-call(s32[32,128]{1,0:T(8,128)} %get-tuple-element.43.table_ref, bf16[1536,512]{1,0:T(8,128)(2,1)} %frames_ref.3, bf16[1536,1024]{1,0:T(8,128)(2,1)} %get-tuple-element.67.grad_a_ref, f32[1,512]{1,0:T(1,128)} %bitcast.22, bf16[512,1024]{1,0:T(8,128)(2,1)} %win_ref.3), custom_call_target="tpu_custom_call" | custom-call | flops 6000000000 | bytes 9437184 | tf_op jit(solution)/shard_map/inputs_back/pallas_call | solution.py:528
  148.4 3.5 %pack.1 = bf16[768,512]{1,0:T(8,128)(2,1)} custom-call(s32[32,128]{1,0:T(8,128)} %get-tuple-element.43.table_ref, bf16[1536,512]{1,0:T(8,128)(2,1)} %bitcast.14), custom_call_target="tpu_custom_call" | custom-call | flops 2000000000 | bytes 2359296 | tf_op jit(solution)/shard_map/pack/pallas_call | solution.py:400
  151.9 14.4 %all-to-all-done.4.got_ref = bf16[32,8,1664]{2,1,0:T(8,128)(2,1)S(1)} async-done(((bf16[32,8,1664]{2,1,0:T(8,128)(2,1)}), bf16[32,8,1664]{2,1,0:T(8,128)(2,1)S(1)}, u32[]{:S(2)}, u32[]{:S(2)}) %all-to-all-start.4) | async-done | bytes 852000 | tf_op jit(solution)/shard_map/all_to_all | solution.py:567
  167.2 3.4 %all-to-all-start.5 = ((bf16[8,8,1664]{2,1,0:T(8,128)(2,1)}), bf16[8,8,1664]{2,1,0:T(8,128)(2,1)S(1)}, u32[]{:S(2)}, u32[]{:S(2)}) async-start(bf16[8,8,1664]{2,1,0:T(8,128)(2,1)} %collect.1), calls=%async_computation.5 | async-start | bytes 425984 | tf_op jit(solution)/shard_map/all_to_all | solution.py:567
  172.1 5.4 %all-to-all-done.5.every_ref = bf16[8,8,1664]{2,1,0:T(8,128)(2,1)S(1)} async-done(((bf16[8,8,1664]{2,1,0:T(8,128)(2,1)}), bf16[8,8,1664]{2,1,0:T(8,128)(2,1)S(1)}, u32[]{:S(2)}, u32[]{:S(2)}) %all-to-all-start.5) | async-done | bytes 213024 | tf_op jit(solution)/shard_map/all_to_all | solution.py:567
  (16 shorter events, 4.7 us)
Async XLA Ops:
  5.2 11.4 %copy-start.2 = (f32[512,31]{0,1:T(8,128)S(1)}, f32[512,31]{0,1:T(8,128)}, u32[]{:S(2)}) copy-start(f32[512,31]{0,1:T(8,128)} %param.22) | copy-start | bytes 190468
  5.2 50.4 %all-to-all-start = ((bf16[32,48,512]{2,1,0:T(8,128)(2,1)}), bf16[32,48,512]{2,1,0:T(8,128)(2,1)S(1)}, u32[]{:S(2)}, u32[]{:S(2)}) async-start(bf16[32,48,512]{2,1,0:T(8,128)(2,1)} %bitcast.17), calls=%async_computation | async-start | bytes 3145728 | tf_op jit(solution)/shard_map/all_to_all | solution.py:567
  55.6 11.1 %copy-start.1 = (bf16[32,48,512]{2,1,0:T(8,128)(2,1)}, bf16[32,48,512]{2,1,0:T(8,128)(2,1)S(1)}, u32[]{:S(2)}) copy-start(bf16[32,48,512]{2,1,0:T(8,128)(2,1)S(1)} %all-to-all-done) | copy-start | bytes 4718596
  73.6 11.3 %all-to-all-start.2 = ((f32[8,8,128]{2,1,0:T(8,128)}), f32[8,8,128]{2,1,0:T(8,128)S(1)}, u32[]{:S(2)}, u32[]{:S(2)}) async-start(f32[8,8,128]{2,1,0:T(8,128)} %get-tuple-element.59), calls=%async_computation.2 | async-start | bytes 65536 | tf_op jit(solution)/shard_map/all_to_all | solution.py:567
  84.9 49.3 %all-to-all-start.3 = ((bf16[32,48,512]{2,1,0:T(8,128)(2,1)}), bf16[32,48,512]{2,1,0:T(8,128)(2,1)S(1)}, u32[]{:S(2)}, u32[]{:S(2)}) async-start(bf16[32,48,512]{2,1,0:T(8,128)(2,1)} %bitcast.15), calls=%async_computation.3 | async-start | bytes 3145728 | tf_op jit(solution)/shard_map/all_to_all | solution.py:567
  129.2 2.7 %collective-permute-start = (bf16[256,1664]{1,0:T(8,128)(2,1)}, bf16[256,1664]{1,0:T(8,128)(2,1)S(1)}, u32[]{:S(2)}, u32[]{:S(2)}) collective-permute-start(bf16[256,1664]{1,0:T(8,128)(2,1)} %get-tuple-element.64), channel_id=1, source_target_pairs={{0,32},{32,0},{1,33},{33,1},{2,34},{34,2},{3,35},{35,3},{4,36},{36... | collective-permute-start | bytes 2555912 | tf_op jit(solution)/shard_map/ppermute | solution.py:571
  134.2 14.2 %copy-start = (bf16[32,48,512]{2,1,0:T(8,128)(2,1)}, bf16[32,48,512]{2,1,0:T(8,128)(2,1)S(1)}, u32[]{:S(2)}) copy-start(bf16[32,48,512]{2,1,0:T(8,128)(2,1)S(1)} %all-to-all-done.3) | copy-start | bytes 4718596
  134.2 32.1 %all-to-all-start.4 = ((bf16[32,8,1664]{2,1,0:T(8,128)(2,1)}), bf16[32,8,1664]{2,1,0:T(8,128)(2,1)S(1)}, u32[]{:S(2)}, u32[]{:S(2)}) async-start(bf16[32,8,1664]{2,1,0:T(8,128)(2,1)} %fusion), calls=%async_computation.4 | async-start | bytes 1703936 | tf_op jit(solution)/shard_map/all_to_all | solution.py:567
  167.2 10.3 %all-to-all-start.5 = ((bf16[8,8,1664]{2,1,0:T(8,128)(2,1)}), bf16[8,8,1664]{2,1,0:T(8,128)(2,1)S(1)}, u32[]{:S(2)}, u32[]{:S(2)}) async-start(bf16[8,8,1664]{2,1,0:T(8,128)(2,1)} %collect.1), calls=%async_computation.5 | async-start | bytes 425984 | tf_op jit(solution)/shard_map/all_to_all | solution.py:567

commit v6 on v5

--- a/solution.py
+++ b/solution.py
@@ -21,6 +21,7 @@
 HALF = POINTS // 2
 PER_DFT = 4
 PER_STEP = 8
+UNROLL = 4
 VMEM_LIMIT = 60 * 2**20
 SMALL_LIMIT = 16 * 2**20
 
@@ -123,13 +124,15 @@
     wide[rows:, :] = jnp.zeros((8, wide.shape[1]), F32)
     copy.wait()
 
-    def step(i, start):
-        base = pl.multiple_of(start // 8 * 8, 8)
-        window = pltpu.roll(wide[pl.ds(base, SPAN + 8), :], SPAN + 8 - start % 8, 0)
-        out_ref[pl.ds(pl.multiple_of(i * SPAN, 16), SPAN), :] = window[:SPAN].astype(BF16)
-        return start + table[i, 0]
-
-    lax.fori_loop(0, loaders, step, jnp.int32(0))
+    def step(group, start):
+        for i in (group * UNROLL + k for k in range(UNROLL)):
+            base = pl.multiple_of(start // 8 * 8, 8)
+            window = pltpu.roll(wide[pl.ds(base, SPAN + 8), :], SPAN + 8 - start % 8, 0)
+            out_ref[pl.ds(pl.multiple_of(i * SPAN, 16), SPAN), :] = window[:SPAN].astype(BF16)
+            start += table[i, 0]
+        return start
+
+    lax.fori_loop(0, loaders // UNROLL, step, jnp.int32(0))
 
 
 def pack_kernel(table_ref, got_ref, out_ref, wide):
@@ -161,7 +164,7 @@
 
 def forward_kernel(
     table_ref, frames_ref, gain_ref, win_ref, qh_ref, ql_ref, ih_ref, il_ref, to_ref, wdw_ref,
-    h_ref, lin_ref, sig_ref, freq_ref, conv_ref, wf_ref, stats_ref, acc,
+    h_ref, slope_ref, sig_ref, freq_ref, conv_ref, wf_ref, stats_ref, acc,
 ):
     step = pl.program_id(0)
 
@@ -178,7 +181,7 @@
     a = dot(h, win_ref[...])
     lin = a[:, :d]
     sig = jax.nn.sigmoid(a[:, d:])
-    lin_ref[...] = lin.astype(BF16)
+    slope_ref[...] = (lin * sig * (1.0 - sig)).astype(BF16)
     sig_ref[...] = sig.astype(BF16)
     gated = masked(lin * sig, lens).astype(BF16)
     wa, wb, wl = (spread(wf_ref[...], k) for k in range(3))
@@ -218,9 +221,15 @@
     return centre, inverse
 
 
+def project_kernel(table_ref, dy_ref, wout_ref, live_dy_ref, grad_ref):
+    dy = masked(dy_ref[...].astype(F32), step_lens(table_ref)).astype(BF16)
+    live_dy_ref[...] = dy
+    grad_ref[...] = dot(dy, wout_ref[...], ((1,), (1,)))
+
+
 def middle_kernel(
-    total, table_ref, conv_ref, dy_ref, stats_ref, gain_ref, bias_ref, wout_ref,
-    swished_ref, live_dy_ref, gbn_ref, sums_ref, moments_ref, acc,
+    total, conv_ref, grad_ref, stats_ref, gain_ref, bias_ref,
+    swished_ref, gbn_ref, sums_ref, moments_ref, acc,
 ):
     step = pl.program_id(0)
 
@@ -234,9 +243,7 @@
     value = normed * gain_ref[...] + bias_ref[...]
     sig = jax.nn.sigmoid(value)
     swished_ref[...] = (value * sig).astype(BF16)
-    dy = masked(dy_ref[...].astype(F32), step_lens(table_ref)).astype(BF16)
-    live_dy_ref[...] = dy
-    grad = dot(dy, wout_ref[...], ((1,), (1,))) * (sig * (1.0 + value * (1.0 - sig)))
+    grad = grad_ref[...] * (sig * (1.0 + value * (1.0 - sig)))
     gbn_ref[...] = grad
     acc[0] += folded(grad)
     acc[1] += folded(grad * normed)
@@ -260,8 +267,8 @@
 
 
 def backward_kernel(
-    total, table_ref, h_ref, lin_ref, sig_ref, freq_ref, conv_ref, gbn_ref, wf_ref, stats_ref, sums_ref,
-    bn_gain_ref, theirs_in, own_in, qh_ref, ih_ref, back_ref,
+    total, table_ref, h_ref, slope_ref, sig_ref, freq_ref, conv_ref, gbn_ref, wf_ref, stats_ref, sums_ref,
+    bn_gain_ref, theirs_in, own_in, qh_ref, ql_ref, ih_ref, il_ref, back_ref,
     grad_a_ref, theirs_ref, own_ref, bias_ref, bn_out_ref, acc, h_all, ga_all,
 ):
     step = pl.program_id(0)
@@ -285,7 +292,7 @@
     parts = []
     for b in range(PER_STEP // PER_DFT):
         rows = slice(b * SPAN * PER_DFT, (b + 1) * SPAN * PER_DFT)
-        spec = dot(qh_ref[...], grad_conv[rows])
+        spec = dot(qh_ref[...], grad_conv[rows]) + dot(ql_ref[...], grad_conv[rows])
         re, im = spec[:n], spec[n:]
         own = freq_ref[b * 2 * n : (b + 1) * 2 * n, :].astype(F32)
         own_re, own_im = own[:n], own[n:]
@@ -295,12 +302,9 @@
         acc[:HALF] += jnp.sum(corr_re.reshape(PER_DFT, HALF, -1), axis=0)
         acc[HALF:] += jnp.sum(corr_im.reshape(PER_DFT, HALF, -1), axis=0)
         turned = jnp.concatenate([re * wa + im * wb, im * wl - re * wb], axis=0).astype(BF16)
-        parts.append(dot(ih_ref[...], turned))
+        parts.append(dot(ih_ref[...], turned) + dot(il_ref[...], turned))
     grad_gated = masked(jnp.concatenate(parts, axis=0), lens)
-    lin = lin_ref[...].astype(F32)
-    sig = sig_ref[...].astype(F32)
-    first = grad_gated * sig
-    grad_a = jnp.concatenate([first, first * lin * (1.0 - sig)], axis=1).astype(BF16)
+    grad_a = jnp.concatenate([grad_gated * s[...].astype(F32) for s in (sig_ref, slope_ref)], axis=1).astype(BF16)
     grad_a_ref[...] = grad_a
     rows = pl.ds(pl.multiple_of(step * PER_STEP * SPAN, 16), PER_STEP * SPAN)
     h_all[rows, :] = h_ref[...]
@@ -328,6 +332,10 @@
     grad_x = masked(grad_x, step_lens(table_ref)).astype(BF16)
     for u in range(PER_STEP):
         gframes_ref[slot_rows(table_ref, u), :] = grad_x[u * SPAN : (u + 1) * SPAN]
+
+
+def pair_kernel(own_ref, got_ref, both_ref):
+    both_ref[...] = (own_ref[...].astype(F32) + got_ref[...].astype(F32)).astype(BF16)
 
 
 def collect_kernel(got_ref, out_ref):
@@ -444,7 +452,23 @@
     )(table, frames, gain, w_in, high, low, high_t, low_t, taps_to, w_dw)
 
 
-def middle(total, table, conv, dy, stats, bn_gain, bn_bias, w_out, copies):
+def project(table, dy, w_out):
+    rows, d = dy.shape
+    steps = rows // (SPAN * PER_STEP)
+    part = rows_of((rows, d), steps)
+    return pl.pallas_call(
+        project_kernel,
+        grid=(steps,),
+        out_shape=(sds((rows, d), BF16), sds((rows, d), F32)),
+        in_specs=[SMEM, part, whole(w_out.shape)],
+        out_specs=(part, part),
+        compiler_params=params(),
+        name="project",
+        cost_estimate=cost(3e9, 6 * rows * d),
+    )(table, dy, w_out)
+
+
+def middle(total, conv, grad, stats, bn_gain, bn_bias, copies):
     rows, d = conv.shape
     steps = rows // (SPAN * PER_STEP)
     part = rows_of((rows, d), steps)
@@ -452,20 +476,14 @@
     return pl.pallas_call(
         functools.partial(middle_kernel, total),
         grid=(steps,),
-        out_shape=(
-            sds((rows, d), BF16),
-            sds((rows, d), BF16),
-            sds((rows, d), F32),
-            sds(tiles, F32),
-            sds((8, 128), F32),
-        ),
-        in_specs=[SMEM, part, part] + [whole(v.shape) for v in (stats, bn_gain, bn_bias, w_out)],
-        out_specs=(part, part, part, whole(tiles), whole((8, 128))),
+        out_shape=(sds((rows, d), BF16), sds((rows, d), F32), sds(tiles, F32), sds((8, 128), F32)),
+        in_specs=[part, part] + [whole(v.shape) for v in (stats, bn_gain, bn_bias)],
+        out_specs=(part, part, whole(tiles), whole((8, 128))),
         scratch_shapes=[pltpu.VMEM((2, 8, d), F32)],
         compiler_params=params(),
         name="middle",
-        cost_estimate=cost(5e9, 12 * rows * d),
-    )(table, conv, dy, stats, bn_gain, bn_bias, w_out)
+        cost_estimate=cost(4e9, 10 * rows * d),
+    )(conv, grad, stats, bn_gain, bn_bias)
 
 
 def outputs(swished, dy, w_out):
@@ -486,8 +504,8 @@
     )(swished, dy, w_out)
 
 
-def backward(total, table, h, lin, sig, freq, conv, gbn, wf, stats, sums, bn_gain, theirs, own, tabs):
-    high, _, high_t, _, _, back = tabs
+def backward(total, table, h, slope, sig, freq, conv, gbn, wf, stats, sums, bn_gain, theirs, own, tabs):
+    high, low, high_t, low_t, _, back = tabs
     rows, d = h.shape
     width = 3 * d + back.shape[1]
     steps = rows // (SPAN * PER_STEP)
@@ -503,7 +521,7 @@
             sds((1, d), F32),
         ),
         in_specs=[SMEM, part, part, part, rows_of(freq.shape, steps), part, part]
-        + [whole(v.shape) for v in (wf, stats, sums, bn_gain, theirs, own, high, high_t, back)],
+        + [whole(v.shape) for v in (wf, stats, sums, bn_gain, theirs, own, high, low, high_t, low_t, back)],
         out_specs=(
             rows_of((rows, 2 * d), steps),
             whole((d // 2, width)),
@@ -519,7 +537,7 @@
         compiler_params=params(),
         name="backward",
         cost_estimate=cost(8e9, 18 * rows * d),
-    )(table, h, lin, sig, freq, conv, gbn, wf, stats, sums, bn_gain, theirs, own, high, high_t, back)
+    )(table, h, slope, sig, freq, conv, gbn, wf, stats, sums, bn_gain, theirs, own, high, low, high_t, low_t, back)
 
 
 def inputs_back(table, frames, grad_a, gain, w_in):
@@ -537,6 +555,21 @@
     )(table, frames, grad_a, gain, w_in)
 
 
+def pair_sum(own, got):
+    rows, width = own.shape
+    part = pl.BlockSpec((rows // 2, width), lambda i: (i, 0))
+    return pl.pallas_call(
+        pair_kernel,
+        grid=(2,),
+        out_shape=sds((rows, width), BF16),
+        in_specs=[part, part],
+        out_specs=part,
+        compiler_params=pltpu.CompilerParams(vmem_limit_bytes=SMALL_LIMIT),
+        name="pair_sum",
+        cost_estimate=cost(2 * rows * width, 6 * rows * width),
+    )(own, got)
+
+
 def collect(got, count):
     vmem = pl.BlockSpec(memory_space=pltpu.VMEM)
     return pl.pallas_call(
@@ -569,7 +602,7 @@
 
 def over_bucket(theirs, own, loaders, ahead):
     got = lax.ppermute(theirs, "c", [(0, 1), (1, 0)])
-    both = (own.astype(F32) + got.astype(F32)).astype(BF16).reshape(loaders, -1, own.shape[1])
+    both = pair_sum(own, got).reshape(loaders, -1, own.shape[1])
     both, ahead = lax.optimization_barrier((both, ahead))
     return swapped(both, BUCKET), ahead
 
@@ -588,20 +621,19 @@
 
     dy, table = unpack(lengths, owners, upstream, loaders)
     dy = swapped(dy.reshape(loaders, SPAN, d), BUCKET).reshape(rows, d)
-    h, lin, sig, freq, conv, wf, stats = forward(table, frames, gain, w_in, w_dw, tabs)
+    h, slope, sig, freq, conv, wf, stats = forward(table, frames, gain, w_in, w_dw, tabs)
     stats = lax.psum(lax.psum(lax.psum(stats, "c"), "y"), "x")
     stats, dy = lax.optimization_barrier((stats, dy))
     stats = swapped(jnp.broadcast_to(stats, (lax.axis_size("z"), *stats.shape)), "z")
-    swished, live_dy, gbn, sums, stats = middle(
-        total, table, conv, dy, stats, bn_gain, bn_bias, w_out, lax.axis_size("z")
-    )
-    sums = jnp.sum(swapped(sums, "z"), axis=0)
+    live_dy, grad = project(table, dy, w_out)
+    swished, gbn, sums, stats = middle(total, conv, grad, stats, bn_gain, bn_bias, lax.axis_size(("c", "z")))
+    sums = jnp.sum(swapped(sums, ("c", "z")), axis=0)
     out, theirs, own = outputs(swished, live_dy, w_out)
     out, sums = lax.optimization_barrier((out, sums))
     out = swapped(out.reshape(loaders, SPAN, d), BUCKET).reshape(rows, d)
-    sums = functools.reduce(lax.psum, ("c", "y", "x"), sums)
+    sums = lax.psum(lax.psum(sums, "y"), "x")
     grad_a, theirs, own, bias_total, gain_total = backward(
-        total, table, h, lin, sig, freq, conv, gbn, wf, stats, sums, bn_gain, theirs, own, tabs
+        total, table, h, slope, sig, freq, conv, gbn, wf, stats, sums, bn_gain, theirs, own, tabs
     )
     got, out = over_bucket(theirs, own, loaders, out)
     gframes = inputs_back(table, frames, grad_a, gain, w_in)

time: 179 us -> 179 us (level)
  blocking collectives: 59.6 us -> 46 us
  Pallas kernels: 52.9 us -> 58.9 us
  starting transfers between devices: 34.7 us -> 40.1 us
  local copies, waits for them, and re-layouts: 2.39 us -> 4.81 us
  other arithmetic: 2.32 us -> 0.02 us
  waiting for transfers between devices: 25.6 us -> 27.4 us
    all_to_all x1 -> x0, blocking collectives: 11.1 us -> none  [swapped(): return lax.all_to_all(value, axes, split_axis=0, concat_axis=0, tiled=True)]
    pallas_call x0 -> x2, Pallas kernels: none -> 5.88 us  [the longest x1 4.84 us: project(): pl.pallas_call(project_kernel, grid=(steps,), out_shape=(sds((rows, d), B...]
    all_to_all x5 -> x6, starting transfers between devices: 34.6 us -> 40 us  [swapped(): return lax.all_to_all(value, axes, split_axis=0, concat_axis=0, tiled=True)]
    psum x3 -> x2, blocking collectives: 24.5 us -> 22.2 us  [local(): sums = lax.psum(lax.psum(sums, 'y'), 'x')]
    reshape x1 -> x0, other arithmetic: 2.31 us -> none  [over_bucket(): (own.astype(F32) + got.astype(F32)).astype(BF16)]
    all_to_all x5 -> x6, waiting for transfers between devices: 23 us -> 24.8 us  [swapped(): return lax.all_to_all(value, axes, split_axis=0, concat_axis=0, tiled=True)]
  transfers between devices with their start and end apart: 6 -> 7, of which waited for: 5 -> 6; matrix products, arithmetic and copies ran while one was open for 3% -> 1% of each run, Pallas kernels for 22% -> 26%
where the time goes in v6:
time: 179 us; the launch traced here: 178 us
  Pallas kernels  58.9 us (33%)
  blocking collectives  46 us (26%)
  starting transfers between devices  40.1 us (22%)
  waiting for transfers between devices  27.4 us (15%)
  local copies, waits for them, and re-layouts  4.81 us (3%)
    all_to_all x6, starting transfers between devices, swapped(): return lax.all_to_all(value, axes, split_axis=0, concat_axis=0, tiled=True)  40 us
    all_to_all x6, waiting for transfers between devices, swapped(): return lax.all_to_all(value, axes, split_axis=0, concat_axis=0, tiled=True)  24.8 us
    psum x3, blocking collectives, local(): stats = lax.psum(lax.psum(lax.psum(stats, 'c'), 'y'), 'x')  23.8 us
    psum x2, blocking collectives, local(): sums = lax.psum(lax.psum(sums, 'y'), 'x')  22.2 us
    pallas_call x1, Pallas kernels, backward(): pl.pallas_call(functools.partial(backward_kernel, total), grid=(steps,),...  12.6 us
    pallas_call x1, Pallas kernels, forward(): pl.pallas_call(forward_kernel, grid=(steps,), out_shape=(sds((rows, d), B...  12.2 us
    pallas_call x1, Pallas kernels, inputs_back(): pl.pallas_call(inputs_kernel, grid=(steps,), out_shape=sds((rows, d), BF1...  6.81 us
    pallas_call x1, Pallas kernels, middle(): pl.pallas_call(functools.partial(middle_kernel, total), grid=(steps,), ou...  6.17 us
  transfers between devices with their start and end apart: 7, of which 6 were waited for; matrix products, arithmetic and copies ran while one was open for 1% of the time, Pallas kernels for 26%

profile of v6, /device:TPU:32, one launch (start us, length us, event | category | flops | bytes accessed | tf_op | source)
XLA Modules:
  0.0 177.9 jit_solution(2765024903390541974)
XLA Ops:
  0.6 4.2 %unpack.1 = (bf16[1536,512]{1,0:T(8,128)(2,1)}, s32[32,128]{1,0:T(8,128)}) custom-call(s32[1,1024]{1,0:T(1,128)} %lengths_ref.1, s32[1,1024]{1,0:T(1,128)} %owners_ref.1, bf16[768,512]{1,0:T(8,128)(2,1)} %upstream_ref.1), custom_call_target="tpu_custom_call" | custom-call | flops 1000000000 | bytes 2359296 | tf_op jit(solution)/shard_map/unpack/pallas_call | solution.py:389
  4.9 11.3 %all-to-all-start = ((bf16[32,48,512]{2,1,0:T(8,128)(2,1)}), bf16[32,48,512]{2,1,0:T(8,128)(2,1)S(1)}, u32[]{:S(2)}, u32[]{:S(2)}) async-start(bf16[32,48,512]{2,1,0:T(8,128)(2,1)} %bitcast.16), calls=%async_computation | async-start | bytes 3145728 | tf_op jit(solution)/shard_map/all_to_all | solution.py:600
  17.1 12.2 %forward.1 = (bf16[1536,512]{1,0:T(8,128)(2,1)}, bf16[1536,512]{1,0:T(8,128)(2,1)}, bf16[1536,512]{1,0:T(8,128)(2,1)}, bf16[2048,512]{1,0:T(8,128)(2,1)}, f32[15...) custom-call(s32[32,128]{1,0:T(8,128)} %get-tuple-element.44.table_ref, bf16[1536,512]{1,0:T(8,128)(2,1)} %frames_ref.3, ...), custom_call_target="tpu_custom_call" | custom-call | flops 10000000000 | bytes 12582912 | tf_op jit(solution)/shard_map/forward/pallas_call | solution.py:425
  29.3 2.6 %psum.35 = f32[8,128]{1,0:T(8,128)S(1)} all-reduce(f32[8,128]{1,0:T(8,128)} %get-tuple-element.50), channel_id=1, replica_groups=mesh['y'=4,'c'=2,'x'=4,'z'=8] {'c'}, use_global_device_ids=true, to_apply=%region_0.0 | all-reduce | flops 1024 | bytes 8192 | tf_op jit(solution)/shard_map/psum | solution.py:625
  31.9 10.7 %psum.36 = f32[8,128]{1,0:T(8,128)S(1)} all-reduce(f32[8,128]{1,0:T(8,128)S(1)} %psum.35), channel_id=1, replica_groups=mesh['y'=4,'c'=2,'x'=4,'z'=8] {'y'}, use_global_device_ids=true, to_apply=%region_1.0 | all-reduce | flops 1024 | bytes 8192 | tf_op jit(solution)/shard_map/psum | solution.py:625
  42.6 10.5 %psum.37 = f32[8,128]{1,0:T(8,128)S(1)} all-reduce(f32[8,128]{1,0:T(8,128)S(1)} %psum.36), channel_id=1, replica_groups=mesh['y'=4,'c'=2,'x'=4,'z'=8] {'x'}, use_global_device_ids=true, to_apply=%region_2.0 | all-reduce | flops 1024 | bytes 8192 | tf_op jit(solution)/shard_map/psum | solution.py:625
  53.1 2.3 %all-to-all-done = bf16[32,48,512]{2,1,0:T(8,128)(2,1)S(1)} async-done(((bf16[32,48,512]{2,1,0:T(8,128)(2,1)}), bf16[32,48,512]{2,1,0:T(8,128)(2,1)S(1)}, u32[]{:S(2)}, u32[]{:S(2)}) %all-to-all-start) | async-done | bytes 1572896 | tf_op jit(solution)/shard_map/all_to_all | solution.py:600
  56.0 5.3 %all-to-all-start.1 = ((f32[8,8,128]{2,1,0:T(8,128)}), f32[8,8,128]{2,1,0:T(8,128)S(1)}, u32[]{:S(2)}, u32[]{:S(2)}) async-start(f32[8,8,128]{2,1,0:T(8,128)} %broadcast_in_dim.3), calls=%async_computation.1 | async-start | bytes 65536 | tf_op jit(solution)/shard_map/all_to_all | solution.py:600
  61.3 4.8 %project.1 = (bf16[1536,512]{1,0:T(8,128)(2,1)}, f32[1536,512]{1,0:T(8,128)}) custom-call(s32[32,128]{1,0:T(8,128)} %get-tuple-element.44.table_ref, bf16[1536,512]{1,0:T(8,128)(2,1)} %bitcast.15, bf16[512,512]{1,0:T(8,128)(2,1)} %wout_ref.3), custom_call_target="tpu_custom_call" | custom-call | flops 3000000000 | bytes 4718592 | tf_op jit(solution)/shard_map/project/pallas_call | solution.py:459
  66.2 1.7 all-to-all-done.1.stats_ref
  68.5 6.2 %middle.1 = (bf16[1536,512]{1,0:T(8,128)(2,1)}, f32[1536,512]{1,0:T(8,128)}, f32[16,8,128]{2,1,0:T(8,128)}, f32[8,128]{1,0:T(8,128)}) custom-call(f32[1536,512]{1,0:T(8,128)} %get-tuple-element.49.conv_ref, f32[1536,512]{1,0:T(8,128)} %get-tuple-element.53.grad_ref, f32[8,8,128]{2,1,0:T(8,128)} %copy-done.4, f32[1,512]{1,0:T(1,128)} %bitcast.18, ...), custom_call_target="tpu_custom_call" | custom-call | flops 4000000000 | bytes 7864320 | tf_op jit(solution)/shard_map/middle/pallas_call | solution.py:476
  74.7 5.5 %all-to-all-start.2 = ((f32[16,8,128]{2,1,0:T(8,128)}), f32[16,8,128]{2,1,0:T(8,128)S(1)}, u32[]{:S(2)}, u32[]{:S(2)}) async-start(f32[16,8,128]{2,1,0:T(8,128)} %get-tuple-element.61), calls=%async_computation.2 | async-start | bytes 131072 | tf_op jit(solution)/shard_map/all_to_all | solution.py:600
  80.2 6.0 %outputs.1 = (bf16[1536,512]{1,0:T(8,128)(2,1)}, bf16[256,512]{1,0:T(8,128)(2,1)}, bf16[256,512]{1,0:T(8,128)(2,1)}) custom-call(bf16[1536,512]{1,0:T(8,128)(2,1)} %get-tuple-element.58.swished_ref, bf16[1536,512]{1,0:T(8,128)(2,1)} %get-tuple-element.59.dy_ref, bf16[512,512]{1,0:T(8,128)(2,1)} %wout_ref.3), custom_call_target="tpu_custom_call" | custom-call | flops 4000000000 | bytes 4718592 | tf_op jit(solution)/shard_map/outputs/pallas_call | solution.py:494
  87.2 6.8 %all-to-all-start.3 = ((bf16[32,48,512]{2,1,0:T(8,128)(2,1)}), bf16[32,48,512]{2,1,0:T(8,128)(2,1)S(1)}, u32[]{:S(2)}, u32[]{:S(2)}) async-start(bf16[32,48,512]{2,1,0:T(8,128)(2,1)} %bitcast.14), calls=%async_computation.3 | async-start | bytes 3145728 | tf_op jit(solution)/shard_map/all_to_all | solution.py:600
  93.9 10.7 %psum.38 = f32[8,128]{1,0:T(8,128)S(1)} all-reduce(f32[8,128]{1,0:T(8,128)S(1)} %reduce_sum.9), channel_id=1, replica_groups=mesh['y'=4,'c'=2,'x'=4,'z'=8] {'y'}, use_global_device_ids=true, to_apply=%region_4.0 | all-reduce | flops 1024 | bytes 8192 | tf_op jit(solution)/shard_map/psum | solution.py:634
  104.7 11.4 %psum.39.sums_ref = f32[8,128]{1,0:T(8,128)} all-reduce(f32[8,128]{1,0:T(8,128)S(1)} %psum.38), channel_id=1, replica_groups=mesh['y'=4,'c'=2,'x'=4,'z'=8] {'x'}, use_global_device_ids=true, to_apply=%region_5.0 | all-reduce | flops 1024 | bytes 8192 | tf_op jit(solution)/shard_map/psum | solution.py:634
  116.1 12.6 %backward.1 = (bf16[1536,1024]{1,0:T(8,128)(2,1)}, bf16[256,1664]{1,0:T(8,128)(2,1)}, bf16[256,1664]{1,0:T(8,128)(2,1)}, f32[1,512]{1,0:T(1,128)}, f32[1,512]{1,0:T(1,128)}) custom-call(s32[32,128]{1,0:T(8,128)} %get-tuple-element.44.table_ref, bf16[1536,512]{1,0:T(8,128)(2,1)} %get-tuple-element.45.h_ref, bf16[1536,512]{1,0:T(8,128)(2,1)} %get-tuple-element.46.slope_ref, ...), custom_call_target="tpu_custom_call" | custom-call | flops 8000000000 | bytes 14155776 | tf_op jit(solution)/shard_map/backward/pallas_call | solution.py:513
  128.8 2.6 %collective-permute-done.got_ref = bf16[256,1664]{1,0:T(8,128)(2,1)S(1)} collective-permute-done((bf16[256,1664]{1,0:T(8,128)(2,1)}, bf16[256,1664]{1,0:T(8,128)(2,1)S(1)}, u32[]{:S(2)}, u32[]{:S(2)}) %collective-permute-start) | collective-permute-done | bytes 852000 | tf_op jit(solution)/shard_map/ppermute | solution.py:604
  133.6 7.7 %all-to-all-start.4 = ((bf16[32,8,1664]{2,1,0:T(8,128)(2,1)}), bf16[32,8,1664]{2,1,0:T(8,128)(2,1)S(1)}, u32[]{:S(2)}, u32[]{:S(2)}) async-start(bf16[32,8,1664]{2,1,0:T(8,128)(2,1)} %bitcast.5), calls=%async_computation.4 | async-start | bytes 1703936 | tf_op jit(solution)/shard_map/all_to_all | solution.py:600
  141.3 6.8 %inputs_back.1 = bf16[1536,512]{1,0:T(8,128)(2,1)} custom-call(s32[32,128]{1,0:T(8,128)} %get-tuple-element.44.table_ref, bf16[1536,512]{1,0:T(8,128)(2,1)} %frames_ref.3, bf16[1536,1024]{1,0:T(8,128)(2,1)} %get-tuple-element.69.grad_a_ref, f32[1,512]{1,0:T(1,128)} %bitcast.21, bf16[512,1024]{1,0:T(8,128)(2,1)} %win_ref.3), custom_call_target="tpu_custom_call" | custom-call | flops 6000000000 | bytes 9437184 | tf_op jit(solution)/shard_map/inputs_back/pallas_call | solution.py:546
  148.1 3.5 %pack.1 = bf16[768,512]{1,0:T(8,128)(2,1)} custom-call(s32[32,128]{1,0:T(8,128)} %get-tuple-element.44.table_ref, bf16[1536,512]{1,0:T(8,128)(2,1)} %bitcast.13), custom_call_target="tpu_custom_call" | custom-call | flops 2000000000 | bytes 2359296 | tf_op jit(solution)/shard_map/pack/pallas_call | solution.py:408
  151.6 14.4 %all-to-all-done.4.got_ref = bf16[32,8,1664]{2,1,0:T(8,128)(2,1)S(1)} async-done(((bf16[32,8,1664]{2,1,0:T(8,128)(2,1)}), bf16[32,8,1664]{2,1,0:T(8,128)(2,1)S(1)}, u32[]{:S(2)}, u32[]{:S(2)}) %all-to-all-start.4) | async-done | bytes 852000 | tf_op jit(solution)/shard_map/all_to_all | solution.py:600
  166.9 3.4 %all-to-all-start.5 = ((bf16[8,8,1664]{2,1,0:T(8,128)(2,1)}), bf16[8,8,1664]{2,1,0:T(8,128)(2,1)S(1)}, u32[]{:S(2)}, u32[]{:S(2)}) async-start(bf16[8,8,1664]{2,1,0:T(8,128)(2,1)} %collect.1), calls=%async_computation.5 | async-start | bytes 425984 | tf_op jit(solution)/shard_map/all_to_all | solution.py:600
  171.8 5.4 %all-to-all-done.5.every_ref = bf16[8,8,1664]{2,1,0:T(8,128)(2,1)S(1)} async-done(((bf16[8,8,1664]{2,1,0:T(8,128)(2,1)}), bf16[8,8,1664]{2,1,0:T(8,128)(2,1)S(1)}, u32[]{:S(2)}, u32[]{:S(2)}) %all-to-all-start.5) | async-done | bytes 213024 | tf_op jit(solution)/shard_map/all_to_all | solution.py:600
  (21 shorter events, 8.5 us)
Async XLA Ops:
  4.9 11.4 %copy-start.3 = (f32[512,31]{0,1:T(8,128)S(1)}, f32[512,31]{0,1:T(8,128)}, u32[]{:S(2)}) copy-start(f32[512,31]{0,1:T(8,128)} %param.22) | copy-start | bytes 190468
  4.9 50.4 %all-to-all-start = ((bf16[32,48,512]{2,1,0:T(8,128)(2,1)}), bf16[32,48,512]{2,1,0:T(8,128)(2,1)S(1)}, u32[]{:S(2)}, u32[]{:S(2)}) async-start(bf16[32,48,512]{2,1,0:T(8,128)(2,1)} %bitcast.16), calls=%async_computation | async-start | bytes 3145728 | tf_op jit(solution)/shard_map/all_to_all | solution.py:600
  55.3 6.0 %copy-start.2 = (bf16[32,48,512]{2,1,0:T(8,128)(2,1)}, bf16[32,48,512]{2,1,0:T(8,128)(2,1)S(1)}, u32[]{:S(2)}) copy-start(bf16[32,48,512]{2,1,0:T(8,128)(2,1)S(1)} %all-to-all-done) | copy-start | bytes 4718596
  56.0 11.9 %all-to-all-start.1 = ((f32[8,8,128]{2,1,0:T(8,128)}), f32[8,8,128]{2,1,0:T(8,128)S(1)}, u32[]{:S(2)}, u32[]{:S(2)}) async-start(f32[8,8,128]{2,1,0:T(8,128)} %broadcast_in_dim.3), calls=%async_computation.1 | async-start | bytes 65536 | tf_op jit(solution)/shard_map/all_to_all | solution.py:600
  67.9 0.6 copy-start.4
  74.7 12.5 %all-to-all-start.2 = ((f32[16,8,128]{2,1,0:T(8,128)}), f32[16,8,128]{2,1,0:T(8,128)S(1)}, u32[]{:S(2)}, u32[]{:S(2)}) async-start(f32[16,8,128]{2,1,0:T(8,128)} %get-tuple-element.61), calls=%async_computation.2 | async-start | bytes 131072 | tf_op jit(solution)/shard_map/all_to_all | solution.py:600
  87.2 46.4 %all-to-all-start.3 = ((bf16[32,48,512]{2,1,0:T(8,128)(2,1)}), bf16[32,48,512]{2,1,0:T(8,128)(2,1)S(1)}, u32[]{:S(2)}, u32[]{:S(2)}) async-start(bf16[32,48,512]{2,1,0:T(8,128)(2,1)} %bitcast.14), calls=%async_computation.3 | async-start | bytes 3145728 | tf_op jit(solution)/shard_map/all_to_all | solution.py:600
  128.7 2.7 %collective-permute-start = (bf16[256,1664]{1,0:T(8,128)(2,1)}, bf16[256,1664]{1,0:T(8,128)(2,1)S(1)}, u32[]{:S(2)}, u32[]{:S(2)}) collective-permute-start(bf16[256,1664]{1,0:T(8,128)(2,1)} %get-tuple-element.66), channel_id=1, source_target_pairs={{0,32},{32,0},{1,33},{33,1},{2,34},{34,2},{3,35},{35,3},{4,36},{36... | collective-permute-start | bytes 2555912 | tf_op jit(solution)/shard_map/ppermute | solution.py:604
  131.4 1.2 copy-start
  133.6 14.5 %copy-start.1 = (bf16[32,48,512]{2,1,0:T(8,128)(2,1)}, bf16[32,48,512]{2,1,0:T(8,128)(2,1)S(1)}, u32[]{:S(2)}) copy-start(bf16[32,48,512]{2,1,0:T(8,128)(2,1)S(1)} %all-to-all-done.3) | copy-start | bytes 4718596
  133.6 32.5 %all-to-all-start.4 = ((bf16[32,8,1664]{2,1,0:T(8,128)(2,1)}), bf16[32,8,1664]{2,1,0:T(8,128)(2,1)S(1)}, u32[]{:S(2)}, u32[]{:S(2)}) async-start(bf16[32,8,1664]{2,1,0:T(8,128)(2,1)} %bitcast.5), calls=%async_computation.4 | async-start | bytes 1703936 | tf_op jit(solution)/shard_map/all_to_all | solution.py:600
  166.9 10.3 %all-to-all-start.5 = ((bf16[8,8,1664]{2,1,0:T(8,128)(2,1)}), bf16[8,8,1664]{2,1,0:T(8,128)(2,1)S(1)}, u32[]{:S(2)}, u32[]{:S(2)}) async-start(bf16[8,8,1664]{2,1,0:T(8,128)(2,1)} %collect.1), calls=%async_computation.5 | async-start | bytes 425984 | tf_op jit(solution)/shard_map/all_to_all | solution.py:600

commit v7 on v6

--- a/solution.py
+++ b/solution.py
@@ -564,7 +564,7 @@
         out_shape=sds((rows, width), BF16),
         in_specs=[part, part],
         out_specs=part,
-        compiler_params=pltpu.CompilerParams(vmem_limit_bytes=SMALL_LIMIT),
+        compiler_params=pltpu.CompilerParams(vmem_limit_bytes=VMEM_LIMIT),
         name="pair_sum",
         cost_estimate=cost(2 * rows * width, 6 * rows * width),
     )(own, got)
@@ -600,11 +600,13 @@
     return lax.all_to_all(value, axes, split_axis=0, concat_axis=0, tiled=True)
 
 
-def over_bucket(theirs, own, loaders, ahead):
-    got = lax.ppermute(theirs, "c", [(0, 1), (1, 0)])
-    both = pair_sum(own, got).reshape(loaders, -1, own.shape[1])
+def over_bucket(theirs, own, ahead, beside):
+    width = own.shape[1]
+    both = pair_sum(own, lax.ppermute(theirs, "c", [(0, 1), (1, 0)]))
     both, ahead = lax.optimization_barrier((both, ahead))
-    return swapped(both, BUCKET), ahead
+    got = swapped(both.reshape(lax.axis_size("x"), -1, width), "x")
+    got, beside = lax.optimization_barrier((got, beside))
+    return swapped(collect(got, 1).reshape(lax.axis_size("z"), -1, width), "z"), ahead, beside
 
 
 def local(frames, lengths, owners, upstream, ln_gain, w_in, w_dw, bn_gain, bn_bias, w_out):
@@ -635,10 +637,10 @@
     grad_a, theirs, own, bias_total, gain_total = backward(
         total, table, h, slope, sig, freq, conv, gbn, wf, stats, sums, bn_gain, theirs, own, tabs
     )
-    got, out = over_bucket(theirs, own, loaders, out)
     gframes = inputs_back(table, frames, grad_a, gain, w_in)
+    got, out, gframes = over_bucket(theirs, own, out, gframes)
     out_frames = pack(table, out, upstream.shape[0])
-    got, gframes, out_frames = lax.optimization_barrier((got, gframes, out_frames))
+    got, out_frames = lax.optimization_barrier((got, out_frames))
     every = swapped(collect(got, lax.axis_size(DP)), DP)
     gwin, gwout, gwdw, gln = finish(every, w_rows, gain_rows, taps)
     return (

time: 179 us -> 183 us (1.022); the launches traced: 178 us -> 180 us
  starting transfers between devices: 40.1 us -> 42.7 us
  waiting for transfers between devices: 27.4 us -> 25.1 us
    all_to_all x6 -> x7, starting transfers between devices: 40 us -> 42.6 us  [swapped(): return lax.all_to_all(value, axes, split_axis=0, concat_axis=0, tiled=True)]
    all_to_all x6 -> x7, waiting for transfers between devices: 24.8 us -> 22.5 us  [swapped(): return lax.all_to_all(value, axes, split_axis=0, concat_axis=0, tiled=True)]
  transfers between devices with their start and end apart: 7 -> 8, of which waited for: 6 -> 7; matrix products, arithmetic and copies ran while one was open for 1% -> 1% of each run, Pallas kernels for 26% -> 27%
where the time goes in v7:
time: 183 us; the launch traced here: 180 us
  Pallas kernels  60.7 us (33%)
  blocking collectives  46 us (25%)
  starting transfers between devices  42.7 us (23%)
  waiting for transfers between devices  25.1 us (14%)
  local copies, waits for them, and re-layouts  4.55 us (2%)
    all_to_all x7, starting transfers between devices, swapped(): return lax.all_to_all(value, axes, split_axis=0, concat_axis=0, tiled=True)  42.6 us
    psum x3, blocking collectives, local(): stats = lax.psum(lax.psum(lax.psum(stats, 'c'), 'y'), 'x')  23.8 us
    all_to_all x7, waiting for transfers between devices, swapped(): return lax.all_to_all(value, axes, split_axis=0, concat_axis=0, tiled=True)  22.5 us
    psum x2, blocking collectives, local(): sums = lax.psum(lax.psum(sums, 'y'), 'x')  22.2 us
    pallas_call x1, Pallas kernels, backward(): pl.pallas_call(functools.partial(backward_kernel, total), grid=(steps,),...  12.6 us
    pallas_call x1, Pallas kernels, forward(): pl.pallas_call(forward_kernel, grid=(steps,), out_shape=(sds((rows, d), B...  12.2 us
    pallas_call x1, Pallas kernels, inputs_back(): pl.pallas_call(inputs_kernel, grid=(steps,), out_shape=sds((rows, d), BF1...  6.81 us
    pallas_call x1, Pallas kernels, middle(): pl.pallas_call(functools.partial(middle_kernel, total), grid=(steps,), ou...  6.16 us
  transfers between devices with their start and end apart: 8, of which 7 were waited for; matrix products, arithmetic and copies ran while one was open for 1% of the time, Pallas kernels for 27%

profile of v7, /device:TPU:32, one launch (start us, length us, event | category | flops | bytes accessed | tf_op | source)
XLA Modules:
  0.0 179.8 jit_solution(9486603430965472384)
XLA Ops:
  0.6 4.2 %unpack.1 = (bf16[1536,512]{1,0:T(8,128)(2,1)}, s32[32,128]{1,0:T(8,128)}) custom-call(s32[1,1024]{1,0:T(1,128)} %lengths_ref.1, s32[1,1024]{1,0:T(1,128)} %owners_ref.1, bf16[768,512]{1,0:T(8,128)(2,1)} %upstream_ref.1), custom_call_target="tpu_custom_call" | custom-call | flops 1000000000 | bytes 2359296 | tf_op jit(solution)/shard_map/unpack/pallas_call | solution.py:389
  4.9 11.3 %all-to-all-start = ((bf16[32,48,512]{2,1,0:T(8,128)(2,1)}), bf16[32,48,512]{2,1,0:T(8,128)(2,1)S(1)}, u32[]{:S(2)}, u32[]{:S(2)}) async-start(bf16[32,48,512]{2,1,0:T(8,128)(2,1)} %bitcast.18), calls=%async_computation | async-start | bytes 3145728 | tf_op jit(solution)/shard_map/all_to_all | solution.py:600
  17.1 12.2 %forward.1 = (bf16[1536,512]{1,0:T(8,128)(2,1)}, bf16[1536,512]{1,0:T(8,128)(2,1)}, bf16[1536,512]{1,0:T(8,128)(2,1)}, bf16[2048,512]{1,0:T(8,128)(2,1)}, f32[15...) custom-call(s32[32,128]{1,0:T(8,128)} %get-tuple-element.45.table_ref, bf16[1536,512]{1,0:T(8,128)(2,1)} %frames_ref.3, ...), custom_call_target="tpu_custom_call" | custom-call | flops 10000000000 | bytes 12582912 | tf_op jit(solution)/shard_map/forward/pallas_call | solution.py:425
  29.3 2.6 %psum.35 = f32[8,128]{1,0:T(8,128)S(1)} all-reduce(f32[8,128]{1,0:T(8,128)} %get-tuple-element.51), channel_id=1, replica_groups=mesh['y'=4,'c'=2,'x'=4,'z'=8] {'c'}, use_global_device_ids=true, to_apply=%region_0.0 | all-reduce | flops 1024 | bytes 8192 | tf_op jit(solution)/shard_map/psum | solution.py:627
  31.9 10.7 %psum.36 = f32[8,128]{1,0:T(8,128)S(1)} all-reduce(f32[8,128]{1,0:T(8,128)S(1)} %psum.35), channel_id=1, replica_groups=mesh['y'=4,'c'=2,'x'=4,'z'=8] {'y'}, use_global_device_ids=true, to_apply=%region_1.0 | all-reduce | flops 1024 | bytes 8192 | tf_op jit(solution)/shard_map/psum | solution.py:627
  42.6 10.5 %psum.37 = f32[8,128]{1,0:T(8,128)S(1)} all-reduce(f32[8,128]{1,0:T(8,128)S(1)} %psum.36), channel_id=1, replica_groups=mesh['y'=4,'c'=2,'x'=4,'z'=8] {'x'}, use_global_device_ids=true, to_apply=%region_2.0 | all-reduce | flops 1024 | bytes 8192 | tf_op jit(solution)/shard_map/psum | solution.py:627
  56.0 5.3 %all-to-all-start.1 = ((f32[8,8,128]{2,1,0:T(8,128)}), f32[8,8,128]{2,1,0:T(8,128)S(1)}, u32[]{:S(2)}, u32[]{:S(2)}) async-start(f32[8,8,128]{2,1,0:T(8,128)} %broadcast_in_dim.3), calls=%async_computation.1 | async-start | bytes 65536 | tf_op jit(solution)/shard_map/all_to_all | solution.py:600
  61.3 4.8 %project.1 = (bf16[1536,512]{1,0:T(8,128)(2,1)}, f32[1536,512]{1,0:T(8,128)}) custom-call(s32[32,128]{1,0:T(8,128)} %get-tuple-element.45.table_ref, bf16[1536,512]{1,0:T(8,128)(2,1)} %bitcast.17, bf16[512,512]{1,0:T(8,128)(2,1)} %wout_ref.3), custom_call_target="tpu_custom_call" | custom-call | flops 3000000000 | bytes 4718592 | tf_op jit(solution)/shard_map/project/pallas_call | solution.py:459
  68.5 6.2 %middle.1 = (bf16[1536,512]{1,0:T(8,128)(2,1)}, f32[1536,512]{1,0:T(8,128)}, f32[16,8,128]{2,1,0:T(8,128)}, f32[8,128]{1,0:T(8,128)}) custom-call(f32[1536,512]{1,0:T(8,128)} %get-tuple-element.50.conv_ref, f32[1536,512]{1,0:T(8,128)} %get-tuple-element.54.grad_ref, f32[8,8,128]{2,1,0:T(8,128)} %copy-done.4, f32[1,512]{1,0:T(1,128)} %bitcast.20, ...), custom_call_target="tpu_custom_call" | custom-call | flops 4000000000 | bytes 7864320 | tf_op jit(solution)/shard_map/middle/pallas_call | solution.py:476
  74.6 5.5 %all-to-all-start.2 = ((f32[16,8,128]{2,1,0:T(8,128)}), f32[16,8,128]{2,1,0:T(8,128)S(1)}, u32[]{:S(2)}, u32[]{:S(2)}) async-start(f32[16,8,128]{2,1,0:T(8,128)} %get-tuple-element.62), calls=%async_computation.2 | async-start | bytes 131072 | tf_op jit(solution)/shard_map/all_to_all | solution.py:600
  80.1 6.0 %outputs.1 = (bf16[1536,512]{1,0:T(8,128)(2,1)}, bf16[256,512]{1,0:T(8,128)(2,1)}, bf16[256,512]{1,0:T(8,128)(2,1)}) custom-call(bf16[1536,512]{1,0:T(8,128)(2,1)} %get-tuple-element.59.swished_ref, bf16[1536,512]{1,0:T(8,128)(2,1)} %get-tuple-element.60.dy_ref, bf16[512,512]{1,0:T(8,128)(2,1)} %wout_ref.3), custom_call_target="tpu_custom_call" | custom-call | flops 4000000000 | bytes 4718592 | tf_op jit(solution)/shard_map/outputs/pallas_call | solution.py:494
  87.1 6.7 %all-to-all-start.3 = ((bf16[32,48,512]{2,1,0:T(8,128)(2,1)}), bf16[32,48,512]{2,1,0:T(8,128)(2,1)S(1)}, u32[]{:S(2)}, u32[]{:S(2)}) async-start(bf16[32,48,512]{2,1,0:T(8,128)(2,1)} %bitcast.16), calls=%async_computation.3 | async-start | bytes 3145728 | tf_op jit(solution)/shard_map/all_to_all | solution.py:600
  93.9 10.7 %psum.38 = f32[8,128]{1,0:T(8,128)S(1)} all-reduce(f32[8,128]{1,0:T(8,128)S(1)} %reduce_sum.9), channel_id=1, replica_groups=mesh['y'=4,'c'=2,'x'=4,'z'=8] {'y'}, use_global_device_ids=true, to_apply=%region_4.0 | all-reduce | flops 1024 | bytes 8192 | tf_op jit(solution)/shard_map/psum | solution.py:636
  104.6 11.4 %psum.39.sums_ref = f32[8,128]{1,0:T(8,128)} all-reduce(f32[8,128]{1,0:T(8,128)S(1)} %psum.38), channel_id=1, replica_groups=mesh['y'=4,'c'=2,'x'=4,'z'=8] {'x'}, use_global_device_ids=true, to_apply=%region_5.0 | all-reduce | flops 1024 | bytes 8192 | tf_op jit(solution)/shard_map/psum | solution.py:636
  116.1 12.6 %backward.1 = (bf16[1536,1024]{1,0:T(8,128)(2,1)}, bf16[256,1664]{1,0:T(8,128)(2,1)}, bf16[256,1664]{1,0:T(8,128)(2,1)}, f32[1,512]{1,0:T(1,128)}, f32[1,512]{1,0:T(1,128)}) custom-call(s32[32,128]{1,0:T(8,128)} %get-tuple-element.45.table_ref, bf16[1536,512]{1,0:T(8,128)(2,1)} %get-tuple-element.46.h_ref, bf16[1536,512]{1,0:T(8,128)(2,1)} %get-tuple-element.47.slope_ref, ...), custom_call_target="tpu_custom_call" | custom-call | flops 8000000000 | bytes 14155776 | tf_op jit(solution)/shard_map/backward/pallas_call | solution.py:513
  128.8 2.6 %collective-permute-done.got_ref = bf16[256,1664]{1,0:T(8,128)(2,1)S(1)} collective-permute-done((bf16[256,1664]{1,0:T(8,128)(2,1)}, bf16[256,1664]{1,0:T(8,128)(2,1)S(1)}, u32[]{:S(2)}, u32[]{:S(2)}) %collective-permute-start) | collective-permute-done | bytes 852000 | tf_op jit(solution)/shard_map/ppermute | solution.py:605
  134.5 3.5 %all-to-all-start.4 = ((bf16[4,64,1664]{2,1,0:T(8,128)(2,1)}), bf16[4,64,1664]{2,1,0:T(8,128)(2,1)S(1)}, u32[]{:S(2)}, u32[]{:S(2)}) async-start(bf16[4,64,1664]{2,1,0:T(8,128)(2,1)} %bitcast.14), calls=%async_computation.4 | async-start | bytes 1703936 | tf_op jit(solution)/shard_map/all_to_all | solution.py:600
  138.0 6.8 %inputs_back.1 = bf16[1536,512]{1,0:T(8,128)(2,1)} custom-call(s32[32,128]{1,0:T(8,128)} %get-tuple-element.45.table_ref, bf16[1536,512]{1,0:T(8,128)(2,1)} %frames_ref.3, bf16[1536,1024]{1,0:T(8,128)(2,1)} %get-tuple-element.70.grad_a_ref, f32[1,512]{1,0:T(1,128)} %bitcast.23, bf16[512,1024]{1,0:T(8,128)(2,1)} %win_ref.3), custom_call_target="tpu_custom_call" | custom-call | flops 6000000000 | bytes 9437184 | tf_op jit(solution)/shard_map/inputs_back/pallas_call | solution.py:546
  144.8 6.7 %all-to-all-done.4.got_ref = bf16[4,64,1664]{2,1,0:T(8,128)(2,1)S(1)} async-done(((bf16[4,64,1664]{2,1,0:T(8,128)(2,1)}), bf16[4,64,1664]{2,1,0:T(8,128)(2,1)S(1)}, u32[]{:S(2)}, u32[]{:S(2)}) %all-to-all-start.4) | async-done | bytes 852000 | tf_op jit(solution)/shard_map/all_to_all | solution.py:600
  152.3 6.9 %all-to-all-start.5 = ((bf16[8,8,1664]{2,1,0:T(8,128)(2,1)}), bf16[8,8,1664]{2,1,0:T(8,128)(2,1)S(1)}, u32[]{:S(2)}, u32[]{:S(2)}) async-start(bf16[8,8,1664]{2,1,0:T(8,128)(2,1)} %bitcast.8), calls=%async_computation.5 | async-start | bytes 425984 | tf_op jit(solution)/shard_map/all_to_all | solution.py:600
  159.2 3.5 %pack.1 = bf16[768,512]{1,0:T(8,128)(2,1)} custom-call(s32[32,128]{1,0:T(8,128)} %get-tuple-element.45.table_ref, bf16[1536,512]{1,0:T(8,128)(2,1)} %bitcast.15), custom_call_target="tpu_custom_call" | custom-call | flops 2000000000 | bytes 2359296 | tf_op jit(solution)/shard_map/pack/pallas_call | solution.py:408
  162.7 5.4 %all-to-all-done.5.got_ref = bf16[8,8,1664]{2,1,0:T(8,128)(2,1)S(1)} async-done(((bf16[8,8,1664]{2,1,0:T(8,128)(2,1)}), bf16[8,8,1664]{2,1,0:T(8,128)(2,1)S(1)}, u32[]{:S(2)}, u32[]{:S(2)}) %all-to-all-start.5) | async-done | bytes 213024 | tf_op jit(solution)/shard_map/all_to_all | solution.py:600
  168.8 3.4 %all-to-all-start.6 = ((bf16[8,8,1664]{2,1,0:T(8,128)(2,1)}), bf16[8,8,1664]{2,1,0:T(8,128)(2,1)S(1)}, u32[]{:S(2)}, u32[]{:S(2)}) async-start(bf16[8,8,1664]{2,1,0:T(8,128)(2,1)} %collect.3), calls=%async_computation.6 | async-start | bytes 425984 | tf_op jit(solution)/shard_map/all_to_all | solution.py:600
  173.7 5.4 %all-to-all-done.6.every_ref = bf16[8,8,1664]{2,1,0:T(8,128)(2,1)S(1)} async-done(((bf16[8,8,1664]{2,1,0:T(8,128)(2,1)}), bf16[8,8,1664]{2,1,0:T(8,128)(2,1)S(1)}, u32[]{:S(2)}, u32[]{:S(2)}) %all-to-all-start.6) | async-done | bytes 213024 | tf_op jit(solution)/shard_map/all_to_all | solution.py:600
  (24 shorter events, 14.2 us)
Async XLA Ops:
  4.9 11.4 %copy-start.3 = (f32[512,31]{0,1:T(8,128)S(1)}, f32[512,31]{0,1:T(8,128)}, u32[]{:S(2)}) copy-start(f32[512,31]{0,1:T(8,128)} %param.22) | copy-start | bytes 190468
  4.9 50.4 %all-to-all-start = ((bf16[32,48,512]{2,1,0:T(8,128)(2,1)}), bf16[32,48,512]{2,1,0:T(8,128)(2,1)S(1)}, u32[]{:S(2)}, u32[]{:S(2)}) async-start(bf16[32,48,512]{2,1,0:T(8,128)(2,1)} %bitcast.18), calls=%async_computation | async-start | bytes 3145728 | tf_op jit(solution)/shard_map/all_to_all | solution.py:600
  55.3 6.0 %copy-start.1 = (bf16[32,48,512]{2,1,0:T(8,128)(2,1)}, bf16[32,48,512]{2,1,0:T(8,128)(2,1)S(1)}, u32[]{:S(2)}) copy-start(bf16[32,48,512]{2,1,0:T(8,128)(2,1)S(1)} %all-to-all-done) | copy-start | bytes 4718596
  56.0 11.9 %all-to-all-start.1 = ((f32[8,8,128]{2,1,0:T(8,128)}), f32[8,8,128]{2,1,0:T(8,128)S(1)}, u32[]{:S(2)}, u32[]{:S(2)}) async-start(f32[8,8,128]{2,1,0:T(8,128)} %broadcast_in_dim.3), calls=%async_computation.1 | async-start | bytes 65536 | tf_op jit(solution)/shard_map/all_to_all | solution.py:600
  67.9 0.6 copy-start.4
  74.6 12.5 %all-to-all-start.2 = ((f32[16,8,128]{2,1,0:T(8,128)}), f32[16,8,128]{2,1,0:T(8,128)S(1)}, u32[]{:S(2)}, u32[]{:S(2)}) async-start(f32[16,8,128]{2,1,0:T(8,128)} %get-tuple-element.62), calls=%async_computation.2 | async-start | bytes 131072 | tf_op jit(solution)/shard_map/all_to_all | solution.py:600
  87.1 47.4 %all-to-all-start.3 = ((bf16[32,48,512]{2,1,0:T(8,128)(2,1)}), bf16[32,48,512]{2,1,0:T(8,128)(2,1)S(1)}, u32[]{:S(2)}, u32[]{:S(2)}) async-start(bf16[32,48,512]{2,1,0:T(8,128)(2,1)} %bitcast.16), calls=%async_computation.3 | async-start | bytes 3145728 | tf_op jit(solution)/shard_map/all_to_all | solution.py:600
  128.7 2.7 %collective-permute-start = (bf16[256,1664]{1,0:T(8,128)(2,1)}, bf16[256,1664]{1,0:T(8,128)(2,1)S(1)}, u32[]{:S(2)}, u32[]{:S(2)}) collective-permute-start(bf16[256,1664]{1,0:T(8,128)(2,1)} %get-tuple-element.67), channel_id=1, source_target_pairs={{0,32},{32,0},{1,33},{33,1},{2,34},{34,2},{3,35},{35,3},{4,36},{36... | collective-permute-start | bytes 2555912 | tf_op jit(solution)/shard_map/ppermute | solution.py:605
  131.3 0.9 copy-start.2
  134.5 10.3 %copy-start = (bf16[32,48,512]{2,1,0:T(8,128)(2,1)}, bf16[32,48,512]{2,1,0:T(8,128)(2,1)S(1)}, u32[]{:S(2)}) copy-start(bf16[32,48,512]{2,1,0:T(8,128)(2,1)S(1)} %all-to-all-done.3) | copy-start | bytes 4718596
  134.5 17.0 %all-to-all-start.4 = ((bf16[4,64,1664]{2,1,0:T(8,128)(2,1)}), bf16[4,64,1664]{2,1,0:T(8,128)(2,1)S(1)}, u32[]{:S(2)}, u32[]{:S(2)}) async-start(bf16[4,64,1664]{2,1,0:T(8,128)(2,1)} %bitcast.14), calls=%async_computation.4 | async-start | bytes 1703936 | tf_op jit(solution)/shard_map/all_to_all | solution.py:600
  152.3 15.7 %all-to-all-start.5 = ((bf16[8,8,1664]{2,1,0:T(8,128)(2,1)}), bf16[8,8,1664]{2,1,0:T(8,128)(2,1)S(1)}, u32[]{:S(2)}, u32[]{:S(2)}) async-start(bf16[8,8,1664]{2,1,0:T(8,128)(2,1)} %bitcast.8), calls=%async_computation.5 | async-start | bytes 425984 | tf_op jit(solution)/shard_map/all_to_all | solution.py:600
  168.8 10.3 %all-to-all-start.6 = ((bf16[8,8,1664]{2,1,0:T(8,128)(2,1)}), bf16[8,8,1664]{2,1,0:T(8,128)(2,1)S(1)}, u32[]{:S(2)}, u32[]{:S(2)}) async-start(bf16[8,8,1664]{2,1,0:T(8,128)(2,1)} %collect.3), calls=%async_computation.6 | async-start | bytes 425984 | tf_op jit(solution)/shard_map/all_to_all | solution.py:600

commit v8 on v6

--- a/solution.py
+++ b/solution.py
@@ -20,7 +20,7 @@
 POINTS = 64
 HALF = POINTS // 2
 PER_DFT = 4
-PER_STEP = 8
+PER_STEP = 16
 UNROLL = 4
 VMEM_LIMIT = 60 * 2**20
 SMALL_LIMIT = 16 * 2**20

time: 179 us -> 176 us (0.983)
  Pallas kernels: 58.9 us -> 55.1 us
  waiting for transfers between devices: 27.4 us -> 30 us
  starting transfers between devices: 40.1 us -> 37.8 us
    all_to_all x6, waiting for transfers between devices: 24.8 us -> 27.4 us  [swapped(): return lax.all_to_all(value, axes, split_axis=0, concat_axis=0, tiled=True)]
    all_to_all x6, starting transfers between devices: 40 us -> 37.7 us  [swapped(): return lax.all_to_all(value, axes, split_axis=0, concat_axis=0, tiled=True)]
  transfers between devices with their start and end apart: 7 -> 7, of which waited for: 6 -> 6; matrix products, arithmetic and copies ran while one was open for 1% -> 1% of each run, Pallas kernels for 26% -> 25%
where the time goes in v8:
time: 176 us; the launch traced here: 175 us
  Pallas kernels  55.1 us (31%)
  blocking collectives  46.4 us (26%)
  starting transfers between devices  37.8 us (21%)
  waiting for transfers between devices  30 us (17%)
  local copies, waits for them, and re-layouts  4.81 us (3%)
    all_to_all x6, starting transfers between devices, swapped(): return lax.all_to_all(value, axes, split_axis=0, concat_axis=0, tiled=True)  37.7 us
    all_to_all x6, waiting for transfers between devices, swapped(): return lax.all_to_all(value, axes, split_axis=0, concat_axis=0, tiled=True)  27.4 us
    psum x3, blocking collectives, local(): stats = lax.psum(lax.psum(lax.psum(stats, 'c'), 'y'), 'x')  23.9 us
    psum x2, blocking collectives, local(): sums = lax.psum(lax.psum(sums, 'y'), 'x')  22.5 us
    pallas_call x1, Pallas kernels, backward(): pl.pallas_call(functools.partial(backward_kernel, total), grid=(steps,),...  12.4 us
    pallas_call x1, Pallas kernels, forward(): pl.pallas_call(forward_kernel, grid=(steps,), out_shape=(sds((rows, d), B...  11.9 us
    pallas_call x1, Pallas kernels, inputs_back(): pl.pallas_call(inputs_kernel, grid=(steps,), out_shape=sds((rows, d), BF1...  6.53 us
    pallas_call x1, Pallas kernels, middle(): pl.pallas_call(functools.partial(middle_kernel, total), grid=(steps,), ou...  5.24 us
  transfers between devices with their start and end apart: 7, of which 6 were waited for; matrix products, arithmetic and copies ran while one was open for 1% of the time, Pallas kernels for 25%

profile of v8, /device:TPU:32, one launch (start us, length us, event | category | flops | bytes accessed | tf_op | source)
XLA Modules:
  0.0 174.9 jit_solution(12190676189970364199)
XLA Ops:
  0.6 4.2 %unpack.1 = (bf16[1536,512]{1,0:T(8,128)(2,1)}, s32[32,128]{1,0:T(8,128)}) custom-call(s32[1,1024]{1,0:T(1,128)} %lengths_ref.1, s32[1,1024]{1,0:T(1,128)} %owners_ref.1, bf16[768,512]{1,0:T(8,128)(2,1)} %upstream_ref.1), custom_call_target="tpu_custom_call" | custom-call | flops 1000000000 | bytes 2359296 | tf_op jit(solution)/shard_map/unpack/pallas_call | solution.py:389
  4.9 11.3 %all-to-all-start = ((bf16[32,48,512]{2,1,0:T(8,128)(2,1)}), bf16[32,48,512]{2,1,0:T(8,128)(2,1)S(1)}, u32[]{:S(2)}, u32[]{:S(2)}) async-start(bf16[32,48,512]{2,1,0:T(8,128)(2,1)} %bitcast.16), calls=%async_computation | async-start | bytes 3145728 | tf_op jit(solution)/shard_map/all_to_all | solution.py:600
  17.1 11.9 %forward.1 = (bf16[1536,512]{1,0:T(8,128)(2,1)}, bf16[1536,512]{1,0:T(8,128)(2,1)}, bf16[1536,512]{1,0:T(8,128)(2,1)}, bf16[2048,512]{1,0:T(8,128)(2,1)}, f32[15...) custom-call(s32[32,128]{1,0:T(8,128)} %get-tuple-element.44.table_ref, bf16[1536,512]{1,0:T(8,128)(2,1)} %frames_ref.3, ...), custom_call_target="tpu_custom_call" | custom-call | flops 10000000000 | bytes 12582912 | tf_op jit(solution)/shard_map/forward/pallas_call | solution.py:425
  29.0 2.6 %psum.35 = f32[8,128]{1,0:T(8,128)S(1)} all-reduce(f32[8,128]{1,0:T(8,128)} %get-tuple-element.50), channel_id=1, replica_groups=mesh['y'=4,'c'=2,'x'=4,'z'=8] {'c'}, use_global_device_ids=true, to_apply=%region_0.0 | all-reduce | flops 1024 | bytes 8192 | tf_op jit(solution)/shard_map/psum | solution.py:625
  31.6 10.7 %psum.36 = f32[8,128]{1,0:T(8,128)S(1)} all-reduce(f32[8,128]{1,0:T(8,128)S(1)} %psum.35), channel_id=1, replica_groups=mesh['y'=4,'c'=2,'x'=4,'z'=8] {'y'}, use_global_device_ids=true, to_apply=%region_1.0 | all-reduce | flops 1024 | bytes 8192 | tf_op jit(solution)/shard_map/psum | solution.py:625
  42.3 10.6 %psum.37 = f32[8,128]{1,0:T(8,128)S(1)} all-reduce(f32[8,128]{1,0:T(8,128)S(1)} %psum.36), channel_id=1, replica_groups=mesh['y'=4,'c'=2,'x'=4,'z'=8] {'x'}, use_global_device_ids=true, to_apply=%region_2.0 | all-reduce | flops 1024 | bytes 8192 | tf_op jit(solution)/shard_map/psum | solution.py:625
  52.9 2.5 %all-to-all-done = bf16[32,48,512]{2,1,0:T(8,128)(2,1)S(1)} async-done(((bf16[32,48,512]{2,1,0:T(8,128)(2,1)}), bf16[32,48,512]{2,1,0:T(8,128)(2,1)S(1)}, u32[]{:S(2)}, u32[]{:S(2)}) %all-to-all-start) | async-done | bytes 1572896 | tf_op jit(solution)/shard_map/all_to_all | solution.py:600
  56.0 4.6 %all-to-all-start.1 = ((f32[8,8,128]{2,1,0:T(8,128)}), f32[8,8,128]{2,1,0:T(8,128)S(1)}, u32[]{:S(2)}, u32[]{:S(2)}) async-start(f32[8,8,128]{2,1,0:T(8,128)} %broadcast_in_dim.3), calls=%async_computation.1 | async-start | bytes 65536 | tf_op jit(solution)/shard_map/all_to_all | solution.py:600
  60.6 3.9 %project.1 = (bf16[1536,512]{1,0:T(8,128)(2,1)}, f32[1536,512]{1,0:T(8,128)}) custom-call(s32[32,128]{1,0:T(8,128)} %get-tuple-element.44.table_ref, bf16[1536,512]{1,0:T(8,128)(2,1)} %bitcast.15, bf16[512,512]{1,0:T(8,128)(2,1)} %wout_ref.3), custom_call_target="tpu_custom_call" | custom-call | flops 3000000000 | bytes 4718592 | tf_op jit(solution)/shard_map/project/pallas_call | solution.py:459
  64.5 2.7 %all-to-all-done.1.stats_ref = f32[8,8,128]{2,1,0:T(8,128)S(1)} async-done(((f32[8,8,128]{2,1,0:T(8,128)}), f32[8,8,128]{2,1,0:T(8,128)S(1)}, u32[]{:S(2)}, u32[]{:S(2)}) %all-to-all-start.1) | async-done | bytes 32800 | tf_op jit(solution)/shard_map/all_to_all | solution.py:600
  67.8 5.2 %middle.1 = (bf16[1536,512]{1,0:T(8,128)(2,1)}, f32[1536,512]{1,0:T(8,128)}, f32[16,8,128]{2,1,0:T(8,128)}, f32[8,128]{1,0:T(8,128)}) custom-call(f32[1536,512]{1,0:T(8,128)} %get-tuple-element.49.conv_ref, f32[1536,512]{1,0:T(8,128)} %get-tuple-element.53.grad_ref, f32[8,8,128]{2,1,0:T(8,128)} %copy-done.4, f32[1,512]{1,0:T(1,128)} %bitcast.18, ...), custom_call_target="tpu_custom_call" | custom-call | flops 4000000000 | bytes 7864320 | tf_op jit(solution)/shard_map/middle/pallas_call | solution.py:476
  73.1 4.8 %all-to-all-start.2 = ((f32[16,8,128]{2,1,0:T(8,128)}), f32[16,8,128]{2,1,0:T(8,128)S(1)}, u32[]{:S(2)}, u32[]{:S(2)}) async-start(f32[16,8,128]{2,1,0:T(8,128)} %get-tuple-element.61), calls=%async_computation.2 | async-start | bytes 131072 | tf_op jit(solution)/shard_map/all_to_all | solution.py:600
  77.8 5.0 %outputs.1 = (bf16[1536,512]{1,0:T(8,128)(2,1)}, bf16[256,512]{1,0:T(8,128)(2,1)}, bf16[256,512]{1,0:T(8,128)(2,1)}) custom-call(bf16[1536,512]{1,0:T(8,128)(2,1)} %get-tuple-element.58.swished_ref, bf16[1536,512]{1,0:T(8,128)(2,1)} %get-tuple-element.59.dy_ref, bf16[512,512]{1,0:T(8,128)(2,1)} %wout_ref.3), custom_call_target="tpu_custom_call" | custom-call | flops 4000000000 | bytes 4718592 | tf_op jit(solution)/shard_map/outputs/pallas_call | solution.py:494
  84.9 6.4 %all-to-all-start.3 = ((bf16[32,48,512]{2,1,0:T(8,128)(2,1)}), bf16[32,48,512]{2,1,0:T(8,128)(2,1)S(1)}, u32[]{:S(2)}, u32[]{:S(2)}) async-start(bf16[32,48,512]{2,1,0:T(8,128)(2,1)} %bitcast.14), calls=%async_computation.3 | async-start | bytes 3145728 | tf_op jit(solution)/shard_map/all_to_all | solution.py:600
  91.2 10.8 %psum.38 = f32[8,128]{1,0:T(8,128)S(1)} all-reduce(f32[8,128]{1,0:T(8,128)S(1)} %reduce_sum.9), channel_id=1, replica_groups=mesh['y'=4,'c'=2,'x'=4,'z'=8] {'y'}, use_global_device_ids=true, to_apply=%region_4.0 | all-reduce | flops 1024 | bytes 8192 | tf_op jit(solution)/shard_map/psum | solution.py:634
  102.0 11.8 %psum.39.sums_ref = f32[8,128]{1,0:T(8,128)} all-reduce(f32[8,128]{1,0:T(8,128)S(1)} %psum.38), channel_id=1, replica_groups=mesh['y'=4,'c'=2,'x'=4,'z'=8] {'x'}, use_global_device_ids=true, to_apply=%region_5.0 | all-reduce | flops 1024 | bytes 8192 | tf_op jit(solution)/shard_map/psum | solution.py:634
  113.8 12.4 %backward.1 = (bf16[1536,1024]{1,0:T(8,128)(2,1)}, bf16[256,1664]{1,0:T(8,128)(2,1)}, bf16[256,1664]{1,0:T(8,128)(2,1)}, f32[1,512]{1,0:T(1,128)}, f32[1,512]{1,0:T(1,128)}) custom-call(s32[32,128]{1,0:T(8,128)} %get-tuple-element.44.table_ref, bf16[1536,512]{1,0:T(8,128)(2,1)} %get-tuple-element.45.h_ref, bf16[1536,512]{1,0:T(8,128)(2,1)} %get-tuple-element.46.slope_ref, ...), custom_call_target="tpu_custom_call" | custom-call | flops 8000000000 | bytes 14155776 | tf_op jit(solution)/shard_map/backward/pallas_call | solution.py:513
  126.3 2.6 %collective-permute-done.got_ref = bf16[256,1664]{1,0:T(8,128)(2,1)S(1)} collective-permute-done((bf16[256,1664]{1,0:T(8,128)(2,1)}, bf16[256,1664]{1,0:T(8,128)(2,1)S(1)}, u32[]{:S(2)}, u32[]{:S(2)}) %collective-permute-start) | collective-permute-done | bytes 852000 | tf_op jit(solution)/shard_map/ppermute | solution.py:604
  131.1 7.2 %all-to-all-start.4 = ((bf16[32,8,1664]{2,1,0:T(8,128)(2,1)}), bf16[32,8,1664]{2,1,0:T(8,128)(2,1)S(1)}, u32[]{:S(2)}, u32[]{:S(2)}) async-start(bf16[32,8,1664]{2,1,0:T(8,128)(2,1)} %bitcast.5), calls=%async_computation.4 | async-start | bytes 1703936 | tf_op jit(solution)/shard_map/all_to_all | solution.py:600
  138.3 6.5 %inputs_back.1 = bf16[1536,512]{1,0:T(8,128)(2,1)} custom-call(s32[32,128]{1,0:T(8,128)} %get-tuple-element.44.table_ref, bf16[1536,512]{1,0:T(8,128)(2,1)} %frames_ref.3, bf16[1536,1024]{1,0:T(8,128)(2,1)} %get-tuple-element.69.grad_a_ref, f32[1,512]{1,0:T(1,128)} %bitcast.21, bf16[512,1024]{1,0:T(8,128)(2,1)} %win_ref.3), custom_call_target="tpu_custom_call" | custom-call | flops 6000000000 | bytes 9437184 | tf_op jit(solution)/shard_map/inputs_back/pallas_call | solution.py:546
  144.8 3.5 %pack.1 = bf16[768,512]{1,0:T(8,128)(2,1)} custom-call(s32[32,128]{1,0:T(8,128)} %get-tuple-element.44.table_ref, bf16[1536,512]{1,0:T(8,128)(2,1)} %bitcast.13), custom_call_target="tpu_custom_call" | custom-call | flops 2000000000 | bytes 2359296 | tf_op jit(solution)/shard_map/pack/pallas_call | solution.py:408
  148.3 14.7 %all-to-all-done.4.got_ref = bf16[32,8,1664]{2,1,0:T(8,128)(2,1)S(1)} async-done(((bf16[32,8,1664]{2,1,0:T(8,128)(2,1)}), bf16[32,8,1664]{2,1,0:T(8,128)(2,1)S(1)}, u32[]{:S(2)}, u32[]{:S(2)}) %all-to-all-start.4) | async-done | bytes 852000 | tf_op jit(solution)/shard_map/all_to_all | solution.py:600
  163.8 3.4 %all-to-all-start.5 = ((bf16[8,8,1664]{2,1,0:T(8,128)(2,1)}), bf16[8,8,1664]{2,1,0:T(8,128)(2,1)S(1)}, u32[]{:S(2)}, u32[]{:S(2)}) async-start(bf16[8,8,1664]{2,1,0:T(8,128)(2,1)} %collect.1), calls=%async_computation.5 | async-start | bytes 425984 | tf_op jit(solution)/shard_map/all_to_all | solution.py:600
  168.8 5.4 %all-to-all-done.5.every_ref = bf16[8,8,1664]{2,1,0:T(8,128)(2,1)S(1)} async-done(((bf16[8,8,1664]{2,1,0:T(8,128)(2,1)}), bf16[8,8,1664]{2,1,0:T(8,128)(2,1)S(1)}, u32[]{:S(2)}, u32[]{:S(2)}) %all-to-all-start.5) | async-done | bytes 213024 | tf_op jit(solution)/shard_map/all_to_all | solution.py:600
  (21 shorter events, 9.5 us)
Async XLA Ops:
  4.9 11.4 %copy-start.3 = (f32[512,31]{0,1:T(8,128)S(1)}, f32[512,31]{0,1:T(8,128)}, u32[]{:S(2)}) copy-start(f32[512,31]{0,1:T(8,128)} %param.22) | copy-start | bytes 190468
  4.9 50.4 %all-to-all-start = ((bf16[32,48,512]{2,1,0:T(8,128)(2,1)}), bf16[32,48,512]{2,1,0:T(8,128)(2,1)S(1)}, u32[]{:S(2)}, u32[]{:S(2)}) async-start(bf16[32,48,512]{2,1,0:T(8,128)(2,1)} %bitcast.16), calls=%async_computation | async-start | bytes 3145728 | tf_op jit(solution)/shard_map/all_to_all | solution.py:600
  55.3 5.3 %copy-start.2 = (bf16[32,48,512]{2,1,0:T(8,128)(2,1)}, bf16[32,48,512]{2,1,0:T(8,128)(2,1)S(1)}, u32[]{:S(2)}) copy-start(bf16[32,48,512]{2,1,0:T(8,128)(2,1)S(1)} %all-to-all-done) | copy-start | bytes 4718596
  56.0 11.2 %all-to-all-start.1 = ((f32[8,8,128]{2,1,0:T(8,128)}), f32[8,8,128]{2,1,0:T(8,128)S(1)}, u32[]{:S(2)}, u32[]{:S(2)}) async-start(f32[8,8,128]{2,1,0:T(8,128)} %broadcast_in_dim.3), calls=%async_computation.1 | async-start | bytes 65536 | tf_op jit(solution)/shard_map/all_to_all | solution.py:600
  67.2 0.6 copy-start.4
  73.1 11.8 %all-to-all-start.2 = ((f32[16,8,128]{2,1,0:T(8,128)}), f32[16,8,128]{2,1,0:T(8,128)S(1)}, u32[]{:S(2)}, u32[]{:S(2)}) async-start(f32[16,8,128]{2,1,0:T(8,128)} %get-tuple-element.61), calls=%async_computation.2 | async-start | bytes 131072 | tf_op jit(solution)/shard_map/all_to_all | solution.py:600
  84.9 46.2 %all-to-all-start.3 = ((bf16[32,48,512]{2,1,0:T(8,128)(2,1)}), bf16[32,48,512]{2,1,0:T(8,128)(2,1)S(1)}, u32[]{:S(2)}, u32[]{:S(2)}) async-start(bf16[32,48,512]{2,1,0:T(8,128)(2,1)} %bitcast.14), calls=%async_computation.3 | async-start | bytes 3145728 | tf_op jit(solution)/shard_map/all_to_all | solution.py:600
  126.2 2.7 %collective-permute-start = (bf16[256,1664]{1,0:T(8,128)(2,1)}, bf16[256,1664]{1,0:T(8,128)(2,1)S(1)}, u32[]{:S(2)}, u32[]{:S(2)}) collective-permute-start(bf16[256,1664]{1,0:T(8,128)(2,1)} %get-tuple-element.66), channel_id=1, source_target_pairs={{0,32},{32,0},{1,33},{33,1},{2,34},{34,2},{3,35},{35,3},{4,36},{36... | collective-permute-start | bytes 2555912 | tf_op jit(solution)/shard_map/ppermute | solution.py:604
  128.9 1.2 copy-start
  131.1 13.7 %copy-start.1 = (bf16[32,48,512]{2,1,0:T(8,128)(2,1)}, bf16[32,48,512]{2,1,0:T(8,128)(2,1)S(1)}, u32[]{:S(2)}) copy-start(bf16[32,48,512]{2,1,0:T(8,128)(2,1)S(1)} %all-to-all-done.3) | copy-start | bytes 4718596
  131.1 32.0 %all-to-all-start.4 = ((bf16[32,8,1664]{2,1,0:T(8,128)(2,1)}), bf16[32,8,1664]{2,1,0:T(8,128)(2,1)S(1)}, u32[]{:S(2)}, u32[]{:S(2)}) async-start(bf16[32,8,1664]{2,1,0:T(8,128)(2,1)} %bitcast.5), calls=%async_computation.4 | async-start | bytes 1703936 | tf_op jit(solution)/shard_map/all_to_all | solution.py:600
  163.8 10.3 %all-to-all-start.5 = ((bf16[8,8,1664]{2,1,0:T(8,128)(2,1)}), bf16[8,8,1664]{2,1,0:T(8,128)(2,1)S(1)}, u32[]{:S(2)}, u32[]{:S(2)}) async-start(bf16[8,8,1664]{2,1,0:T(8,128)(2,1)} %collect.1), calls=%async_computation.5 | async-start | bytes 425984 | tf_op jit(solution)/shard_map/all_to_all | solution.py:600

commit v9 on v8

--- a/solution.py
+++ b/solution.py
@@ -21,7 +21,7 @@
 HALF = POINTS // 2
 PER_DFT = 4
 PER_STEP = 16
-UNROLL = 4
+UNROLL = 8
 VMEM_LIMIT = 60 * 2**20
 SMALL_LIMIT = 16 * 2**20
 
@@ -203,7 +203,7 @@
     @pl.when(step == pl.num_programs(0) - 1)
     def _():
         sums = [jnp.sum(acc[k], axis=0, keepdims=True) for k in range(2)]
-        stats_ref[...] = as_tile(*sums)
+        stats_ref[...] = jnp.broadcast_to(as_tile(*sums)[None], stats_ref.shape)
 
 
 def split(value, theirs_ref, own_ref):
@@ -417,7 +417,7 @@
     )(table, got)
 
 
-def forward(table, frames, gain, w_in, w_dw, tabs):
+def forward(table, frames, gain, w_in, w_dw, tabs, copies):
     high, low, high_t, low_t, taps_to, _ = tabs
     rows, d = frames.shape
     steps = rows // (SPAN * PER_STEP)
@@ -432,7 +432,7 @@
             sds(freq, BF16),
             sds((rows, d), F32),
             sds((3 * HALF, d), F32),
-            sds((8, 128), F32),
+            sds((copies, 8, 128), F32),
         ),
         in_specs=[SMEM, whole(frames.shape), whole(gain.shape), whole(w_in.shape)]
         + [whole(v.shape) for v in (high, low, high_t, low_t, taps_to, w_dw)],
@@ -443,7 +443,7 @@
             rows_of(freq, steps),
             rows_of((rows, d), steps),
             whole((3 * HALF, d)),
-            whole((8, 128)),
+            whole((copies, 8, 128)),
         ),
         scratch_shapes=[pltpu.VMEM((2, 8, d), F32)],
         compiler_params=params(),
@@ -621,10 +621,10 @@
 
     dy, table = unpack(lengths, owners, upstream, loaders)
     dy = swapped(dy.reshape(loaders, SPAN, d), BUCKET).reshape(rows, d)
-    h, slope, sig, freq, conv, wf, stats = forward(table, frames, gain, w_in, w_dw, tabs)
+    h, slope, sig, freq, conv, wf, stats = forward(table, frames, gain, w_in, w_dw, tabs, lax.axis_size("z"))
     stats = lax.psum(lax.psum(lax.psum(stats, "c"), "y"), "x")
     stats, dy = lax.optimization_barrier((stats, dy))
-    stats = swapped(jnp.broadcast_to(stats, (lax.axis_size("z"), *stats.shape)), "z")
+    stats = swapped(stats, "z")
     live_dy, grad = project(table, dy, w_out)
     swished, gbn, sums, stats = middle(total, conv, grad, stats, bn_gain, bn_bias, lax.axis_size(("c", "z")))
     sums = jnp.sum(swapped(sums, ("c", "z")), axis=0)

time: 176 us -> 189 us (1.074)
  blocking collectives: 46.4 us -> 58.1 us
    psum x3, blocking collectives: 23.9 us -> 39 us  [local(): stats = lax.psum(lax.psum(lax.psum(stats, 'c'), 'y'), 'x')]
    psum x2, blocking collectives: 22.5 us -> 19.1 us  [local(): sums = lax.psum(lax.psum(sums, 'y'), 'x')]
  transfers between devices with their start and end apart: 7 -> 7, of which waited for: 6 -> 6; matrix products, arithmetic and copies ran while one was open for 1% -> 1% of each run, Pallas kernels for 25% -> 24%
where the time goes in v9:
time: 189 us; the launch traced here: 188 us
  blocking collectives  58.1 us (31%)
  Pallas kernels  55.2 us (29%)
  starting transfers between devices  39.3 us (21%)
  waiting for transfers between devices  30.1 us (16%)
  local copies, waits for them, and re-layouts  4.15 us (2%)
    all_to_all x6, starting transfers between devices, swapped(): return lax.all_to_all(value, axes, split_axis=0, concat_axis=0, tiled=True)  39.2 us
    psum x3, blocking collectives, local(): stats = lax.psum(lax.psum(lax.psum(stats, 'c'), 'y'), 'x')  39 us
    all_to_all x6, waiting for transfers between devices, swapped(): return lax.all_to_all(value, axes, split_axis=0, concat_axis=0, tiled=True)  27.5 us
    psum x2, blocking collectives, local(): sums = lax.psum(lax.psum(sums, 'y'), 'x')  19.1 us
    pallas_call x1, Pallas kernels, backward(): pl.pallas_call(functools.partial(backward_kernel, total), grid=(steps,),...  12.4 us
    pallas_call x1, Pallas kernels, forward(): pl.pallas_call(forward_kernel, grid=(steps,), out_shape=(sds((rows, d), B...  11.9 us
    pallas_call x1, Pallas kernels, inputs_back(): pl.pallas_call(inputs_kernel, grid=(steps,), out_shape=sds((rows, d), BF1...  6.53 us
    pallas_call x1, Pallas kernels, middle(): pl.pallas_call(functools.partial(middle_kernel, total), grid=(steps,), ou...  5.24 us
  transfers between devices with their start and end apart: 7, of which 6 were waited for; matrix products, arithmetic and copies ran while one was open for 1% of the time, Pallas kernels for 24%

profile of v9, /device:TPU:32, one launch (start us, length us, event | category | flops | bytes accessed | tf_op | source)
XLA Modules:
  0.0 187.6 jit_solution(2193149053055283011)
XLA Ops:
  0.6 4.3 %unpack.1 = (bf16[1536,512]{1,0:T(8,128)(2,1)}, s32[32,128]{1,0:T(8,128)}) custom-call(s32[1,1024]{1,0:T(1,128)} %lengths_ref.1, s32[1,1024]{1,0:T(1,128)} %owners_ref.1, bf16[768,512]{1,0:T(8,128)(2,1)} %upstream_ref.1), custom_call_target="tpu_custom_call" | custom-call | flops 1000000000 | bytes 2359296 | tf_op jit(solution)/shard_map/unpack/pallas_call | solution.py:389
  4.9 11.3 %all-to-all-start = ((bf16[32,48,512]{2,1,0:T(8,128)(2,1)}), bf16[32,48,512]{2,1,0:T(8,128)(2,1)S(1)}, u32[]{:S(2)}, u32[]{:S(2)}) async-start(bf16[32,48,512]{2,1,0:T(8,128)(2,1)} %bitcast.16), calls=%async_computation | async-start | bytes 3145728 | tf_op jit(solution)/shard_map/all_to_all | solution.py:600
  17.1 11.9 %forward.1 = (bf16[1536,512]{1,0:T(8,128)(2,1)}, bf16[1536,512]{1,0:T(8,128)(2,1)}, bf16[1536,512]{1,0:T(8,128)(2,1)}, bf16[2048,512]{1,0:T(8,128)(2,1)}, f32[15...) custom-call(s32[32,128]{1,0:T(8,128)} %get-tuple-element.44.table_ref, bf16[1536,512]{1,0:T(8,128)(2,1)} %frames_ref.3, ...), custom_call_target="tpu_custom_call" | custom-call | flops 10000000000 | bytes 12582912 | tf_op jit(solution)/shard_map/forward/pallas_call | solution.py:425
  29.0 4.1 %psum.35 = f32[8,8,128]{2,1,0:T(8,128)S(1)} all-reduce(f32[8,8,128]{2,1,0:T(8,128)} %get-tuple-element.50), channel_id=1, replica_groups=mesh['y'=4,'c'=2,'x'=4,'z'=8] {'c'}, use_global_device_ids=true, to_apply=%region_0.0 | all-reduce | flops 8192 | bytes 65536 | tf_op jit(solution)/shard_map/psum | solution.py:625
  33.1 17.3 %psum.36 = f32[8,8,128]{2,1,0:T(8,128)S(1)} all-reduce(f32[8,8,128]{2,1,0:T(8,128)S(1)} %psum.35), channel_id=1, replica_groups=mesh['y'=4,'c'=2,'x'=4,'z'=8] {'y'}, use_global_device_ids=true, to_apply=%region_1.0 | all-reduce | flops 8192 | bytes 65536 | tf_op jit(solution)/shard_map/psum | solution.py:625
  50.4 17.6 %psum.37 = f32[8,8,128]{2,1,0:T(8,128)} all-reduce(f32[8,8,128]{2,1,0:T(8,128)S(1)} %psum.36), channel_id=1, replica_groups=mesh['y'=4,'c'=2,'x'=4,'z'=8] {'x'}, use_global_device_ids=true, to_apply=%region_2.0 | all-reduce | flops 8192 | bytes 65536 | tf_op jit(solution)/shard_map/psum | solution.py:625
  68.0 7.2 %all-to-all-start.1 = ((f32[8,8,128]{2,1,0:T(8,128)}), f32[8,8,128]{2,1,0:T(8,128)S(1)}, u32[]{:S(2)}, u32[]{:S(2)}) async-start(f32[8,8,128]{2,1,0:T(8,128)} %psum.37), calls=%async_computation.1 | async-start | bytes 65536 | tf_op jit(solution)/shard_map/all_to_all | solution.py:600
  75.3 3.9 %project.1 = (bf16[1536,512]{1,0:T(8,128)(2,1)}, f32[1536,512]{1,0:T(8,128)}) custom-call(s32[32,128]{1,0:T(8,128)} %get-tuple-element.44.table_ref, bf16[1536,512]{1,0:T(8,128)(2,1)} %bitcast.15, bf16[512,512]{1,0:T(8,128)(2,1)} %wout_ref.3), custom_call_target="tpu_custom_call" | custom-call | flops 3000000000 | bytes 4718592 | tf_op jit(solution)/shard_map/project/pallas_call | solution.py:459
  79.1 2.7 %all-to-all-done.1.stats_ref = f32[8,8,128]{2,1,0:T(8,128)S(1)} async-done(((f32[8,8,128]{2,1,0:T(8,128)}), f32[8,8,128]{2,1,0:T(8,128)S(1)}, u32[]{:S(2)}, u32[]{:S(2)}) %all-to-all-start.1) | async-done | bytes 32800 | tf_op jit(solution)/shard_map/all_to_all | solution.py:600
  82.5 5.2 %middle.1 = (bf16[1536,512]{1,0:T(8,128)(2,1)}, f32[1536,512]{1,0:T(8,128)}, f32[16,8,128]{2,1,0:T(8,128)}, f32[8,128]{1,0:T(8,128)}) custom-call(f32[1536,512]{1,0:T(8,128)} %get-tuple-element.49.conv_ref, f32[1536,512]{1,0:T(8,128)} %get-tuple-element.53.grad_ref, f32[8,8,128]{2,1,0:T(8,128)} %copy-done.4, f32[1,512]{1,0:T(1,128)} %bitcast.18, ...), custom_call_target="tpu_custom_call" | custom-call | flops 4000000000 | bytes 7864320 | tf_op jit(solution)/shard_map/middle/pallas_call | solution.py:476
  87.7 4.8 %all-to-all-start.2 = ((f32[16,8,128]{2,1,0:T(8,128)}), f32[16,8,128]{2,1,0:T(8,128)S(1)}, u32[]{:S(2)}, u32[]{:S(2)}) async-start(f32[16,8,128]{2,1,0:T(8,128)} %get-tuple-element.61), calls=%async_computation.2 | async-start | bytes 131072 | tf_op jit(solution)/shard_map/all_to_all | solution.py:600
  92.5 5.0 %outputs.1 = (bf16[1536,512]{1,0:T(8,128)(2,1)}, bf16[256,512]{1,0:T(8,128)(2,1)}, bf16[256,512]{1,0:T(8,128)(2,1)}) custom-call(bf16[1536,512]{1,0:T(8,128)(2,1)} %get-tuple-element.58.swished_ref, bf16[1536,512]{1,0:T(8,128)(2,1)} %get-tuple-element.59.dy_ref, bf16[512,512]{1,0:T(8,128)(2,1)} %wout_ref.3), custom_call_target="tpu_custom_call" | custom-call | flops 4000000000 | bytes 4718592 | tf_op jit(solution)/shard_map/outputs/pallas_call | solution.py:494
  99.5 6.2 %all-to-all-start.3 = ((bf16[32,48,512]{2,1,0:T(8,128)(2,1)}), bf16[32,48,512]{2,1,0:T(8,128)(2,1)S(1)}, u32[]{:S(2)}, u32[]{:S(2)}) async-start(bf16[32,48,512]{2,1,0:T(8,128)(2,1)} %bitcast.14), calls=%async_computation.3 | async-start | bytes 3145728 | tf_op jit(solution)/shard_map/all_to_all | solution.py:600
  105.7 7.8 %psum.38 = f32[8,128]{1,0:T(8,128)S(1)} all-reduce(f32[8,128]{1,0:T(8,128)S(1)} %reduce_sum.9), channel_id=1, replica_groups=mesh['y'=4,'c'=2,'x'=4,'z'=8] {'y'}, use_global_device_ids=true, to_apply=%region_4.0 | all-reduce | flops 1024 | bytes 8192 | tf_op jit(solution)/shard_map/psum | solution.py:634
  113.5 11.3 %psum.39.sums_ref = f32[8,128]{1,0:T(8,128)} all-reduce(f32[8,128]{1,0:T(8,128)S(1)} %psum.38), channel_id=1, replica_groups=mesh['y'=4,'c'=2,'x'=4,'z'=8] {'x'}, use_global_device_ids=true, to_apply=%region_5.0 | all-reduce | flops 1024 | bytes 8192 | tf_op jit(solution)/shard_map/psum | solution.py:634
  124.8 12.4 %backward.1 = (bf16[1536,1024]{1,0:T(8,128)(2,1)}, bf16[256,1664]{1,0:T(8,128)(2,1)}, bf16[256,1664]{1,0:T(8,128)(2,1)}, f32[1,512]{1,0:T(1,128)}, f32[1,512]{1,0:T(1,128)}) custom-call(s32[32,128]{1,0:T(8,128)} %get-tuple-element.44.table_ref, bf16[1536,512]{1,0:T(8,128)(2,1)} %get-tuple-element.45.h_ref, bf16[1536,512]{1,0:T(8,128)(2,1)} %get-tuple-element.46.slope_ref, ...), custom_call_target="tpu_custom_call" | custom-call | flops 8000000000 | bytes 14155776 | tf_op jit(solution)/shard_map/backward/pallas_call | solution.py:513
  137.3 2.6 %collective-permute-done.got_ref = bf16[256,1664]{1,0:T(8,128)(2,1)S(1)} collective-permute-done((bf16[256,1664]{1,0:T(8,128)(2,1)}, bf16[256,1664]{1,0:T(8,128)(2,1)S(1)}, u32[]{:S(2)}, u32[]{:S(2)}) %collective-permute-start) | collective-permute-done | bytes 852000 | tf_op jit(solution)/shard_map/ppermute | solution.py:604
  142.1 2.7 %all-to-all-done.3 = bf16[32,48,512]{2,1,0:T(8,128)(2,1)S(1)} async-done(((bf16[32,48,512]{2,1,0:T(8,128)(2,1)}), bf16[32,48,512]{2,1,0:T(8,128)(2,1)S(1)}, u32[]{:S(2)}, u32[]{:S(2)}) %all-to-all-start.3) | async-done | bytes 1572896 | tf_op jit(solution)/shard_map/all_to_all | solution.py:600
  144.8 6.2 %all-to-all-start.4 = ((bf16[32,8,1664]{2,1,0:T(8,128)(2,1)}), bf16[32,8,1664]{2,1,0:T(8,128)(2,1)S(1)}, u32[]{:S(2)}, u32[]{:S(2)}) async-start(bf16[32,8,1664]{2,1,0:T(8,128)(2,1)} %bitcast.5), calls=%async_computation.4 | async-start | bytes 1703936 | tf_op jit(solution)/shard_map/all_to_all | solution.py:600
  151.0 6.5 %inputs_back.1 = bf16[1536,512]{1,0:T(8,128)(2,1)} custom-call(s32[32,128]{1,0:T(8,128)} %get-tuple-element.44.table_ref, bf16[1536,512]{1,0:T(8,128)(2,1)} %frames_ref.3, bf16[1536,1024]{1,0:T(8,128)(2,1)} %get-tuple-element.69.grad_a_ref, f32[1,512]{1,0:T(1,128)} %bitcast.21, bf16[512,1024]{1,0:T(8,128)(2,1)} %win_ref.3), custom_call_target="tpu_custom_call" | custom-call | flops 6000000000 | bytes 9437184 | tf_op jit(solution)/shard_map/inputs_back/pallas_call | solution.py:546
  157.6 3.5 %pack.1 = bf16[768,512]{1,0:T(8,128)(2,1)} custom-call(s32[32,128]{1,0:T(8,128)} %get-tuple-element.44.table_ref, bf16[1536,512]{1,0:T(8,128)(2,1)} %bitcast.13), custom_call_target="tpu_custom_call" | custom-call | flops 2000000000 | bytes 2359296 | tf_op jit(solution)/shard_map/pack/pallas_call | solution.py:408
  161.0 14.7 %all-to-all-done.4.got_ref = bf16[32,8,1664]{2,1,0:T(8,128)(2,1)S(1)} async-done(((bf16[32,8,1664]{2,1,0:T(8,128)(2,1)}), bf16[32,8,1664]{2,1,0:T(8,128)(2,1)S(1)}, u32[]{:S(2)}, u32[]{:S(2)}) %all-to-all-start.4) | async-done | bytes 852000 | tf_op jit(solution)/shard_map/all_to_all | solution.py:600
  176.5 3.4 %all-to-all-start.5 = ((bf16[8,8,1664]{2,1,0:T(8,128)(2,1)}), bf16[8,8,1664]{2,1,0:T(8,128)(2,1)S(1)}, u32[]{:S(2)}, u32[]{:S(2)}) async-start(bf16[8,8,1664]{2,1,0:T(8,128)(2,1)} %collect.1), calls=%async_computation.5 | async-start | bytes 425984 | tf_op jit(solution)/shard_map/all_to_all | solution.py:600
  181.5 5.4 %all-to-all-done.5.every_ref = bf16[8,8,1664]{2,1,0:T(8,128)(2,1)S(1)} async-done(((bf16[8,8,1664]{2,1,0:T(8,128)(2,1)}), bf16[8,8,1664]{2,1,0:T(8,128)(2,1)S(1)}, u32[]{:S(2)}, u32[]{:S(2)}) %all-to-all-start.5) | async-done | bytes 213024 | tf_op jit(solution)/shard_map/all_to_all | solution.py:600
  (20 shorter events, 8.9 us)
Async XLA Ops:
  4.9 11.4 %copy-start.3 = (f32[512,31]{0,1:T(8,128)S(1)}, f32[512,31]{0,1:T(8,128)}, u32[]{:S(2)}) copy-start(f32[512,31]{0,1:T(8,128)} %param.22) | copy-start | bytes 190468
  4.9 63.1 %all-to-all-start = ((bf16[32,48,512]{2,1,0:T(8,128)(2,1)}), bf16[32,48,512]{2,1,0:T(8,128)(2,1)S(1)}, u32[]{:S(2)}, u32[]{:S(2)}) async-start(bf16[32,48,512]{2,1,0:T(8,128)(2,1)} %bitcast.16), calls=%async_computation | async-start | bytes 3145728 | tf_op jit(solution)/shard_map/all_to_all | solution.py:600
  68.0 7.2 %copy-start.2 = (bf16[32,48,512]{2,1,0:T(8,128)(2,1)}, bf16[32,48,512]{2,1,0:T(8,128)(2,1)S(1)}, u32[]{:S(2)}) copy-start(bf16[32,48,512]{2,1,0:T(8,128)(2,1)S(1)} %all-to-all-done) | copy-start | bytes 4718596
  68.0 13.8 %all-to-all-start.1 = ((f32[8,8,128]{2,1,0:T(8,128)}), f32[8,8,128]{2,1,0:T(8,128)S(1)}, u32[]{:S(2)}, u32[]{:S(2)}) async-start(f32[8,8,128]{2,1,0:T(8,128)} %psum.37), calls=%async_computation.1 | async-start | bytes 65536 | tf_op jit(solution)/shard_map/all_to_all | solution.py:600
  81.8 0.6 copy-start.4
  87.7 11.8 %all-to-all-start.2 = ((f32[16,8,128]{2,1,0:T(8,128)}), f32[16,8,128]{2,1,0:T(8,128)S(1)}, u32[]{:S(2)}, u32[]{:S(2)}) async-start(f32[16,8,128]{2,1,0:T(8,128)} %get-tuple-element.61), calls=%async_computation.2 | async-start | bytes 131072 | tf_op jit(solution)/shard_map/all_to_all | solution.py:600
  99.5 45.3 %all-to-all-start.3 = ((bf16[32,48,512]{2,1,0:T(8,128)(2,1)}), bf16[32,48,512]{2,1,0:T(8,128)(2,1)S(1)}, u32[]{:S(2)}, u32[]{:S(2)}) async-start(bf16[32,48,512]{2,1,0:T(8,128)(2,1)} %bitcast.14), calls=%async_computation.3 | async-start | bytes 3145728 | tf_op jit(solution)/shard_map/all_to_all | solution.py:600
  137.2 2.7 %collective-permute-start = (bf16[256,1664]{1,0:T(8,128)(2,1)}, bf16[256,1664]{1,0:T(8,128)(2,1)S(1)}, u32[]{:S(2)}, u32[]{:S(2)}) collective-permute-start(bf16[256,1664]{1,0:T(8,128)(2,1)} %get-tuple-element.66), channel_id=1, source_target_pairs={{0,32},{32,0},{1,33},{33,1},{2,34},{34,2},{3,35},{35,3},{4,36},{36... | collective-permute-start | bytes 2555912 | tf_op jit(solution)/shard_map/ppermute | solution.py:604
  139.9 1.2 copy-start
  144.8 12.8 %copy-start.1 = (bf16[32,48,512]{2,1,0:T(8,128)(2,1)}, bf16[32,48,512]{2,1,0:T(8,128)(2,1)S(1)}, u32[]{:S(2)}) copy-start(bf16[32,48,512]{2,1,0:T(8,128)(2,1)S(1)} %all-to-all-done.3) | copy-start | bytes 4718596
  144.8 31.0 %all-to-all-start.4 = ((bf16[32,8,1664]{2,1,0:T(8,128)(2,1)}), bf16[32,8,1664]{2,1,0:T(8,128)(2,1)S(1)}, u32[]{:S(2)}, u32[]{:S(2)}) async-start(bf16[32,8,1664]{2,1,0:T(8,128)(2,1)} %bitcast.5), calls=%async_computation.4 | async-start | bytes 1703936 | tf_op jit(solution)/shard_map/all_to_all | solution.py:600
  176.5 10.3 %all-to-all-start.5 = ((bf16[8,8,1664]{2,1,0:T(8,128)(2,1)}), bf16[8,8,1664]{2,1,0:T(8,128)(2,1)S(1)}, u32[]{:S(2)}, u32[]{:S(2)}) async-start(bf16[8,8,1664]{2,1,0:T(8,128)(2,1)} %collect.1), calls=%async_computation.5 | async-start | bytes 425984 | tf_op jit(solution)/shard_map/all_to_all | solution.py:600

commit v10 on v8

--- a/solution.py
+++ b/solution.py
@@ -254,16 +254,9 @@
         sums_ref[...] = jnp.broadcast_to(as_tile(*sums)[None], sums_ref.shape)
 
 
-def output_kernel(swished_ref, dy_ref, wout_ref, out_ref, theirs_ref, own_ref, sw_all, dy_all):
-    step = pl.program_id(0)
+def output_kernel(swished_ref, dy_ref, wout_ref, out_ref, theirs_ref, own_ref):
     out_ref[...] = dot(swished_ref[...], wout_ref[...]).astype(BF16)
-    rows = pl.ds(pl.multiple_of(step * PER_STEP * SPAN, 16), PER_STEP * SPAN)
-    sw_all[rows, :] = swished_ref[...]
-    dy_all[rows, :] = dy_ref[...]
-
-    @pl.when(step == pl.num_programs(0) - 1)
-    def _():
-        split(dot(sw_all[...], dy_all[...], ((0,), (0,))), theirs_ref, own_ref)
+    split(dot(swished_ref[...], dy_ref[...], ((0,), (0,))), theirs_ref, own_ref)
 
 
 def backward_kernel(
@@ -488,16 +481,14 @@
 
 def outputs(swished, dy, w_out):
     rows, d = swished.shape
-    steps = rows // (SPAN * PER_STEP)
-    part = rows_of((rows, d), steps)
+    part = whole((rows, d))
     half = (d // 2, d)
     return pl.pallas_call(
         output_kernel,
-        grid=(steps,),
+        grid=(1,),
         out_shape=(sds((rows, d), BF16), sds(half, BF16), sds(half, BF16)),
         in_specs=[part, part, whole(w_out.shape)],
         out_specs=(part, whole(half), whole(half)),
-        scratch_shapes=[pltpu.VMEM((rows, d), BF16), pltpu.VMEM((rows, d), BF16)],
         compiler_params=params(),
         name="outputs",
         cost_estimate=cost(4e9, 6 * rows * d),

time: 176 us -> 176 us (level)
  no operation moved by 1% of the time
where the time goes in v10:
time: 176 us; the launch traced here: 175 us
  Pallas kernels  54.8 us (31%)
  blocking collectives  46.4 us (26%)
  starting transfers between devices  37.6 us (21%)
  waiting for transfers between devices  30.3 us (17%)
  local copies, waits for them, and re-layouts  4.81 us (3%)
    all_to_all x6, starting transfers between devices, swapped(): return lax.all_to_all(value, axes, split_axis=0, concat_axis=0, tiled=True)  37.5 us
    all_to_all x6, waiting for transfers between devices, swapped(): return lax.all_to_all(value, axes, split_axis=0, concat_axis=0, tiled=True)  27.8 us
    psum x3, blocking collectives, local(): stats = lax.psum(lax.psum(lax.psum(stats, 'c'), 'y'), 'x')  23.9 us
    psum x2, blocking collectives, local(): sums = lax.psum(lax.psum(sums, 'y'), 'x')  22.5 us
    pallas_call x1, Pallas kernels, backward(): pl.pallas_call(functools.partial(backward_kernel, total), grid=(steps,),...  12.4 us
    pallas_call x1, Pallas kernels, forward(): pl.pallas_call(forward_kernel, grid=(steps,), out_shape=(sds((rows, d), B...  11.9 us
    pallas_call x1, Pallas kernels, inputs_back(): pl.pallas_call(inputs_kernel, grid=(steps,), out_shape=sds((rows, d), BF1...  6.53 us
    pallas_call x1, Pallas kernels, middle(): pl.pallas_call(functools.partial(middle_kernel, total), grid=(steps,), ou...  5.24 us
  transfers between devices with their start and end apart: 7, of which 6 were waited for; matrix products, arithmetic and copies ran while one was open for 1% of the time, Pallas kernels for 25%

profile of v10, /device:TPU:32, one launch (start us, length us, event | category | flops | bytes accessed | tf_op | source)
XLA Modules:
  0.0 174.7 jit_solution(4461264880167322861)
XLA Ops:
  0.6 4.2 %unpack.1 = (bf16[1536,512]{1,0:T(8,128)(2,1)}, s32[32,128]{1,0:T(8,128)}) custom-call(s32[1,1024]{1,0:T(1,128)} %lengths_ref.1, s32[1,1024]{1,0:T(1,128)} %owners_ref.1, bf16[768,512]{1,0:T(8,128)(2,1)} %upstream_ref.1), custom_call_target="tpu_custom_call" | custom-call | flops 1000000000 | bytes 2359296 | tf_op jit(solution)/shard_map/unpack/pallas_call | solution.py:382
  4.9 11.3 %all-to-all-start = ((bf16[32,48,512]{2,1,0:T(8,128)(2,1)}), bf16[32,48,512]{2,1,0:T(8,128)(2,1)S(1)}, u32[]{:S(2)}, u32[]{:S(2)}) async-start(bf16[32,48,512]{2,1,0:T(8,128)(2,1)} %bitcast.16), calls=%async_computation | async-start | bytes 3145728 | tf_op jit(solution)/shard_map/all_to_all | solution.py:591
  17.1 11.9 %forward.1 = (bf16[1536,512]{1,0:T(8,128)(2,1)}, bf16[1536,512]{1,0:T(8,128)(2,1)}, bf16[1536,512]{1,0:T(8,128)(2,1)}, bf16[2048,512]{1,0:T(8,128)(2,1)}, f32[15...) custom-call(s32[32,128]{1,0:T(8,128)} %get-tuple-element.44.table_ref, bf16[1536,512]{1,0:T(8,128)(2,1)} %frames_ref.3, ...), custom_call_target="tpu_custom_call" | custom-call | flops 10000000000 | bytes 12582912 | tf_op jit(solution)/shard_map/forward/pallas_call | solution.py:418
  29.0 2.6 %psum.35 = f32[8,128]{1,0:T(8,128)S(1)} all-reduce(f32[8,128]{1,0:T(8,128)} %get-tuple-element.50), channel_id=1, replica_groups=mesh['y'=4,'c'=2,'x'=4,'z'=8] {'c'}, use_global_device_ids=true, to_apply=%region_0.0 | all-reduce | flops 1024 | bytes 8192 | tf_op jit(solution)/shard_map/psum | solution.py:616
  31.6 10.7 %psum.36 = f32[8,128]{1,0:T(8,128)S(1)} all-reduce(f32[8,128]{1,0:T(8,128)S(1)} %psum.35), channel_id=1, replica_groups=mesh['y'=4,'c'=2,'x'=4,'z'=8] {'y'}, use_global_device_ids=true, to_apply=%region_1.0 | all-reduce | flops 1024 | bytes 8192 | tf_op jit(solution)/shard_map/psum | solution.py:616
  42.3 10.6 %psum.37 = f32[8,128]{1,0:T(8,128)S(1)} all-reduce(f32[8,128]{1,0:T(8,128)S(1)} %psum.36), channel_id=1, replica_groups=mesh['y'=4,'c'=2,'x'=4,'z'=8] {'x'}, use_global_device_ids=true, to_apply=%region_2.0 | all-reduce | flops 1024 | bytes 8192 | tf_op jit(solution)/shard_map/psum | solution.py:616
  52.9 2.5 %all-to-all-done = bf16[32,48,512]{2,1,0:T(8,128)(2,1)S(1)} async-done(((bf16[32,48,512]{2,1,0:T(8,128)(2,1)}), bf16[32,48,512]{2,1,0:T(8,128)(2,1)S(1)}, u32[]{:S(2)}, u32[]{:S(2)}) %all-to-all-start) | async-done | bytes 1572896 | tf_op jit(solution)/shard_map/all_to_all | solution.py:591
  56.0 4.6 %all-to-all-start.1 = ((f32[8,8,128]{2,1,0:T(8,128)}), f32[8,8,128]{2,1,0:T(8,128)S(1)}, u32[]{:S(2)}, u32[]{:S(2)}) async-start(f32[8,8,128]{2,1,0:T(8,128)} %broadcast_in_dim.3), calls=%async_computation.1 | async-start | bytes 65536 | tf_op jit(solution)/shard_map/all_to_all | solution.py:591
  60.6 3.9 %project.1 = (bf16[1536,512]{1,0:T(8,128)(2,1)}, f32[1536,512]{1,0:T(8,128)}) custom-call(s32[32,128]{1,0:T(8,128)} %get-tuple-element.44.table_ref, bf16[1536,512]{1,0:T(8,128)(2,1)} %bitcast.15, bf16[512,512]{1,0:T(8,128)(2,1)} %wout_ref.3), custom_call_target="tpu_custom_call" | custom-call | flops 3000000000 | bytes 4718592 | tf_op jit(solution)/shard_map/project/pallas_call | solution.py:452
  64.5 2.7 %all-to-all-done.1.stats_ref = f32[8,8,128]{2,1,0:T(8,128)S(1)} async-done(((f32[8,8,128]{2,1,0:T(8,128)}), f32[8,8,128]{2,1,0:T(8,128)S(1)}, u32[]{:S(2)}, u32[]{:S(2)}) %all-to-all-start.1) | async-done | bytes 32800 | tf_op jit(solution)/shard_map/all_to_all | solution.py:591
  67.8 5.2 %middle.1 = (bf16[1536,512]{1,0:T(8,128)(2,1)}, f32[1536,512]{1,0:T(8,128)}, f32[16,8,128]{2,1,0:T(8,128)}, f32[8,128]{1,0:T(8,128)}) custom-call(f32[1536,512]{1,0:T(8,128)} %get-tuple-element.49.conv_ref, f32[1536,512]{1,0:T(8,128)} %get-tuple-element.53.grad_ref, f32[8,8,128]{2,1,0:T(8,128)} %copy-done.4, f32[1,512]{1,0:T(1,128)} %bitcast.18, ...), custom_call_target="tpu_custom_call" | custom-call | flops 4000000000 | bytes 7864320 | tf_op jit(solution)/shard_map/middle/pallas_call | solution.py:469
  73.1 4.8 %all-to-all-start.2 = ((f32[16,8,128]{2,1,0:T(8,128)}), f32[16,8,128]{2,1,0:T(8,128)S(1)}, u32[]{:S(2)}, u32[]{:S(2)}) async-start(f32[16,8,128]{2,1,0:T(8,128)} %get-tuple-element.61), calls=%async_computation.2 | async-start | bytes 131072 | tf_op jit(solution)/shard_map/all_to_all | solution.py:591
  77.8 4.6 %outputs.1 = (bf16[1536,512]{1,0:T(8,128)(2,1)}, bf16[256,512]{1,0:T(8,128)(2,1)}, bf16[256,512]{1,0:T(8,128)(2,1)}) custom-call(bf16[1536,512]{1,0:T(8,128)(2,1)} %get-tuple-element.58.swished_ref, bf16[1536,512]{1,0:T(8,128)(2,1)} %get-tuple-element.59.dy_ref, bf16[512,512]{1,0:T(8,128)(2,1)} %wout_ref.3), custom_call_target="tpu_custom_call" | custom-call | flops 4000000000 | bytes 4718592 | tf_op jit(solution)/shard_map/outputs/pallas_call | solution.py:486
  84.9 6.0 %all-to-all-start.3 = ((bf16[32,48,512]{2,1,0:T(8,128)(2,1)}), bf16[32,48,512]{2,1,0:T(8,128)(2,1)S(1)}, u32[]{:S(2)}, u32[]{:S(2)}) async-start(bf16[32,48,512]{2,1,0:T(8,128)(2,1)} %bitcast.14), calls=%async_computation.3 | async-start | bytes 3145728 | tf_op jit(solution)/shard_map/all_to_all | solution.py:591
  90.9 10.7 %psum.38 = f32[8,128]{1,0:T(8,128)S(1)} all-reduce(f32[8,128]{1,0:T(8,128)S(1)} %reduce_sum.9), channel_id=1, replica_groups=mesh['y'=4,'c'=2,'x'=4,'z'=8] {'y'}, use_global_device_ids=true, to_apply=%region_4.0 | all-reduce | flops 1024 | bytes 8192 | tf_op jit(solution)/shard_map/psum | solution.py:625
  101.6 11.7 %psum.39.sums_ref = f32[8,128]{1,0:T(8,128)} all-reduce(f32[8,128]{1,0:T(8,128)S(1)} %psum.38), channel_id=1, replica_groups=mesh['y'=4,'c'=2,'x'=4,'z'=8] {'x'}, use_global_device_ids=true, to_apply=%region_5.0 | all-reduce | flops 1024 | bytes 8192 | tf_op jit(solution)/shard_map/psum | solution.py:625
  113.4 12.4 %backward.1 = (bf16[1536,1024]{1,0:T(8,128)(2,1)}, bf16[256,1664]{1,0:T(8,128)(2,1)}, bf16[256,1664]{1,0:T(8,128)(2,1)}, f32[1,512]{1,0:T(1,128)}, f32[1,512]{1,0:T(1,128)}) custom-call(s32[32,128]{1,0:T(8,128)} %get-tuple-element.44.table_ref, bf16[1536,512]{1,0:T(8,128)(2,1)} %get-tuple-element.45.h_ref, bf16[1536,512]{1,0:T(8,128)(2,1)} %get-tuple-element.46.slope_ref, ...), custom_call_target="tpu_custom_call" | custom-call | flops 8000000000 | bytes 14155776 | tf_op jit(solution)/shard_map/backward/pallas_call | solution.py:504
  125.9 2.6 %collective-permute-done.got_ref = bf16[256,1664]{1,0:T(8,128)(2,1)S(1)} collective-permute-done((bf16[256,1664]{1,0:T(8,128)(2,1)}, bf16[256,1664]{1,0:T(8,128)(2,1)S(1)}, u32[]{:S(2)}, u32[]{:S(2)}) %collective-permute-start) | collective-permute-done | bytes 852000 | tf_op jit(solution)/shard_map/ppermute | solution.py:595
  130.6 7.4 %all-to-all-start.4 = ((bf16[32,8,1664]{2,1,0:T(8,128)(2,1)}), bf16[32,8,1664]{2,1,0:T(8,128)(2,1)S(1)}, u32[]{:S(2)}, u32[]{:S(2)}) async-start(bf16[32,8,1664]{2,1,0:T(8,128)(2,1)} %bitcast.5), calls=%async_computation.4 | async-start | bytes 1703936 | tf_op jit(solution)/shard_map/all_to_all | solution.py:591
  138.1 6.5 %inputs_back.1 = bf16[1536,512]{1,0:T(8,128)(2,1)} custom-call(s32[32,128]{1,0:T(8,128)} %get-tuple-element.44.table_ref, bf16[1536,512]{1,0:T(8,128)(2,1)} %frames_ref.3, bf16[1536,1024]{1,0:T(8,128)(2,1)} %get-tuple-element.69.grad_a_ref, f32[1,512]{1,0:T(1,128)} %bitcast.21, bf16[512,1024]{1,0:T(8,128)(2,1)} %win_ref.3), custom_call_target="tpu_custom_call" | custom-call | flops 6000000000 | bytes 9437184 | tf_op jit(solution)/shard_map/inputs_back/pallas_call | solution.py:537
  144.6 3.5 %pack.1 = bf16[768,512]{1,0:T(8,128)(2,1)} custom-call(s32[32,128]{1,0:T(8,128)} %get-tuple-element.44.table_ref, bf16[1536,512]{1,0:T(8,128)(2,1)} %bitcast.13), custom_call_target="tpu_custom_call" | custom-call | flops 2000000000 | bytes 2359296 | tf_op jit(solution)/shard_map/pack/pallas_call | solution.py:401
  148.1 14.7 %all-to-all-done.4.got_ref = bf16[32,8,1664]{2,1,0:T(8,128)(2,1)S(1)} async-done(((bf16[32,8,1664]{2,1,0:T(8,128)(2,1)}), bf16[32,8,1664]{2,1,0:T(8,128)(2,1)S(1)}, u32[]{:S(2)}, u32[]{:S(2)}) %all-to-all-start.4) | async-done | bytes 852000 | tf_op jit(solution)/shard_map/all_to_all | solution.py:591
  163.6 3.4 %all-to-all-start.5 = ((bf16[8,8,1664]{2,1,0:T(8,128)(2,1)}), bf16[8,8,1664]{2,1,0:T(8,128)(2,1)S(1)}, u32[]{:S(2)}, u32[]{:S(2)}) async-start(bf16[8,8,1664]{2,1,0:T(8,128)(2,1)} %collect.1), calls=%async_computation.5 | async-start | bytes 425984 | tf_op jit(solution)/shard_map/all_to_all | solution.py:591
  168.5 5.4 %all-to-all-done.5.every_ref = bf16[8,8,1664]{2,1,0:T(8,128)(2,1)S(1)} async-done(((bf16[8,8,1664]{2,1,0:T(8,128)(2,1)}), bf16[8,8,1664]{2,1,0:T(8,128)(2,1)S(1)}, u32[]{:S(2)}, u32[]{:S(2)}) %all-to-all-start.5) | async-done | bytes 213024 | tf_op jit(solution)/shard_map/all_to_all | solution.py:591
  (21 shorter events, 9.9 us)
Async XLA Ops:
  4.9 11.4 %copy-start.3 = (f32[512,31]{0,1:T(8,128)S(1)}, f32[512,31]{0,1:T(8,128)}, u32[]{:S(2)}) copy-start(f32[512,31]{0,1:T(8,128)} %param.22) | copy-start | bytes 190468
  4.9 50.4 %all-to-all-start = ((bf16[32,48,512]{2,1,0:T(8,128)(2,1)}), bf16[32,48,512]{2,1,0:T(8,128)(2,1)S(1)}, u32[]{:S(2)}, u32[]{:S(2)}) async-start(bf16[32,48,512]{2,1,0:T(8,128)(2,1)} %bitcast.16), calls=%async_computation | async-start | bytes 3145728 | tf_op jit(solution)/shard_map/all_to_all | solution.py:591
  55.3 5.3 %copy-start.2 = (bf16[32,48,512]{2,1,0:T(8,128)(2,1)}, bf16[32,48,512]{2,1,0:T(8,128)(2,1)S(1)}, u32[]{:S(2)}) copy-start(bf16[32,48,512]{2,1,0:T(8,128)(2,1)S(1)} %all-to-all-done) | copy-start | bytes 4718596
  56.0 11.2 %all-to-all-start.1 = ((f32[8,8,128]{2,1,0:T(8,128)}), f32[8,8,128]{2,1,0:T(8,128)S(1)}, u32[]{:S(2)}, u32[]{:S(2)}) async-start(f32[8,8,128]{2,1,0:T(8,128)} %broadcast_in_dim.3), calls=%async_computation.1 | async-start | bytes 65536 | tf_op jit(solution)/shard_map/all_to_all | solution.py:591
  67.2 0.6 copy-start.4
  73.1 11.8 %all-to-all-start.2 = ((f32[16,8,128]{2,1,0:T(8,128)}), f32[16,8,128]{2,1,0:T(8,128)S(1)}, u32[]{:S(2)}, u32[]{:S(2)}) async-start(f32[16,8,128]{2,1,0:T(8,128)} %get-tuple-element.61), calls=%async_computation.2 | async-start | bytes 131072 | tf_op jit(solution)/shard_map/all_to_all | solution.py:591
  84.9 45.8 %all-to-all-start.3 = ((bf16[32,48,512]{2,1,0:T(8,128)(2,1)}), bf16[32,48,512]{2,1,0:T(8,128)(2,1)S(1)}, u32[]{:S(2)}, u32[]{:S(2)}) async-start(bf16[32,48,512]{2,1,0:T(8,128)(2,1)} %bitcast.14), calls=%async_computation.3 | async-start | bytes 3145728 | tf_op jit(solution)/shard_map/all_to_all | solution.py:591
  125.8 2.7 %collective-permute-start = (bf16[256,1664]{1,0:T(8,128)(2,1)}, bf16[256,1664]{1,0:T(8,128)(2,1)S(1)}, u32[]{:S(2)}, u32[]{:S(2)}) collective-permute-start(bf16[256,1664]{1,0:T(8,128)(2,1)} %get-tuple-element.66), channel_id=1, source_target_pairs={{0,32},{32,0},{1,33},{33,1},{2,34},{34,2},{3,35},{35,3},{4,36},{36... | collective-permute-start | bytes 2555912 | tf_op jit(solution)/shard_map/ppermute | solution.py:595
  128.4 1.2 copy-start
  130.6 14.0 %copy-start.1 = (bf16[32,48,512]{2,1,0:T(8,128)(2,1)}, bf16[32,48,512]{2,1,0:T(8,128)(2,1)S(1)}, u32[]{:S(2)}) copy-start(bf16[32,48,512]{2,1,0:T(8,128)(2,1)S(1)} %all-to-all-done.3) | copy-start | bytes 4718596
  130.6 32.2 %all-to-all-start.4 = ((bf16[32,8,1664]{2,1,0:T(8,128)(2,1)}), bf16[32,8,1664]{2,1,0:T(8,128)(2,1)S(1)}, u32[]{:S(2)}, u32[]{:S(2)}) async-start(bf16[32,8,1664]{2,1,0:T(8,128)(2,1)} %bitcast.5), calls=%async_computation.4 | async-start | bytes 1703936 | tf_op jit(solution)/shard_map/all_to_all | solution.py:591
  163.6 10.3 %all-to-all-start.5 = ((bf16[8,8,1664]{2,1,0:T(8,128)(2,1)}), bf16[8,8,1664]{2,1,0:T(8,128)(2,1)S(1)}, u32[]{:S(2)}, u32[]{:S(2)}) async-start(bf16[8,8,1664]{2,1,0:T(8,128)(2,1)} %collect.1), calls=%async_computation.5 | async-start | bytes 425984 | tf_op jit(solution)/shard_map/all_to_all | solution.py:591
